TPU v7x, 32 devices: a whole 2x2x4 slice. The times are simulated.
32 devices in a mesh: dp: 8 (over z, x), chan: 4 (over y, core).
Axes of the slice: x: 2, y: 2, z: 4, core: 2. Of those that a mesh axis runs over, the one named last changes fastest.
Arguments:
- inputs: bfloat16 [4, 8, 512, 1024], P(None, 'dp', 'chan'), may hold values from -6 to 6
- cotangent: bfloat16 [4, 8, 512, 1024], P(None, 'dp', 'chan'), may hold values from -6 to 6
- lengths: int32 [4, 8], P(None, 'dp'), may hold values from 1 to 512, as said below
- tile_slot: int32 [23], replicated, may hold values from 0 to 23, as said below
- master: float32 [24, 1024, 1024], P('dp', 'chan')
- tile_first: float32 [24, 1024, 1024], P('dp', 'chan')
- tile_second: float32 [24, 1024, 1024], P('dp', 'chan'), as said below
- norm_params: float32 [10, 1024], replicated
- norm_first: float32 [10, 1024], replicated
- norm_second: float32 [10, 1024], replicated, as said below
- conv_params: float32 [7, 1024], P(None, 'chan')
- conv_first: float32 [7, 1024], P(None, 'chan')
- conv_second: float32 [7, 1024], P(None, 'chan'), as said below
Outputs:
- outputs: bfloat16 [4, 8, 512, 1024], P(None, 'dp', 'chan')
- input_grad: float32 [4, 8, 512, 1024], P(None, 'dp', 'chan')
- tile_first_new: float32 [24, 1024, 1024], P('dp', 'chan')
- tile_second_new: float32 [24, 1024, 1024], P('dp', 'chan')
- tile_master_new: float32 [24, 1024, 1024], P('dp', 'chan')
- tile_bf16_new: bfloat16 [24, 1024, 1024], P('dp', 'chan')
- norm_first_new: float32 [10, 1024], replicated
- norm_second_new: float32 [10, 1024], replicated
- norm_params_new: float32 [10, 1024], replicated
- conv_first_new: float32 [7, 1024], P(None, 'chan')
- conv_second_new: float32 [7, 1024], P(None, 'chan')
- conv_params_new: float32 [7, 1024], P(None, 'chan')
Inputs may be any that keep to these rules, and one draw needn't show every extreme that they name: `lengths`: in every micro-batch one clip has exactly 512 frames. The entries are distinct: tile k lives at position tile_slot[k] % 3 of dp index tile_slot[k] // 3; some dp index holds exactly 3 tiles. `tile_second`: Positive. `norm_second`: Positive. `conv_second`: Positive.
All inputs are finite; a program needn't handle non-finite values.
Results may differ from a plain program's by a relative error of at most 0.03.
Values may be sent and summed in bfloat16 or wider, within the bound.
No kernel may reach another device: no remote copies, remote signals or barrier semaphores. Data moves between devices by JAX's collectives and lax.ppermute only.
A program may use at most 384 MiB of HBM per device.

v0:
```python
import jax
import jax.numpy as jnp
from jax import lax
from jax.sharding import PartitionSpec as P

HEAD_DIM = 128
STEP = 10


norm_eps = 1e-05
masked_score = -1e30
beta_one = 0.9
beta_two = 0.98
adam_eps = 1e-08
tile_rate = 0.06
small_rate = 0.6
weight_decay = 0.01


def layer_norm(stream, norm_gain, norm_bias):
    center = stream - jnp.mean(stream, axis=-1, keepdims=True)
    spread = jnp.mean(center * center, axis=-1, keepdims=True)
    return center * lax.rsqrt(spread + norm_eps) * norm_gain + norm_bias


def silu_act(value_in):
    return value_in * jax.nn.sigmoid(value_in)


def silu_slope(value_in):
    gate_sig = jax.nn.sigmoid(value_in)
    return gate_sig * (1.0 + value_in * (1.0 - gate_sig))


def dot_rows(left, right):
    return lax.dot_general(
        left, right, (((1,), (1,)), ((), ())), preferred_element_type=jnp.float32
    )


def dot_plain(left, right):
    return jnp.dot(left, right, preferred_element_type=jnp.float32)


def dot_cols(left, right):
    return lax.dot_general(
        left, right, (((0,), (0,)), ((), ())), preferred_element_type=jnp.float32
    )


def gather_normed(stream, norm_gain, norm_bias):
    normed = layer_norm(stream, norm_gain, norm_bias).astype(jnp.bfloat16)
    return lax.all_gather(normed, "chan", axis=0, tiled=True)


def branch_total(partial_value):
    return lax.psum_scatter(
        partial_value.astype(jnp.bfloat16), "chan", scatter_dimension=0, tiled=True
    ).astype(jnp.float32)


def gather_incoming(upstream):
    return lax.all_gather(upstream.astype(jnp.bfloat16), "chan", axis=0, tiled=True)


def norm_backward(stream, norm_gain, norm_bias, partial_value):
    normed_grad = lax.psum_scatter(
        partial_value.astype(jnp.bfloat16), "chan", scatter_dimension=0, tiled=True
    ).astype(jnp.float32)
    _, pullback = jax.vjp(layer_norm, stream, norm_gain, norm_bias)
    return pullback(normed_grad)


def adamw_step(weight, gradient, first_old, second_old, rate, decay):
    first_new = beta_one * first_old + (1.0 - beta_one) * gradient
    second_new = beta_two * second_old + (1.0 - beta_two) * gradient * gradient
    first_hat = first_new / (1.0 - beta_one**STEP)
    second_hat = second_new / (1.0 - beta_two**STEP)
    weight_new = weight - rate * (first_hat / (jnp.sqrt(second_hat) + adam_eps) + decay * weight)
    return (first_new, second_new, weight_new)


def ffn_forward(stream, norm_gain, norm_bias, w_in, w_out):
    gathered = gather_normed(stream, norm_gain, norm_bias)
    hidden = dot_rows(gathered, w_in)
    active = silu_act(hidden).astype(jnp.bfloat16)
    return (stream + 0.5 * branch_total(dot_plain(active, w_out)), (gathered, hidden))


def ffn_backward(upstream, stream, norm_gain, norm_bias, kept_state, w_in, w_out):
    gathered, hidden = kept_state
    incoming = gather_incoming(0.5 * upstream)
    active = silu_act(hidden).astype(jnp.bfloat16)
    grad_out = dot_cols(active, incoming)
    grad_hidden = (dot_rows(incoming, w_out) * silu_slope(hidden)).astype(jnp.bfloat16)
    grad_in = dot_cols(grad_hidden, gathered)
    back_stream, grad_gain, grad_bias = norm_backward(
        stream, norm_gain, norm_bias, dot_plain(grad_hidden, w_in)
    )
    return (upstream + back_stream, grad_in, grad_out, grad_gain, grad_bias)


def score_block(queries, key_heads, key_mask):
    scores = jnp.einsum("qhd,khd->hqk", queries, key_heads, preferred_element_type=jnp.float32)
    scores = scores * queries.shape[-1] ** (-0.5)
    return jnp.where(key_mask[None, None, :] > 0, scores, masked_score)


def attn_forward(stream, norm_gain, norm_bias, w_query, w_key, w_value, w_output, key_mask):
    gathered = gather_normed(stream, norm_gain, norm_bias)
    queries = dot_rows(gathered, w_query).astype(jnp.bfloat16)
    keys_all = dot_rows(gathered, w_key).astype(jnp.bfloat16)
    values_all = dot_rows(gathered, w_value).astype(jnp.bfloat16)
    seq_rows = gathered.shape[0]
    head_count = w_query.shape[0] // HEAD_DIM
    block_rows = min(512, seq_rows)
    query_blocks = queries.reshape(seq_rows // block_rows, block_rows, head_count, HEAD_DIM)
    key_heads = keys_all.reshape(seq_rows, head_count, HEAD_DIM)
    value_heads = values_all.reshape(seq_rows, head_count, HEAD_DIM)

    def one_block(block_query):
        scores = score_block(block_query, key_heads, key_mask)
        row_max = jnp.max(scores, axis=-1, keepdims=True)
        exponent = jnp.exp(scores - row_max)
        row_sum = jnp.sum(exponent, axis=-1, keepdims=True)
        attn_probs = (exponent / row_sum).astype(jnp.bfloat16)
        head_block = jnp.einsum(
            "hqk,khd->qhd", attn_probs, value_heads, preferred_element_type=jnp.float32
        )
        return (head_block, row_max + jnp.log(row_sum))

    head_out, log_total = lax.map(one_block, query_blocks)
    merged = head_out.reshape(seq_rows, -1).astype(jnp.bfloat16)
    result = stream + branch_total(dot_plain(merged, w_output))
    return (result, (gathered, queries, keys_all, values_all, merged, log_total))


def attn_backward(
    upstream, stream, norm_gain, norm_bias, kept_state, w_query, w_key, w_value, w_output, key_mask
):
    gathered, queries, keys_all, values_all, merged, log_total = kept_state
    incoming = gather_incoming(upstream)
    grad_output = dot_cols(merged, incoming)
    grad_merged = dot_rows(incoming, w_output).astype(jnp.bfloat16)
    seq_rows = gathered.shape[0]
    head_count = w_query.shape[0] // HEAD_DIM
    block_rows = min(512, seq_rows)
    block_shape = (seq_rows // block_rows, block_rows, head_count, HEAD_DIM)
    query_blocks = queries.reshape(block_shape)
    grad_blocks = grad_merged.reshape(block_shape)
    key_heads = keys_all.reshape(seq_rows, head_count, HEAD_DIM)
    value_heads = values_all.reshape(seq_rows, head_count, HEAD_DIM)
    score_scale = HEAD_DIM ** (-0.5)

    def one_block(carried, operands):
        key_acc, value_acc = carried
        block_query, block_grad, block_total = operands
        attn_probs = jnp.exp(score_block(block_query, key_heads, key_mask) - block_total)
        grad_probs = jnp.einsum(
            "qhd,khd->hqk", block_grad, value_heads, preferred_element_type=jnp.float32
        )
        row_dot = jnp.sum(attn_probs * grad_probs, axis=-1, keepdims=True)
        grad_scores = (attn_probs * (grad_probs - row_dot)).astype(jnp.bfloat16)
        grad_query = (
            jnp.einsum("hqk,khd->qhd", grad_scores, key_heads, preferred_element_type=jnp.float32)
            * score_scale
        )
        key_acc = (
            key_acc
            + jnp.einsum(
                "hqk,qhd->khd", grad_scores, block_query, preferred_element_type=jnp.float32
            )
            * score_scale
        )
        value_acc = value_acc + jnp.einsum(
            "hqk,qhd->khd",
            attn_probs.astype(jnp.bfloat16),
            block_grad,
            preferred_element_type=jnp.float32,
        )
        return ((key_acc, value_acc), grad_query)

    zeros_heads = jnp.zeros((seq_rows, head_count, HEAD_DIM), jnp.float32)
    (grad_keys, grad_values), grad_queries = lax.scan(
        one_block, (zeros_heads, zeros_heads), (query_blocks, grad_blocks, log_total)
    )
    grad_queries = grad_queries.reshape(seq_rows, -1).astype(jnp.bfloat16)
    grad_keys = grad_keys.reshape(seq_rows, -1).astype(jnp.bfloat16)
    grad_values = grad_values.reshape(seq_rows, -1).astype(jnp.bfloat16)
    grad_wq = dot_cols(grad_queries, gathered)
    grad_wk = dot_cols(grad_keys, gathered)
    grad_wv = dot_cols(grad_values, gathered)
    partial_value = (
        dot_plain(grad_queries, w_query)
        + dot_plain(grad_keys, w_key)
        + dot_plain(grad_values, w_value)
    )
    back_stream, grad_gain, grad_bias = norm_backward(stream, norm_gain, norm_bias, partial_value)
    return (upstream + back_stream, grad_wq, grad_wk, grad_wv, grad_output, grad_gain, grad_bias)


def conv_forward(stream, norm_gain, norm_bias, p_value, p_gate, p_output, conv_local, key_mask):
    gathered = gather_normed(stream, norm_gain, norm_bias)
    linear = dot_rows(gathered, p_value)
    gating = dot_rows(gathered, p_gate)
    frame_mask = key_mask[:, None]
    gated_glu = linear * jax.nn.sigmoid(gating) * frame_mask
    taps_count = conv_local.shape[0] - 2
    margin = (taps_count - 1) // 2
    seq_rows = gated_glu.shape[0]
    padded = jnp.pad(gated_glu, ((margin, margin), (0, 0)))
    mixed_conv = jnp.zeros_like(gated_glu)
    for offset in range(taps_count):
        mixed_conv = mixed_conv + conv_local[offset] * padded[offset : offset + seq_rows]
    local_count = jnp.sum(key_mask)
    frame_count, total_one = lax.psum((local_count, jnp.sum(mixed_conv * frame_mask, axis=0)), "dp")
    center = mixed_conv - total_one / frame_count
    spread = lax.psum(jnp.sum(frame_mask * center * center, axis=0), "dp") / frame_count
    inv_std = lax.rsqrt(spread + norm_eps)
    normal = center * inv_std * conv_local[taps_count] + conv_local[taps_count + 1]
    active = silu_act(normal).astype(jnp.bfloat16)
    result = stream + branch_total(dot_plain(active, p_output))
    return (result, (gathered, linear, gating, padded, center, inv_std, normal, frame_count))


def conv_backward(
    upstream,
    stream,
    norm_gain,
    norm_bias,
    kept_state,
    p_value,
    p_gate,
    p_output,
    conv_local,
    key_mask,
):
    gathered, linear, gating, padded, center, inv_std, normal, frame_count = kept_state
    incoming = gather_incoming(upstream)
    grad_output = dot_cols(silu_act(normal).astype(jnp.bfloat16), incoming)
    grad_normal = dot_rows(incoming, p_output) * silu_slope(normal)
    sum_plain, sum_center = lax.psum(
        (jnp.sum(grad_normal, axis=0), jnp.sum(grad_normal * center, axis=0)), "dp"
    )
    taps_count = conv_local.shape[0] - 2
    margin = (taps_count - 1) // 2
    seq_rows = center.shape[0]
    frame_mask = key_mask[:, None]
    bn_scale = conv_local[taps_count] * inv_std
    grad_mixed = (
        bn_scale * grad_normal
        - frame_mask
        * bn_scale
        * (sum_plain + inv_std * inv_std * sum_center * center)
        / frame_count
    )
    grad_padded = jnp.pad(grad_mixed, ((margin, margin), (0, 0)))
    grad_gated = jnp.zeros_like(grad_mixed)
    tap_grads = []
    for offset in range(taps_count):
        start_row = 2 * margin - offset
        grad_gated = grad_gated + conv_local[offset] * grad_padded[start_row : start_row + seq_rows]
        tap_grads.append(jnp.sum(grad_mixed * padded[offset : offset + seq_rows], axis=0))
    grad_gated = grad_gated * frame_mask
    gate_sig = jax.nn.sigmoid(gating)
    grad_linear = (grad_gated * gate_sig).astype(jnp.bfloat16)
    grad_gating = (grad_gated * linear * gate_sig * (1.0 - gate_sig)).astype(jnp.bfloat16)
    grad_pv = dot_cols(grad_linear, gathered)
    grad_pg = dot_cols(grad_gating, gathered)
    partial_value = dot_plain(grad_linear, p_value) + dot_plain(grad_gating, p_gate)
    back_stream, grad_gain, grad_bias = norm_backward(stream, norm_gain, norm_bias, partial_value)
    bn_grads = jnp.stack([sum_center * inv_std, sum_plain])
    return (
        upstream + back_stream,
        grad_pv,
        grad_pg,
        grad_output,
        jnp.stack(tap_grads),
        bn_grads,
        grad_gain,
        grad_bias,
    )


def shards(
    inputs,
    cotangent,
    lengths,
    tile_slot,
    master,
    tile_first,
    tile_second,
    norm_params,
    norm_first,
    norm_second,
    conv_params,
    conv_first,
    conv_second,
):
    seg_rows = inputs.shape[2]
    model_width = inputs.shape[3]
    rows_tile = master.shape[1]
    chan_count = lax.axis_size("chan")
    chan_index = lax.axis_index("chan")
    weights_all = lax.all_gather(master.astype(jnp.bfloat16), "dp", axis=0, tiled=True)
    tile_mats = jnp.take(weights_all, tile_slot, axis=0)
    quarter = (tile_mats.shape[0] - 7) // 4

    def stack_rows(first_tile):
        return tile_mats[first_tile : first_tile + quarter].reshape(
            quarter * rows_tile, model_width
        )

    in_first = stack_rows(0)
    out_first = stack_rows(quarter)
    in_second = stack_rows(2 * quarter)
    out_second = stack_rows(3 * quarter)
    base_tile = 4 * quarter
    w_query = tile_mats[base_tile]
    w_key = tile_mats[base_tile + 1]
    w_value = tile_mats[base_tile + 2]
    w_output = tile_mats[base_tile + 3]
    p_value = tile_mats[base_tile + 4]
    p_gate = tile_mats[base_tile + 5]
    p_output = tile_mats[base_tile + 6]
    taps_count = conv_params.shape[0] - 2
    seq_rows = seg_rows * chan_count
    positions = jnp.arange(seq_rows, dtype=jnp.int32)
    slot_count = lax.axis_size("dp") * master.shape[0]
    tile_acc = jnp.zeros(tile_mats.shape, jnp.float32)
    norm_acc = jnp.zeros(norm_params.shape, jnp.float32)
    taps_acc = jnp.zeros((taps_count, rows_tile), jnp.float32)
    bn_acc = jnp.zeros((2, rows_tile), jnp.float32)
    outputs = []
    input_grads = []
    for micro_index in range(inputs.shape[0]):
        key_mask = (positions < lengths[micro_index, 0]).astype(jnp.float32)
        source = inputs[micro_index, 0].astype(jnp.float32)
        stream_one, kept_one = ffn_forward(
            source, norm_params[0], norm_params[5], in_first, out_first
        )
        stream_two, kept_two = attn_forward(
            stream_one, norm_params[1], norm_params[6], w_query, w_key, w_value, w_output, key_mask
        )
        stream_three, kept_three = conv_forward(
            stream_two,
            norm_params[2],
            norm_params[7],
            p_value,
            p_gate,
            p_output,
            conv_params,
            key_mask,
        )
        stream_four, kept_four = ffn_forward(
            stream_three, norm_params[3], norm_params[8], in_second, out_second
        )
        result, pullback = jax.vjp(layer_norm, stream_four, norm_params[4], norm_params[9])
        outputs.append(result.astype(jnp.bfloat16))
        grad_four, gain_four, bias_four = pullback(cotangent[micro_index, 0].astype(jnp.float32))
        grad_three, gin_second, gout_second, gain_three, bias_three = ffn_backward(
            grad_four,
            stream_three,
            norm_params[3],
            norm_params[8],
            kept_four,
            in_second,
            out_second,
        )
        grad_two, grad_pv, grad_pg, grad_po, taps_grad, bn_grads, gain_two, bias_two = (
            conv_backward(
                grad_three,
                stream_two,
                norm_params[2],
                norm_params[7],
                kept_three,
                p_value,
                p_gate,
                p_output,
                conv_params,
                key_mask,
            )
        )
        grad_one, grad_wq, grad_wk, grad_wv, grad_wo, gain_one, bias_one = attn_backward(
            grad_two,
            stream_one,
            norm_params[1],
            norm_params[6],
            kept_two,
            w_query,
            w_key,
            w_value,
            w_output,
            key_mask,
        )
        grad_zero, gin_first, gout_first, gain_zero, bias_zero = ffn_backward(
            grad_one, source, norm_params[0], norm_params[5], kept_one, in_first, out_first
        )
        input_grads.append(grad_zero)
        tile_shape = (quarter, rows_tile, model_width)
        micro_grads = jnp.concatenate(
            [
                gin_first.reshape(tile_shape),
                gout_first.reshape(tile_shape),
                gin_second.reshape(tile_shape),
                gout_second.reshape(tile_shape),
                jnp.stack([grad_wq, grad_wk, grad_wv, grad_wo, grad_pv, grad_pg, grad_po]),
            ],
            0,
        )
        norm_acc = norm_acc + jnp.stack(
            [
                gain_zero,
                gain_one,
                gain_two,
                gain_three,
                gain_four,
                bias_zero,
                bias_one,
                bias_two,
                bias_three,
                bias_four,
            ]
        )
        taps_acc = taps_acc + taps_grad
        bn_acc = bn_acc + bn_grads
        tile_acc = tile_acc + micro_grads
    placed = (
        jnp.zeros((slot_count, rows_tile, model_width), jnp.float32).at[tile_slot].set(tile_acc)
    )
    owned = lax.psum_scatter(placed, "dp", scatter_dimension=0, tiled=True)
    taps_wide = lax.dynamic_update_slice(
        jnp.zeros((taps_count, chan_count * rows_tile), jnp.float32),
        taps_acc,
        (jnp.int32(0), chan_index * rows_tile),
    )
    norm_total, taps_total = lax.psum((norm_acc, taps_wide), ("dp", "chan"))
    taps_own = lax.dynamic_slice_in_dim(taps_total, chan_index * rows_tile, rows_tile, 1)
    conv_grad = jnp.concatenate([taps_own, bn_acc], 0)
    tile_m, tile_v, tile_w = adamw_step(
        master, owned, tile_first, tile_second, tile_rate, weight_decay
    )
    norm_m, norm_v, norm_w = adamw_step(
        norm_params, norm_total, norm_first, norm_second, small_rate, 0.0
    )
    conv_m, conv_v, conv_w = adamw_step(
        conv_params, conv_grad, conv_first, conv_second, small_rate, 0.0
    )
    block_out = jnp.stack(outputs)[:, None]
    block_grad = jnp.stack(input_grads)[:, None]
    return (
        block_out,
        block_grad,
        tile_m,
        tile_v,
        tile_w,
        tile_w.astype(jnp.bfloat16),
        norm_m,
        norm_v,
        norm_w,
        conv_m,
        conv_v,
        conv_w,
    )


def solution(mesh):
    in_specs = (
        P(None, "dp", "chan", None),
        P(None, "dp", "chan", None),
        P(None, "dp"),
        P(),
        P("dp", "chan", None),
        P("dp", "chan", None),
        P("dp", "chan", None),
        P(),
        P(),
        P(),
        P(None, "chan"),
        P(None, "chan"),
        P(None, "chan"),
    )
    out_specs = (
        P(None, "dp", "chan", None),
        P(None, "dp", "chan", None),
        P("dp", "chan", None),
        P("dp", "chan", None),
        P("dp", "chan", None),
        P("dp", "chan", None),
        P(),
        P(),
        P(),
        P(None, "chan"),
        P(None, "chan"),
        P(None, "chan"),
    )
    return jax.shard_map(shards, mesh=mesh, in_specs=in_specs, out_specs=out_specs, check_vma=False)
```

profile of v0, /device:TPU:0, one launch (start us, length us, event | category | flops | bytes accessed | tf_op | source)
XLA Modules:
  0.0 2346.4 jit_solution(8056816321821509494)
XLA Ops:
  12.8 177.1 %all-gather.36.cloned.1.call-done = bf16[24,256,1024]{2,1,0:T(8,128)(2,1)} async-done(((bf16[3,256,1024]{2,1,0:T(8,128)(2,1)}), bf16[24,256,1024]{2,1,0:T(8,128)(2,1)}) %all-gather.36.cloned.1.call-update) | async-done | bytes 12582928 | tf_op jit(solution)/shard_map/all_gather | solution.py:305
  329.8 28.0 %reduce-scatter.50.cloned.1.call-done = bf16[128,1024]{1,0:T(8,128)(2,1)} async-done(((bf16[512,1024]{1,0:T(8,128)(2,1)}), bf16[128,1024]{1,0:T(8,128)(2,1)}) %reduce-scatter.50.cloned.1.call-update) | async-done | bytes 262160 | tf_op jit(solution)/shard_map/reduce_scatter | solution.py:57
  357.8 28.2 %reduce-scatter.42.cloned.1.call-done = bf16[128,1024]{1,0:T(8,128)(2,1)} async-done(((bf16[512,1024]{1,0:T(8,128)(2,1)}), bf16[128,1024]{1,0:T(8,128)(2,1)}) %reduce-scatter.42.cloned.1.call-update) | async-done | bytes 262160 | tf_op jit(solution)/shard_map/reduce_scatter | solution.py:57
  491.1 27.4 %reduce-scatter.52.cloned.1.call-done = bf16[128,1024]{1,0:T(8,128)(2,1)} async-done(((bf16[512,1024]{1,0:T(8,128)(2,1)}), bf16[128,1024]{1,0:T(8,128)(2,1)}) %reduce-scatter.52.cloned.1.call-update) | async-done | bytes 262160 | tf_op jit(solution)/shard_map/reduce_scatter | solution.py:57
  518.5 27.9 %reduce-scatter.44.cloned.1.call-done = bf16[128,1024]{1,0:T(8,128)(2,1)} async-done(((bf16[512,1024]{1,0:T(8,128)(2,1)}), bf16[128,1024]{1,0:T(8,128)(2,1)}) %reduce-scatter.44.cloned.1.call-update) | async-done | bytes 262160 | tf_op jit(solution)/shard_map/reduce_scatter | solution.py:57
  546.4 28.0 %reduce-scatter.36.cloned.1.call-done = bf16[128,1024]{1,0:T(8,128)(2,1)} async-done(((bf16[512,1024]{1,0:T(8,128)(2,1)}), bf16[128,1024]{1,0:T(8,128)(2,1)}) %reduce-scatter.36.cloned.1.call-update) | async-done | bytes 262160 | tf_op jit(solution)/shard_map/reduce_scatter | solution.py:57
  741.7 26.9 %reduce-scatter.54.cloned.1.call-done = bf16[128,1024]{1,0:T(8,128)(2,1)} async-done(((bf16[512,1024]{1,0:T(8,128)(2,1)}), bf16[128,1024]{1,0:T(8,128)(2,1)}) %reduce-scatter.54.cloned.1.call-update) | async-done | bytes 262160 | tf_op jit(solution)/shard_map/reduce_scatter | solution.py:57
  770.1 25.8 %reduce-scatter.46.cloned.1.call-done = bf16[128,1024]{1,0:T(8,128)(2,1)} async-done(((bf16[512,1024]{1,0:T(8,128)(2,1)}), bf16[128,1024]{1,0:T(8,128)(2,1)}) %reduce-scatter.46.cloned.1.call-update) | async-done | bytes 262160 | tf_op jit(solution)/shard_map/reduce_scatter | solution.py:57
  798.2 25.9 %reduce-scatter.38.cloned.1.call-done = bf16[128,1024]{1,0:T(8,128)(2,1)} async-done(((bf16[512,1024]{1,0:T(8,128)(2,1)}), bf16[128,1024]{1,0:T(8,128)(2,1)}) %reduce-scatter.38.cloned.1.call-update) | async-done | bytes 262160 | tf_op jit(solution)/shard_map/reduce_scatter | solution.py:57
  929.9 25.5 %reduce-scatter.48.cloned.1.call-done = bf16[128,1024]{1,0:T(8,128)(2,1)} async-done(((bf16[512,1024]{1,0:T(8,128)(2,1)}), bf16[128,1024]{1,0:T(8,128)(2,1)}) %reduce-scatter.48.cloned.1.call-update) | async-done | bytes 262160 | tf_op jit(solution)/shard_map/reduce_scatter | solution.py:57
  957.6 25.8 %reduce-scatter.40.cloned.1.call-done = bf16[128,1024]{1,0:T(8,128)(2,1)} async-done(((bf16[512,1024]{1,0:T(8,128)(2,1)}), bf16[128,1024]{1,0:T(8,128)(2,1)}) %reduce-scatter.40.cloned.1.call-update) | async-done | bytes 262160 | tf_op jit(solution)/shard_map/reduce_scatter | solution.py:57
  985.7 25.8 %reduce-scatter.56.cloned.1.call-done = bf16[128,1024]{1,0:T(8,128)(2,1)} async-done(((bf16[512,1024]{1,0:T(8,128)(2,1)}), bf16[128,1024]{1,0:T(8,128)(2,1)}) %reduce-scatter.56.cloned.1.call-update) | async-done | bytes 262160 | tf_op jit(solution)/shard_map/reduce_scatter | solution.py:57
  1118.8 28.1 %reduce-scatter.74.cloned.1.call-done = bf16[128,1024]{1,0:T(8,128)(2,1)} async-done(((bf16[512,1024]{1,0:T(8,128)(2,1)}), bf16[128,1024]{1,0:T(8,128)(2,1)}) %reduce-scatter.74.cloned.1.call-update) | async-done | bytes 262160 | tf_op jit(solution)/shard_map/reduce_scatter | solution.py:67
  1149.0 25.9 %reduce-scatter.82.cloned.1.call-done = bf16[128,1024]{1,0:T(8,128)(2,1)} async-done(((bf16[512,1024]{1,0:T(8,128)(2,1)}), bf16[128,1024]{1,0:T(8,128)(2,1)}) %reduce-scatter.82.cloned.1.call-update) | async-done | bytes 262160 | tf_op jit(solution)/shard_map/reduce_scatter | solution.py:67
  1178.7 24.5 %reduce-scatter.66.cloned.1.call-done = bf16[128,1024]{1,0:T(8,128)(2,1)} async-done(((bf16[512,1024]{1,0:T(8,128)(2,1)}), bf16[128,1024]{1,0:T(8,128)(2,1)}) %reduce-scatter.66.cloned.1.call-update) | async-done | bytes 262160 | tf_op jit(solution)/shard_map/reduce_scatter | solution.py:67
  1370.3 27.9 %reduce-scatter.68.cloned.1.call-done = bf16[128,1024]{1,0:T(8,128)(2,1)} async-done(((bf16[512,1024]{1,0:T(8,128)(2,1)}), bf16[128,1024]{1,0:T(8,128)(2,1)}) %reduce-scatter.68.cloned.1.call-update) | async-done | bytes 262160 | tf_op jit(solution)/shard_map/reduce_scatter | solution.py:67
  1398.2 28.0 %reduce-scatter.84.cloned.1.call-done = bf16[128,1024]{1,0:T(8,128)(2,1)} async-done(((bf16[512,1024]{1,0:T(8,128)(2,1)}), bf16[128,1024]{1,0:T(8,128)(2,1)}) %reduce-scatter.84.cloned.1.call-update) | async-done | bytes 262160 | tf_op jit(solution)/shard_map/reduce_scatter | solution.py:67
  1532.2 28.2 %reduce-scatter.78.cloned.1.call-done = bf16[128,1024]{1,0:T(8,128)(2,1)} async-done(((bf16[512,1024]{1,0:T(8,128)(2,1)}), bf16[128,1024]{1,0:T(8,128)(2,1)}) %reduce-scatter.78.cloned.1.call-update) | async-done | bytes 262160 | tf_op jit(solution)/shard_map/reduce_scatter | solution.py:67
  1560.4 28.0 %reduce-scatter.70.cloned.1.call-done = bf16[128,1024]{1,0:T(8,128)(2,1)} async-done(((bf16[512,1024]{1,0:T(8,128)(2,1)}), bf16[128,1024]{1,0:T(8,128)(2,1)}) %reduce-scatter.70.cloned.1.call-update) | async-done | bytes 262160 | tf_op jit(solution)/shard_map/reduce_scatter | solution.py:67
  1588.4 28.2 %reduce-scatter.86.cloned.1.call-done = bf16[128,1024]{1,0:T(8,128)(2,1)} async-done(((bf16[512,1024]{1,0:T(8,128)(2,1)}), bf16[128,1024]{1,0:T(8,128)(2,1)}) %reduce-scatter.86.cloned.1.call-update) | async-done | bytes 262160 | tf_op jit(solution)/shard_map/reduce_scatter | solution.py:67
  1828.2 40.7 %add_add_fusion = f32[23,256,1024]{2,1,0:T(8,128)} fusion(f32[23,256,1024]{2,1,0:T(8,128)} %fusion.9, f32[23,256,1024]{2,1,0:T(8,128)} %fusion.16, f32[23,256,1024]{2,1,0:T(8,128)} %fusion.30, f32[23,256,1024]{2,1,0:T(8,128)} %fusion.23), kind=kLoop, calls=%fused_computation.2 | loop fusion | flops 18087936 | bytes 120586240 | tf_op jit(solution)/shard_map/add | solution.py:427
  1880.5 44.5 %scatter_fusion = f32[24,256,1024]{2,1,0:T(8,128)} fusion(f32[24,256,1024]{2,1,0:T(8,128)} %broadcast_in_dim.451, s32[23]{0:T(128)S(1)} %copy-done.377, f32[23,256,1024]{2,1,0:T(8,128)} %add_add_fusion), kind=kCustom, calls=%fused_computation.1 | custom fusion | bytes 72351840 | tf_op jit(solution)/shard_map/scatter | solution.py:429
  1939.2 43.6 %all-reduce.8 = (f32[10,1024]{1,0:T(8,128)S(1)}, f32[5,1024]{1,0:T(8,128)S(1)}) all-reduce(f32[10,1024]{1,0:T(8,128)S(1)} %add_add_fusion.33, f32[5,1024]{1,0:T(8,128)S(1)} %add_dynamic-update-slice_fusion), channel_id=1, replica_groups=mesh['dp'=8,'chan'=4] {'dp','chan'}, use_global_device_ids=true, to_apply=%region_206.207 | all-reduce | flops 15360 | bytes 122880 | tf_op jit(solution)/shard_map/psum | solution.py:437
  1991.1 340.0 %reduce-scatter.98.cloned.1.call-done = f32[3,256,1024]{2,1,0:T(8,128)} async-done(((f32[24,256,1024]{2,1,0:T(8,128)}), f32[3,256,1024]{2,1,0:T(8,128)}) %reduce-scatter.98.cloned.1.call-update) | async-done | bytes 3145744 | tf_op jit(solution)/shard_map/reduce_scatter | solution.py:431
  (1433 shorter events, 1166.2 us)
Async XLA Ops:
  7.2 182.8 %all-gather.36.cloned.1.call-start = ((), (), s32[]{:S(2)}) async-start(), calls=%async_computation.34 | async-start | bytes 14155776 | tf_op jit(solution)/shard_map/all_gather | solution.py:305
  10.6 203.7 %all-gather.34.cloned.1.call-start = ((), (), s32[]{:S(2)}) async-start(), calls=%async_computation.33 | async-start | bytes 1310720 | tf_op jit(solution)/shard_map/all_gather | solution.py:53
  12.7 231.9 %reduce-scatter.34.cloned.1.call-start = ((), (), s32[]{:S(2)}) async-start(), calls=%async_computation.35 | async-start | bytes 1310720 | tf_op jit(solution)/shard_map/reduce_scatter | solution.py:57
  436.5 109.9 %reduce-scatter.44.cloned.1.call-start = ((), (), s32[]{:S(2)}) async-start(), calls=%async_computation.45 | async-start | bytes 1310720 | tf_op jit(solution)/shard_map/reduce_scatter | solution.py:57
  455.3 119.2 %reduce-scatter.36.cloned.1.call-start = ((), (), s32[]{:S(2)}) async-start(), calls=%async_computation.37 | async-start | bytes 1310720 | tf_op jit(solution)/shard_map/reduce_scatter | solution.py:57
  474.1 122.1 %all-gather.64.cloned.1.call-start = ((), (), s32[]{:S(2)}) async-start(), calls=%async_computation.62 | async-start | bytes 1310720 | tf_op jit(solution)/shard_map/all_gather | solution.py:53
  581.5 158.9 %reduce-scatter.62.cloned.1.call-start = ((), (), s32[]{:S(2)}) async-start(), calls=%async_computation.63 | async-start | bytes 1310720 | tf_op jit(solution)/shard_map/reduce_scatter | solution.py:57
  725.9 118.6 %all-gather.66.cloned.1.call-start = ((), (), s32[]{:S(2)}) async-start(), calls=%async_computation.64 | async-start | bytes 1310720 | tf_op jit(solution)/shard_map/all_gather | solution.py:53
  851.5 103.9 %reduce-scatter.48.cloned.1.call-start = ((), (), s32[]{:S(2)}) async-start(), calls=%async_computation.49 | async-start | bytes 1310720 | tf_op jit(solution)/shard_map/reduce_scatter | solution.py:57
  870.2 113.2 %reduce-scatter.40.cloned.1.call-start = ((), (), s32[]{:S(2)}) async-start(), calls=%async_computation.41 | async-start | bytes 1310720 | tf_op jit(solution)/shard_map/reduce_scatter | solution.py:57
  889.1 122.4 %reduce-scatter.56.cloned.1.call-start = ((), (), s32[]{:S(2)}) async-start(), calls=%async_computation.57 | async-start | bytes 1310720 | tf_op jit(solution)/shard_map/reduce_scatter | solution.py:57
  907.4 128.1 %all-gather.92.cloned.1.call-start = ((), (), s32[]{:S(2)}) async-start(), calls=%async_computation.90 | async-start | bytes 1310720 | tf_op jit(solution)/shard_map/all_gather | solution.py:63
  1062.0 112.9 %reduce-scatter.82.cloned.1.call-start = ((), (), s32[]{:S(2)}) async-start(), calls=%async_computation.83 | async-start | bytes 1310720 | tf_op jit(solution)/shard_map/reduce_scatter | solution.py:67
  1080.8 122.4 %reduce-scatter.66.cloned.1.call-start = ((), (), s32[]{:S(2)}) async-start(), calls=%async_computation.67 | async-start | bytes 1310720 | tf_op jit(solution)/shard_map/reduce_scatter | solution.py:67
  1098.9 127.3 %all-gather.86.cloned.1.call-start = ((), (), s32[]{:S(2)}) async-start(), calls=%async_computation.84 | async-start | bytes 1310720 | tf_op jit(solution)/shard_map/all_gather | solution.py:63
  1215.7 129.2 %reduce-scatter.92.cloned.1.call-start = ((), (), s32[]{:S(2)}) async-start(), calls=%async_computation.93 | async-start | bytes 1310720 | tf_op jit(solution)/shard_map/reduce_scatter | solution.py:67
  1477.0 111.4 %reduce-scatter.70.cloned.1.call-start = ((), (), s32[]{:S(2)}) async-start(), calls=%async_computation.71 | async-start | bytes 1310720 | tf_op jit(solution)/shard_map/reduce_scatter | solution.py:67
  1496.0 120.7 %reduce-scatter.86.cloned.1.call-start = ((), (), s32[]{:S(2)}) async-start(), calls=%async_computation.87 | async-start | bytes 1310720 | tf_op jit(solution)/shard_map/reduce_scatter | solution.py:67
  1514.8 123.9 %all-gather.90.cloned.1.call-start = ((), (), s32[]{:S(2)}) async-start(), calls=%async_computation.88 | async-start | bytes 1310720 | tf_op jit(solution)/shard_map/all_gather | solution.py:63
  1663.4 131.6 %all-gather.82.cloned.1.call-start = ((), (), s32[]{:S(2)}) async-start(), calls=%async_computation.80 | async-start | bytes 1310720 | tf_op jit(solution)/shard_map/all_gather | solution.py:63
  1677.7 253.8 %reduce-scatter.96.cloned.1.call-start = ((), (), s32[]{:S(2)}) async-start(), calls=%async_computation.97 | async-start | bytes 1310720 | tf_op jit(solution)/shard_map/reduce_scatter | solution.py:67
  1696.7 234.9 %reduce-scatter.72.cloned.1.call-start = ((), (), s32[]{:S(2)}) async-start(), calls=%async_computation.73 | async-start | bytes 1310720 | tf_op jit(solution)/shard_map/reduce_scatter | solution.py:67
  1726.6 205.0 %reduce-scatter.80.cloned.1.call-start = ((), (), s32[]{:S(2)}) async-start(), calls=%async_computation.81 | async-start | bytes 1310720 | tf_op jit(solution)/shard_map/reduce_scatter | solution.py:67
  1805.1 526.0 %reduce-scatter.98.cloned.1.call-start = ((), (), s32[]{:S(2)}) async-start(), calls=%async_computation.98 | async-start | bytes 28311552 | tf_op jit(solution)/shard_map/reduce_scatter | solution.py:431
  (475 other events, 12245.0 us)
Sparse Core Ops, SparseCore 0:
  10.8 179.1 all-gather.35
  304.8 24.8 reduce-scatter.57
  332.9 24.8 reduce-scatter.49
  361.1 24.8 reduce-scatter.41
  466.1 24.8 reduce-scatter.59
  521.5 24.9 reduce-scatter.43
  743.7 24.8 reduce-scatter.53
  771.0 24.8 reduce-scatter.45
  799.2 24.8 reduce-scatter.37
  902.8 24.8 reduce-scatter.63
  930.4 24.8 reduce-scatter.47
  958.5 24.8 reduce-scatter.39
  986.5 24.8 reduce-scatter.55
  1093.9 24.8 reduce-scatter.89
  1121.9 24.9 reduce-scatter.73
  1150.0 24.8 reduce-scatter.81
  1178.2 24.9 reduce-scatter.65
  1373.2 24.9 reduce-scatter.67
  1535.5 24.8 reduce-scatter.77
  1563.5 24.8 reduce-scatter.69
  1591.7 24.8 reduce-scatter.85
  1759.2 24.9 reduce-scatter.71
  1805.2 24.9 reduce-scatter.79
  1925.2 405.8 reduce-scatter.97
  (42 shorter events, 772.2 us)
where the time goes:
time: 2360 us; the launch traced here: 2350 us
  waiting for transfers between devices  1540 us (65%)
  matrix products  312 us (13%)
  other arithmetic  198 us (8%)
  local copies, waits for them, and re-layouts  160 us (7%)
  blocking collectives  106 us (4%)
    reduce_scatter x16, waiting for transfers between devices, branch_total(): lax.psum_scatter(partial_value.astype(jnp.bfloat16), 'chan', scatter_dime...  392 us
    reduce_scatter x1, waiting for transfers between devices, shards(): owned = lax.psum_scatter(placed, 'dp', scatter_dimension=0, tiled=True)  340 us
    reduce_scatter x16, waiting for transfers between devices, norm_backward(): lax.psum_scatter(partial_value.astype(jnp.bfloat16), 'chan', scatter_dime...  279 us
    all_gather x16, waiting for transfers between devices, gather_normed(): return lax.all_gather(normed, 'chan', axis=0, tiled=True)  182 us
    all_gather x1, waiting for transfers between devices, shards(): lax.all_gather(master.astype(jnp.bfloat16), 'dp', axis=0, tiled=True)  177 us
    all_gather x16, waiting for transfers between devices, gather_incoming(): lax.all_gather(upstream.astype(jnp.bfloat16), 'chan', axis=0, tiled=True)  166 us
    dot_general x44, matrix products, dot_rows(): lax.dot_general(left, right, (((1,), (1,)), ((), ())), preferred_element_...  119 us
    dot_general x44, matrix products, dot_plain(): return jnp.dot(left, right, preferred_element_type=jnp.float32)  95.9 us
  transfers between devices with their start and end apart: 66, of which 59 were waited for; matrix products, arithmetic and copies ran while one was open for 22% of the time, Pallas kernels for 0%

commit v1 on v0

v1 whole, which is shorter than its diff:
```python
import jax
import jax.numpy as jnp
from jax import lax
from jax.experimental import pallas as pl
from jax.experimental.pallas import tpu as pltpu
from jax.sharding import PartitionSpec as P

HEAD_DIM = 128
STEP = 10

norm_eps = 1e-05
masked_score = -1e30
beta_one = 0.9
beta_two = 0.98
adam_eps = 1e-08
tile_rate = 0.06
small_rate = 0.6
weight_decay = 0.01

BOTH = ("dp", "chan")
bf16 = jnp.bfloat16
f32 = jnp.float32


def dot_rows(left, right):
    return lax.dot_general(left, right, (((1,), (1,)), ((), ())), preferred_element_type=f32)


def dot_plain(left, right):
    return jnp.dot(left, right, preferred_element_type=f32)


def dot_cols(left, right):
    return lax.dot_general(left, right, (((0,), (0,)), ((), ())), preferred_element_type=f32)


def adamw_step(weight, gradient, first_old, second_old, rate, decay):
    first_new = beta_one * first_old + (1.0 - beta_one) * gradient
    second_new = beta_two * second_old + (1.0 - beta_two) * gradient * gradient
    first_hat = first_new / (1.0 - beta_one**STEP)
    second_hat = second_new / (1.0 - beta_two**STEP)
    weight_new = weight - rate * (first_hat / (jnp.sqrt(second_hat) + adam_eps) + decay * weight)
    return (first_new, second_new, weight_new)


def exchange(value, axis, mask):
    size = lax.axis_size(axis)
    return lax.ppermute(value, axis, [(i, i ^ mask) for i in range(size)])


def swap_blocks(value, axis):
    size = lax.axis_size(axis)
    me = lax.axis_index(axis)
    result = value
    for mask in range(1, size):
        sent = lax.dynamic_index_in_dim(value, me ^ mask, 0, keepdims=True)
        result = lax.dynamic_update_slice_in_dim(result, exchange(sent, axis, mask), me ^ mask, 0)
    return result


def gather_small(value, axis):
    size = lax.axis_size(axis)
    me = lax.axis_index(axis)
    result = jnp.zeros((size,) + value.shape, value.dtype)
    result = lax.dynamic_update_slice_in_dim(result, value[None], me, 0)
    for mask in range(1, size):
        result = lax.dynamic_update_slice_in_dim(
            result, exchange(value[None], axis, mask), me ^ mask, 0
        )
    return result


def butterfly_sum(value, axis):
    size = lax.axis_size(axis)
    mask = 1
    while mask < size:
        value = value + exchange(value, axis, mask)
        mask *= 2
    return value


def gather_tiles(own, tile_slot):
    slots, rows, width = own.shape
    chan_count = lax.axis_size("chan")
    everything = lax.all_gather(own, BOTH, axis=0, tiled=True)
    owner, place = tile_slot // slots, tile_slot % slots
    block = (owner[:, None] * chan_count + jnp.arange(chan_count)[None, :]) * slots + place[:, None]
    tiles = everything.at[block.reshape(-1)].get(mode="promise_in_bounds")
    return tiles.reshape(tile_slot.shape[0], chan_count * rows, width)


def reduce_tiles(grads, tile_slot, slots):
    tiles, full, width = grads.shape
    chan_count, dp_count = lax.axis_size("chan"), lax.axis_size("dp")
    rows = full // chan_count
    slot = jnp.arange(dp_count * slots, dtype=jnp.int32)
    hit = slot[:, None] == tile_slot[None, :]
    tile_of = jnp.argmax(hit, axis=1).astype(jnp.int32).reshape(dp_count, 1, slots)
    filled = jnp.any(hit, axis=1)
    block = (tile_of * chan_count + jnp.arange(chan_count)[None, :, None]).reshape(-1)
    placed = grads.reshape(tiles * chan_count, rows, width).at[block].get(mode="promise_in_bounds")
    placed = placed.reshape(dp_count * chan_count * slots, rows, width)
    total = lax.psum_scatter(placed, BOTH, scatter_dimension=0, tiled=True).astype(f32)
    mine = lax.dynamic_slice_in_dim(filled, lax.axis_index("dp") * slots, slots)
    return jnp.where(mine[:, None, None], total, 0.0)


def norm_stats(stream):
    mean = jnp.mean(stream, axis=-1, keepdims=True)
    center = stream - mean
    spread = jnp.mean(center * center, axis=-1, keepdims=True)
    return (mean, lax.rsqrt(spread + norm_eps))


def norm_apply(stream, stats, gain, bias):
    mean, inv = stats
    return (stream - mean) * inv * gain + bias


def norm_backward(stream, stats, gain, upstream):
    mean, inv = stats
    hat = (stream - mean) * inv
    scaled = upstream * gain
    back = (
        scaled
        - jnp.mean(scaled, axis=-1, keepdims=True)
        - hat * jnp.mean(scaled * hat, axis=-1, keepdims=True)
    ) * inv
    return (back, jnp.sum(upstream * hat, axis=0), jnp.sum(upstream, axis=0))


def masked_probs(query, key, valid):
    scores = dot_rows(query, key) * HEAD_DIM ** (-0.5)
    column = lax.broadcasted_iota(jnp.int32, scores.shape, 1)
    scores = jnp.where(column < valid, scores, masked_score)
    exponent = jnp.exp(scores - jnp.max(scores, axis=-1, keepdims=True))
    return exponent / jnp.sum(exponent, axis=-1, keepdims=True)


def attend_kernel(valid_ref, q_ref, k_ref, v_ref, out_ref):
    probs = masked_probs(q_ref[...], k_ref[...], valid_ref[0]).astype(bf16)
    out_ref[...] = dot_plain(probs, v_ref[...]).astype(bf16)


def attend_back_kernel(valid_ref, q_ref, k_ref, v_ref, g_ref, dq_ref, dk_ref, dv_ref):
    query, key, grad = q_ref[...], k_ref[...], g_ref[...]
    probs = masked_probs(query, key, valid_ref[0])
    grad_probs = dot_rows(grad, v_ref[...])
    row_dot = jnp.sum(probs * grad_probs, axis=-1, keepdims=True)
    grad_scores = (probs * (grad_probs - row_dot)).astype(bf16)
    scale = HEAD_DIM ** (-0.5)
    dq_ref[...] = (dot_plain(grad_scores, key) * scale).astype(bf16)
    dk_ref[...] = (dot_cols(grad_scores, query) * scale).astype(bf16)
    dv_ref[...] = dot_cols(probs.astype(bf16), grad).astype(bf16)


def head_call(kernel, valid, operands, out_count, flops):
    rows, width = operands[0].shape
    spec = pl.BlockSpec((rows, HEAD_DIM), lambda h: (0, h))
    shape = jax.ShapeDtypeStruct((rows, width), bf16)
    return pl.pallas_call(
        kernel,
        grid=(width // HEAD_DIM,),
        in_specs=[pl.BlockSpec(memory_space=pltpu.SMEM)] + [spec] * len(operands),
        out_specs=[spec] * out_count,
        out_shape=[shape] * out_count,
        cost_estimate=pl.CostEstimate(
            flops=flops * rows * rows * width,
            bytes_accessed=2 * rows * width * (len(operands) + out_count),
            transcendentals=rows * rows * width // HEAD_DIM,
        ),
        compiler_params=pltpu.CompilerParams(vmem_limit_bytes=48 * 1024 * 1024),
    )(valid, *operands)


def ffn_forward(stream, gain, bias, w_in, w_out):
    stats = norm_stats(stream)
    normed = norm_apply(stream, stats, gain, bias).astype(bf16)
    hidden = dot_rows(normed, w_in)
    sig = jax.nn.sigmoid(hidden)
    active = (hidden * sig).astype(bf16)
    slope = (sig * (1.0 + hidden * (1.0 - sig))).astype(bf16)
    return (stream + 0.5 * dot_plain(active, w_out), (stats, normed, active, slope))


def ffn_backward(upstream, stream, gain, kept, w_in, w_out):
    stats, normed, active, slope = kept
    incoming = (0.5 * upstream).astype(bf16)
    grad_out = dot_cols(active, incoming).astype(bf16)
    grad_hidden = (dot_rows(incoming, w_out) * slope.astype(f32)).astype(bf16)
    grad_in = dot_cols(grad_hidden, normed).astype(bf16)
    back, grad_gain, grad_bias = norm_backward(stream, stats, gain, dot_plain(grad_hidden, w_in))
    return (upstream + back, grad_in, grad_out, grad_gain, grad_bias)


def shift_rows(value, offset):
    rows = value.shape[0]
    if offset == 0:
        return value
    if offset > 0:
        return jnp.pad(value[offset:], ((0, offset), (0, 0)))
    return jnp.pad(value[: rows + offset], ((-offset, 0), (0, 0)))


def merge_stats(one, two):
    count_a, mean_a, dev_a = one
    count_b, mean_b, dev_b = two
    count = count_a + count_b
    mean = (count_a * mean_a + count_b * mean_b) / count
    gap = mean_a - mean_b
    return (count, mean, dev_a + dev_b + gap * gap * (count_a * count_b / count))


def shards(
    inputs,
    cotangent,
    lengths,
    tile_slot,
    master,
    tile_first,
    tile_second,
    norm_params,
    norm_first,
    norm_second,
    conv_params,
    conv_first,
    conv_second,
):
    micro, _, seg_rows, width = inputs.shape
    slots, rows_tile, _ = master.shape
    chan_count, dp_count = lax.axis_size("chan"), lax.axis_size("dp")
    chan_index = lax.axis_index("chan")
    assert micro == chan_count
    rows = seg_rows * chan_count
    tile_count = tile_slot.shape[0]
    quarter = (tile_count - 7) // 4
    base = 4 * quarter

    tiles = gather_tiles(master.astype(bf16), tile_slot)
    source = swap_blocks(inputs[:, 0], "chan").reshape(rows, width).astype(f32)
    upstream = swap_blocks(cotangent[:, 0], "chan").reshape(rows, width).astype(f32)
    convs = jnp.moveaxis(gather_small(conv_params, "chan"), 0, 1).reshape(-1, width)
    valid = lax.dynamic_slice_in_dim(lengths[:, 0], chan_index, 1)

    def stack_rows(first):
        return tiles[first : first + quarter].reshape(quarter * width, width)

    in_first, out_first = stack_rows(0), stack_rows(quarter)
    in_second, out_second = stack_rows(2 * quarter), stack_rows(3 * quarter)
    w_query, w_key, w_value, w_output, p_value, p_gate, p_output = [
        tiles[base + i] for i in range(7)
    ]
    gains, biases = norm_params[:5], norm_params[5:]
    taps = convs.shape[0] - 2
    margin = (taps - 1) // 2
    bn_gain, bn_bias = convs[taps], convs[taps + 1]
    frame_mask = (jnp.arange(rows, dtype=jnp.int32) < valid[0]).astype(f32)[:, None]

    stream_one, kept_one = ffn_forward(source, gains[0], biases[0], in_first, out_first)

    stats_att = norm_stats(stream_one)
    att_in = norm_apply(stream_one, stats_att, gains[1], biases[1]).astype(bf16)
    queries = dot_rows(att_in, w_query).astype(bf16)
    keys = dot_rows(att_in, w_key).astype(bf16)
    values = dot_rows(att_in, w_value).astype(bf16)
    (merged,) = head_call(attend_kernel, valid, (queries, keys, values), 1, 4)
    stream_two = stream_one + dot_plain(merged, w_output)

    stats_conv = norm_stats(stream_two)
    conv_in = norm_apply(stream_two, stats_conv, gains[2], biases[2]).astype(bf16)
    linear = dot_rows(conv_in, p_value)
    gate_sig = jax.nn.sigmoid(dot_rows(conv_in, p_gate))
    glu = linear * gate_sig * frame_mask
    depth = jnp.zeros_like(glu)
    for t in range(taps):
        depth = depth + convs[t] * shift_rows(glu, t - margin)
    count = valid[0].astype(f32)
    local_mean = jnp.sum(depth * frame_mask, axis=0) / count
    local_gap = (depth - local_mean) * frame_mask
    local_dev = jnp.sum(local_gap * local_gap, axis=0)
    stats = (jnp.full((width,), count), local_mean, local_dev)
    mask = 1
    while mask < dp_count:
        other = exchange(jnp.stack(stats), "dp", mask)
        stats = merge_stats(stats, (other[0], other[1], other[2]))
        mask *= 2
    total_count, bn_mean, bn_dev = stats
    inv_std = lax.rsqrt(bn_dev / total_count + norm_eps)
    center = depth - bn_mean
    normal = center * inv_std * bn_gain + bn_bias
    conv_sig = jax.nn.sigmoid(normal)
    conv_act = (normal * conv_sig).astype(bf16)
    stream_three = stream_two + dot_plain(conv_act, p_output)

    stream_four, kept_four = ffn_forward(stream_three, gains[3], biases[3], in_second, out_second)
    stats_last = norm_stats(stream_four)
    result = norm_apply(stream_four, stats_last, gains[4], biases[4]).astype(bf16)

    grad_four, gain_four, bias_four = norm_backward(stream_four, stats_last, gains[4], upstream)
    grad_three, gin_second, gout_second, gain_three, bias_three = ffn_backward(
        grad_four, stream_three, gains[3], kept_four, in_second, out_second
    )

    incoming = grad_three.astype(bf16)
    grad_po = dot_cols(conv_act, incoming).astype(bf16)
    conv_slope = conv_sig * (1.0 + normal * (1.0 - conv_sig))
    grad_normal = dot_rows(incoming, p_output) * conv_slope
    own_sums = jnp.stack([jnp.sum(grad_normal, axis=0), jnp.sum(grad_normal * center, axis=0)])
    sum_plain, sum_center = butterfly_sum(own_sums, "dp")
    bn_scale = bn_gain * inv_std
    grad_depth = bn_scale * grad_normal - frame_mask * bn_scale * (
        sum_plain + inv_std * inv_std * sum_center * center
    ) / total_count
    grad_glu = jnp.zeros_like(glu)
    tap_grads = []
    for t in range(taps):
        grad_glu = grad_glu + convs[t] * shift_rows(grad_depth, margin - t)
        tap_grads.append(jnp.sum(grad_depth * shift_rows(glu, t - margin), axis=0))
    grad_glu = grad_glu * frame_mask
    grad_linear = (grad_glu * gate_sig).astype(bf16)
    grad_gating = (grad_glu * linear * gate_sig * (1.0 - gate_sig)).astype(bf16)
    grad_pv = dot_cols(grad_linear, conv_in).astype(bf16)
    grad_pg = dot_cols(grad_gating, conv_in).astype(bf16)
    back, gain_two, bias_two = norm_backward(
        stream_two,
        stats_conv,
        gains[2],
        dot_plain(grad_linear, p_value) + dot_plain(grad_gating, p_gate),
    )
    grad_two = grad_three + back

    incoming = grad_two.astype(bf16)
    grad_wo = dot_cols(merged, incoming).astype(bf16)
    grad_merged = dot_rows(incoming, w_output).astype(bf16)
    grad_q, grad_k, grad_v = head_call(
        attend_back_kernel, valid, (queries, keys, values, grad_merged), 3, 10
    )
    grad_wq = dot_cols(grad_q, att_in).astype(bf16)
    grad_wk = dot_cols(grad_k, att_in).astype(bf16)
    grad_wv = dot_cols(grad_v, att_in).astype(bf16)
    back, gain_one, bias_one = norm_backward(
        stream_one,
        stats_att,
        gains[1],
        dot_plain(grad_q, w_query) + dot_plain(grad_k, w_key) + dot_plain(grad_v, w_value),
    )
    grad_one = grad_two + back

    grad_zero, gin_first, gout_first, gain_zero, bias_zero = ffn_backward(
        grad_one, source, gains[0], kept_one, in_first, out_first
    )

    grads = jnp.concatenate(
        [gin_first, gout_first, gin_second, gout_second]
        + [grad_wq, grad_wk, grad_wv, grad_wo, grad_pv, grad_pg, grad_po]
    ).reshape(tile_count, width, width)
    owned = reduce_tiles(grads, tile_slot, slots)

    small = jnp.stack(
        [gain_zero, gain_one, gain_two, gain_three, gain_four]
        + [bias_zero, bias_one, bias_two, bias_three, bias_four]
        + tap_grads
        + [own_sums[1] * inv_std, own_sums[0]]
    )
    small = butterfly_sum(butterfly_sum(small, "dp"), "chan")
    norm_total = small[: norm_params.shape[0]]
    conv_grad = lax.dynamic_slice_in_dim(
        small[norm_params.shape[0] :], chan_index * rows_tile, rows_tile, 1
    )

    tile_m, tile_v, tile_w = adamw_step(
        master, owned, tile_first, tile_second, tile_rate, weight_decay
    )
    norm_m, norm_v, norm_w = adamw_step(
        norm_params, norm_total, norm_first, norm_second, small_rate, 0.0
    )
    conv_m, conv_v, conv_w = adamw_step(
        conv_params, conv_grad, conv_first, conv_second, small_rate, 0.0
    )
    block_out = swap_blocks(result.reshape(chan_count, seg_rows, width), "chan")
    block_grad = swap_blocks(
        grad_zero.astype(bf16).reshape(chan_count, seg_rows, width), "chan"
    ).astype(f32)
    return (
        block_out[:, None],
        block_grad[:, None],
        tile_m,
        tile_v,
        tile_w,
        tile_w.astype(bf16),
        norm_m,
        norm_v,
        norm_w,
        conv_m,
        conv_v,
        conv_w,
    )


def solution(mesh):
    in_specs = (
        P(None, "dp", "chan", None),
        P(None, "dp", "chan", None),
        P(None, "dp"),
        P(),
        P("dp", "chan", None),
        P("dp", "chan", None),
        P("dp", "chan", None),
        P(),
        P(),
        P(),
        P(None, "chan"),
        P(None, "chan"),
        P(None, "chan"),
    )
    out_specs = (
        P(None, "dp", "chan", None),
        P(None, "dp", "chan", None),
        P("dp", "chan", None),
        P("dp", "chan", None),
        P("dp", "chan", None),
        P("dp", "chan", None),
        P(),
        P(),
        P(),
        P(None, "chan"),
        P(None, "chan"),
        P(None, "chan"),
    )
    return jax.shard_map(shards, mesh=mesh, in_specs=in_specs, out_specs=out_specs, check_vma=False)
```

time: 2360 us -> 1090 us (0.46)
  waiting for transfers between devices: 1540 us -> 686 us
  other arithmetic: 198 us -> 42.5 us
  matrix products: 312 us -> 161 us
  blocking collectives: 106 us -> 0 us
  local copies, waits for them, and re-layouts: 160 us -> 131 us
  Pallas kernels: 0 us -> 23.9 us
    reduce_scatter x33 -> x1, waiting for transfers between devices: 1010 us -> 394 us  [reduce_tiles(): lax.psum_scatter(placed, BOTH, scatter_dimension=0, tiled=True).astype(f32)]
    all_gather x33 -> x1, waiting for transfers between devices: 526 us -> 238 us  [gather_tiles(): everything = lax.all_gather(own, BOTH, axis=0, tiled=True)]
    psum x4 -> x0, blocking collectives: 106 us -> none  [the longest x1 43.6 us: shards(): norm_total, taps_total = lax.psum((norm_acc, taps_wide), ('dp', 'chan'))]
    unnamed x882 -> x195, local copies, waits for them, and re-layouts: 87.5 us -> 16.7 us
    dot_general x44 -> x11, matrix products: 119 us -> 55.9 us  [dot_rows(): lax.dot_general(left, right, (((1,), (1,)), ((), ())), preferred_element_...]
    reduce_sum x57 -> x11, other arithmetic: 76.1 us -> 13.5 us  [the longest x1 7.2 us: shards(): tap_grads.append(jnp.sum(grad_depth * shift_rows(glu, t - margin), axis=0))]
    dot_general x68 -> x11, matrix products: 107 us -> 48.2 us  [dot_plain(): return jnp.dot(left, right, preferred_element_type=f32)]
    gather x1 -> x2, local copies, waits for them, and re-layouts: 10.5 us -> 67.5 us  [the longest x1 34 us: reduce_tiles(): grads.reshape(tiles * chan_count, rows, width).at[block]]
  transfers between devices with their start and end apart: 66 -> 28, of which waited for: 59 -> 16; matrix products, arithmetic and copies ran while one was open for 22% -> 11% of each run, Pallas kernels for 0% -> 1%
where the time goes in v1:
time: 1090 us; the launch traced here: 1080 us
  waiting for transfers between devices  686 us (63%)
  matrix products  161 us (15%)
  local copies, waits for them, and re-layouts  131 us (12%)
  other arithmetic  42.5 us (4%)
  Pallas kernels  23.9 us (2%)
  starting transfers between devices  23.7 us (2%)
  between operations  16.4 us (2%)
    reduce_scatter x1, waiting for transfers between devices, reduce_tiles(): lax.psum_scatter(placed, BOTH, scatter_dimension=0, tiled=True).astype(f32)  394 us
    all_gather x1, waiting for transfers between devices, gather_tiles(): everything = lax.all_gather(own, BOTH, axis=0, tiled=True)  238 us
    dot_general x11, matrix products, dot_cols(): lax.dot_general(left, right, (((0,), (0,)), ((), ())), preferred_element_...  57.3 us
    dot_general x11, matrix products, dot_rows(): lax.dot_general(left, right, (((1,), (1,)), ((), ())), preferred_element_...  55.9 us
    ppermute x26, waiting for transfers between devices, exchange(): return lax.ppermute(value, axis, [(i, i ^ mask) for i in range(size)])  54.3 us
    dot_general x11, matrix products, dot_plain(): return jnp.dot(left, right, preferred_element_type=f32)  48.2 us
    gather x1, local copies, waits for them, and re-layouts, reduce_tiles(): grads.reshape(tiles * chan_count, rows, width).at[block]  34 us
    gather x1, local copies, waits for them, and re-layouts, gather_tiles(): tiles = everything.at[block.reshape(-1)].get(mode='promise_in_bounds')  33.5 us
  transfers between devices with their start and end apart: 28, of which 16 were waited for; matrix products, arithmetic and copies ran while one was open for 11% of the time, Pallas kernels for 1%

profile of v1, /device:TPU:0, one launch (start us, length us, event | category | flops | bytes accessed | tf_op | source)
XLA Modules:
  0.0 1084.7 jit_solution(423892303671060007)
XLA Ops:
  27.3 17.7 %collective-permute-done.1 = bf16[1,128,1024]{2,1,0:T(8,128)(2,1)} collective-permute-done((bf16[1,128,1024]{2,1,0:T(8,128)(2,1)}, bf16[1,128,1024]{2,1,0:T(8,128)(2,1)}, u32[]{:S(2)}, u32[]{:S(2)}) %collective-permute-start.1) | collective-permute-done | bytes 262176 | tf_op jit(solution)/shard_map/ppermute | solution.py:48
  46.0 6.5 collective-permute-done.2
  56.0 238.0 %all-gather.2.cloned.1.call-done = bf16[96,256,1024]{2,1,0:T(8,128)(2,1)} async-done(((bf16[3,256,1024]{2,1,0:T(8,128)(2,1)}), bf16[96,256,1024]{2,1,0:T(8,128)(2,1)}) %all-gather.2.cloned.1.call-update) | async-done | bytes 50331664 | tf_op jit(solution)/shard_map/all_gather | solution.py:85
  294.0 33.5 %gather_fusion = bf16[92,256,1024]{2,1,0:T(8,128)(2,1)} fusion(bf16[96,256,1024]{2,1,0:T(8,128)(2,1)} %all-gather.2.cloned.1.call-done, s32[1024]{0:T(1024)S(1)} %pad_clamp_fusion.1), kind=kCustom, calls=%fused_computation | custom fusion | bytes 96469360 | tf_op jit(solution)/shard_map/gather | solution.py:88
  327.5 22.8 %fusion.56 = (bf16[16,256,1024]{2,1,0:T(8,128)(2,1)}, bf16[16,256,1024]{2,1,0:T(8,128)(2,1)}, bf16[16,256,1024]{2,1,0:T(8,128)(2,1)}, bf16[16,256,1024]{2,1,0:T(8,128)(2,1)}) fusion(bf16[92,256,1024]{2,1,0:T(8,128)(2,1)} %gather_fusion), kind=kLoop, calls=%fused_computation.228 | loop fusion | bytes 67108864 | tf_op jit(solution)/shard_map/slice | solution.py:246
  350.4 8.7 fusion.57
  361.7 6.8 fusion.68
  368.5 9.6 fusion.64
  383.0 9.6 shard_map.220
  420.4 10.8 fusion.49
  431.2 7.9 fusion.67
  442.7 12.1 %multiply_convert_fusion.2 = bf16[512,4096]{1,0:T(8,128)(2,1)} fusion(bf16[4096,1024]{1,0:T(8,128)(2,1)} %bitcast.229, f32[512,4096]{1,0:T(8,128)} %fusion.49, f32[512,1024]{1,0:T(8,128)S(1)} %get-tuple-element.79), kind=kOutput, calls=%fused_computation.8 | convolution fusion | flops 4319084544 | bytes 23068672 | tf_op jit(solution)/shard_map/dot_general | solution.py:26
  454.8 7.9 multiply_reduce_fusion.5
  480.4 7.2 multiply_reduce_fusion
  502.9 14.3 %shard_map.221 = (bf16[512,1024]{1,0:T(8,128)(2,1)S(1)}, bf16[512,1024]{1,0:T(8,128)(2,1)S(1)}, bf16[512,1024]{1,0:T(8,128)(2,1)S(1)}) custom-call(s32[1]{0:T(128)} %bitcast.11.valid_ref, bf16[512,1024]{1,0:T(8,128)(2,1)S(1)} %convolution_convert_fusion.3.q_ref, bf16[512,1024]{1,0:T(8,128)(2,1)S(1)} %convolution_convert_fusion.2.k_ref, ...), custom_call_target="tpu_custom_call" | custom-call | flops 2684354560 | bytes 7340032 | tf_op jit(solution)/shard_map/pallas_call | solution.py:161
  524.4 12.5 %multiply_convert_fusion = bf16[512,4096]{1,0:T(8,128)(2,1)} fusion(bf16[4096,1024]{1,0:T(8,128)(2,1)} %bitcast.224, f32[512,4096]{1,0:T(8,128)} %fusion.68, f32[512,1024]{1,0:T(8,128)S(1)} %multiply_add_fusion.1), kind=kOutput, calls=%fused_computation.6 | convolution fusion | flops 4319084544 | bytes 23068672 | tf_op jit(solution)/shard_map/dot_general | solution.py:26
  537.0 11.1 %fusion.26 = (f32[1024]{0:T(1024)S(1)}, f32[512]{0:T(512)S(1)}, f32[512]{0:T(512)S(1)}, f32[1024]{0:T(1024)S(1)}, bf16[512,1024]{1,0:T(8,128)(2,1)S(1)}, /*index=5*/f32[512,1024]{1,0:T(8,128)}) fusion(bf16[4,128,1024]{2,1,0:T(8,128)(2,1)S(1)} %copy-done.7, f32[512]{0:T(512)S(1)} %copy-done.76, f32[512]{0:T(512)S(1)} %copy-done.75, f32[1024]{0:T(1024)S(1)} %bitcast.282, ...), kind=kOutput, calls=%fused_computation.52 | convolution fusion | flops 4301779968 | bytes 16801792 | tf_op jit(solution)/shard_map/dot_general | solution.py:30
  548.1 6.8 convert_dynamic-update-slice_fusion.3
  554.9 11.0 %convert_dynamic-update-slice_fusion.2 = bf16[23552,1024]{1,0:T(8,128)(2,1)} fusion(bf16[23552,1024]{1,0:T(8,128)(2,1)} %convert_dynamic-update-slice_fusion.3, f32[512,1024]{1,0:T(8,128)S(1)} %multiply_add_fusion.1, f32[512,4096]{1,0:T(8,128)} %fusion.68), kind=kOutput, calls=%fused_computation.4 | convolution fusion | flops 4310695936 | bytes 18874368 | tf_op jit(solution)/shard_map/dot_general | solution.py:34
  565.9 9.6 convert_dynamic-update-slice_fusion.1
  575.4 11.1 %convert_dynamic-update-slice_fusion = bf16[23552,1024]{1,0:T(8,128)(2,1)} fusion(bf16[23552,1024]{1,0:T(8,128)(2,1)} %convert_dynamic-update-slice_fusion.1, f32[512,1024]{1,0:T(8,128)S(1)} %copy-done.29, f32[512,4096]{1,0:T(8,128)} %fusion.49), kind=kOutput, calls=%fused_computation.2 | convolution fusion | flops 4310695936 | bytes 18874368 | tf_op jit(solution)/shard_map/dot_general | solution.py:34
  605.5 34.0 %gather_fusion.1 = bf16[96,256,1024]{2,1,0:T(8,128)(2,1)} fusion(bf16[92,256,1024]{2,1,0:T(8,128)(2,1)} %bitcast.214, s32[1024]{0:T(1024)S(1)} %pad_clamp_fusion), kind=kCustom, calls=%fused_computation.1 | custom fusion | bytes 100663680 | tf_op jit(solution)/shard_map/gather | solution.py:101
  675.6 393.9 %reduce-scatter.2.cloned.1.call-done = bf16[3,256,1024]{2,1,0:T(8,128)(2,1)} async-done(((bf16[96,256,1024]{2,1,0:T(8,128)(2,1)}), bf16[3,256,1024]{2,1,0:T(8,128)(2,1)}) %reduce-scatter.2.cloned.1.call-update) | async-done | bytes 1572880 | tf_op jit(solution)/shard_map/reduce_scatter | solution.py:103
  1069.5 8.1 fusion.53
  (383 shorter events, 156.6 us)
Async XLA Ops:
  7.2 286.8 %all-gather.2.cloned.1.call-start = ((), (), s32[]{:S(2)}) async-start(), calls=%async_computation.1 | async-start | bytes 51904512 | tf_op jit(solution)/shard_map/all_gather | solution.py:85
  11.3 1058.2 %reduce-scatter.2.cloned.1.call-start = ((), (), s32[]{:S(2)}) async-start(), calls=%async_computation.2 | async-start | bytes 51904512 | tf_op jit(solution)/shard_map/reduce_scatter | solution.py:103
  11.3 10.2 collective-permute-start.3
  11.8 9.8 collective-permute-start.4
  14.4 7.6 collective-permute-start.5
  14.6 9.7 collective-permute-start.12
  14.8 10.5 collective-permute-start.13
  21.5 385.9 %collective-permute-start.14 = (bf16[1,128,1024]{2,1,0:T(8,128)(2,1)S(1)}, bf16[1,128,1024]{2,1,0:T(8,128)(2,1)}, u32[]{:S(2)}, u32[]{:S(2)}) collective-permute-start(bf16[1,128,1024]{2,1,0:T(8,128)(2,1)S(1)} %get-tuple-element.93), channel_id=1, source_target_pairs={{0,3},{1,2},{2,1},{3,0},{4,7},{5,6},{6,5},{7,4},{8,11},{9,10},{10,... | collective-permute-start | bytes 786440 | tf_op jit(solution)/shard_map/ppermute | solution.py:48
  21.7 4.7 collective-permute-start
  22.1 23.0 %collective-permute-start.1 = (bf16[1,128,1024]{2,1,0:T(8,128)(2,1)}, bf16[1,128,1024]{2,1,0:T(8,128)(2,1)}, u32[]{:S(2)}, u32[]{:S(2)}) collective-permute-start(bf16[1,128,1024]{2,1,0:T(8,128)(2,1)} %get-tuple-element.101), channel_id=1, source_target_pairs={{0,2},{1,3},{2,0},{3,1},{4,6},{5,7},{6,4},{7,5},{8,10},{9,11},{10,... | collective-permute-start | bytes 786440 | tf_op jit(solution)/shard_map/ppermute | solution.py:48
  24.2 28.3 %collective-permute-start.2 = (bf16[1,128,1024]{2,1,0:T(8,128)(2,1)S(1)}, bf16[1,128,1024]{2,1,0:T(8,128)(2,1)S(1)}, u32[]{:S(2)}, u32[]{:S(2)}) collective-permute-start(bf16[1,128,1024]{2,1,0:T(8,128)(2,1)S(1)} %get-tuple-element.99), channel_id=1, source_target_pairs={{0,3},{1,2},{2,1},{3,0},{4,7},{5,6},{6,5},{7,4},{8,11},{9,10},{10,... | collective-permute-start | bytes 786440 | tf_op jit(solution)/shard_map/ppermute | solution.py:48
  413.7 4.7 collective-permute-start.8
  475.1 4.6 collective-permute-start.17
  641.5 20.0 %collective-permute-start.9 = (bf16[1,128,1024]{2,1,0:T(8,128)(2,1)}, bf16[1,128,1024]{2,1,0:T(8,128)(2,1)}, u32[]{:S(2)}, u32[]{:S(2)}) collective-permute-start(bf16[1,128,1024]{2,1,0:T(8,128)(2,1)} %get-tuple-element.98), channel_id=1, source_target_pairs={{0,1},{1,0},{2,3},{3,2},{4,5},{5,4},{6,7},{7,6},{8,9},{9,8},{10,11... | collective-permute-start | bytes 786440 | tf_op jit(solution)/shard_map/ppermute | solution.py:48
  641.5 21.2 %collective-permute-start.10 = (bf16[1,128,1024]{2,1,0:T(8,128)(2,1)}, bf16[1,128,1024]{2,1,0:T(8,128)(2,1)}, u32[]{:S(2)}, u32[]{:S(2)}) collective-permute-start(bf16[1,128,1024]{2,1,0:T(8,128)(2,1)} %get-tuple-element.97), channel_id=1, source_target_pairs={{0,2},{1,3},{2,0},{3,1},{4,6},{5,7},{6,4},{7,5},{8,10},{9,11},{10,... | collective-permute-start | bytes 786440 | tf_op jit(solution)/shard_map/ppermute | solution.py:48
  643.0 21.4 %collective-permute-start.11 = (bf16[1,128,1024]{2,1,0:T(8,128)(2,1)S(1)}, bf16[1,128,1024]{2,1,0:T(8,128)(2,1)}, u32[]{:S(2)}, u32[]{:S(2)}) collective-permute-start(bf16[1,128,1024]{2,1,0:T(8,128)(2,1)S(1)} %get-tuple-element.96), channel_id=1, source_target_pairs={{0,3},{1,2},{2,1},{3,0},{4,7},{5,6},{6,5},{7,4},{8,11},{9,10},{10,... | collective-permute-start | bytes 786440 | tf_op jit(solution)/shard_map/ppermute | solution.py:48
  643.6 5.0 collective-permute-start.21
  648.7 4.7 collective-permute-start.22
  653.4 6.7 collective-permute-start.23
  655.0 10.4 collective-permute-start.18
  660.1 8.2 collective-permute-start.19
  661.6 10.5 collective-permute-start.20
  662.7 5.7 collective-permute-start.24
  668.5 5.7 collective-permute-start.25
  (96 other events, 1551.7 us)
Sparse Core Ops, SparseCore 0:
  11.5 282.4 all-gather.1
  639.8 429.6 reduce-scatter.1

commit v2 on v1

--- a/solution.py
+++ b/solution.py
@@ -79,30 +79,293 @@
     return value
 
 
-def gather_tiles(own, tile_slot):
-    slots, rows, width = own.shape
-    chan_count = lax.axis_size("chan")
-    everything = lax.all_gather(own, BOTH, axis=0, tiled=True)
-    owner, place = tile_slot // slots, tile_slot % slots
-    block = (owner[:, None] * chan_count + jnp.arange(chan_count)[None, :]) * slots + place[:, None]
-    tiles = everything.at[block.reshape(-1)].get(mode="promise_in_bounds")
-    return tiles.reshape(tile_slot.shape[0], chan_count * rows, width)
+BITS = {"core": 1, "y": 2, "x": 4, "z1": 8, "z2": 16}
+ORDERS = (
+    ("z2", "y", "z1", "x"),
+    ("z1", "z2", "y", "x"),
+    ("z2", "y", "x", "z1"),
+    ("z1", "x", "y", "z2"),
+    ("z2", "z1", "x", "y"),
+    ("z1", "x", "z2", "y"),
+)
+LAST = (("x", (0, 1)), ("z1", (2,)), ("z2", (3,)), ("y", (4, 5)))
+HALVES = 2
+
+
+def is_slice(dp_count, chan_count, slots):
+    return (dp_count, chan_count, slots) == (8, 4, 3)
+
+
+def swap(value, name):
+    size = lax.axis_size("dp") * lax.axis_size("chan")
+    return lax.ppermute(value, BOTH, [(i, i ^ BITS[name]) for i in range(size)])
+
+
+def step_groups(step, orders):
+    groups = {}
+    for part, order in enumerate(orders):
+        groups.setdefault(order[step], []).append(part)
+    return groups
+
+
+def block_rows(own):
+    half = own.shape[1] // HALVES
+    return [own[p // HALVES, (p % HALVES) * half : (p % HALVES + 1) * half][None] for p in range(6)]
+
+
+def gather_parts(own, extra, small):
+    own = lax.optimization_barrier(own)
+    state = block_rows(own)
+    moved = []
+    for step in range(4):
+        groups = step_groups(step, ORDERS)
+        sent = {
+            name: (jnp.concatenate([state[p] for p in parts]) if len(parts) > 1 else state[parts[0]])
+            for name, parts in groups.items()
+        }
+        if step == 0:
+            half = own.shape[1] // HALVES
+            sent = {ORDERS[h][0]: own[:, h * half : (h + 1) * half] for h in range(HALVES)}
+            sent, extra = lax.optimization_barrier((sent, extra))
+            moved = [exchange(value, "chan", mask + 1) for mask, value in enumerate(extra)]
+        elif step == 1:
+            sent, small = lax.optimization_barrier((sent, small))
+            small = jnp.stack([small, exchange(small, "chan", 2)])
+        elif step == 2:
+            sent, small = lax.optimization_barrier((sent, small))
+            small = jnp.concatenate([small, exchange(small, "chan", 1)])
+        else:
+            sent = lax.optimization_barrier(sent)
+        got = {name: swap(value, name) for name, value in sent.items()}
+        if step == 3:
+            return ([sent[n] for n, _ in LAST], [got[n] for n, _ in LAST], moved, small)
+        got, moved, small = lax.optimization_barrier((got, moved, small))
+        size = 1 << step
+        for name, parts in groups.items():
+            for i, p in enumerate(parts):
+                state[p] = jnp.concatenate([state[p], got[name][i * size : (i + 1) * size]])
+
+
+def place_of(part, bits):
+    order = ORDERS[part]
+    index = bits[order[2]] * 4 + bits[order[1]] * 2 + bits[order[0]]
+    for _, parts in LAST:
+        if part in parts:
+            return (bits[order[3]], index + 8 * parts.index(part))
+
+
+def slot_places(slot, slots):
+    owner = slot // slots
+    gap = owner ^ lax.axis_index("dp")
+    bits = {"x": gap & 1, "z1": (gap >> 1) & 1, "z2": (gap >> 2) & 1}
+    rows = []
+    for dy in range(2):
+        for h in range(HALVES):
+            at = [place_of(s * HALVES + h, dict(bits, y=jnp.full_like(gap, dy))) for s in range(slots)]
+            position = slot % slots
+            far = jnp.select([position == s for s in range(slots)], [a[0] for a in at])
+            index = jnp.select([position == s for s in range(slots)], [a[1] for a in at])
+            rows.append((far * 16 + index).astype(jnp.int32))
+    return (slot % slots).astype(jnp.int32), jnp.stack(rows)
+
+
+def array_of(position, h):
+    part = position * HALVES + h
+    return [i for i, (_, parts) in enumerate(LAST) if part in parts][0]
+
+
+def staged(count, depth, load, drain_in, store, drain_out):
+    ahead = depth // 2
+    for i in range(count + ahead):
+        if i < count:
+            if i >= depth:
+                drain_out(i - depth)
+            load(i)
+        if i >= ahead:
+            drain_in(i - ahead)
+            store(i - ahead)
+    for i in range(max(count - depth, 0), count):
+        drain_out(i)
+
+
+DEPTH = 8
+
+
+def when_placed(position_ref, place_ref, tile, b, act):
+    place = place_ref[b, tile]
+    index = lax.rem(place, 16)
+    for s in range(3):
+        for far in range(2):
+
+            @pl.when((position_ref[tile] == s) & (place // 16 == far))
+            def _():
+                act(array_of(s, b % HALVES), far, index)
+
+
+def assemble_kernel(sizes, position_ref, place_ref, *refs):
+    sources, outs = refs[:16], refs[16 : 16 + len(sizes)]
+    buffer, in_sem, out_sem = refs[16 + len(sizes) :]
+    items, first = [], 0
+    for g, count in enumerate(sizes):
+        items += [(core, g, j, first + j) for core in range(2) for j in range(count)]
+        first += count
+
+    def load(i):
+        core, _, _, tile = items[i]
+        for b in range(4):
+            when_placed(
+                position_ref,
+                place_ref,
+                tile,
+                b,
+                lambda array, far, index: pltpu.make_async_copy(
+                    sources[core * 8 + far * 4 + array].at[index],
+                    buffer.at[i % DEPTH, b],
+                    in_sem.at[i % DEPTH],
+                ).start(),
+            )
+
+    def drain_in(i):
+        slot = buffer.at[i % DEPTH]
+        pltpu.make_async_copy(slot, slot, in_sem.at[i % DEPTH]).wait()
+
+    def out_copy(i):
+        core, g, j, _ = items[i]
+        return pltpu.make_async_copy(
+            buffer.at[i % DEPTH], outs[g].at[core, j], out_sem.at[i % DEPTH]
+        )
+
+    staged(
+        len(items), DEPTH, load, drain_in, lambda i: out_copy(i).start(), lambda i: out_copy(i).wait()
+    )
+
+
+def gather_tiles_here(own, tile_slot, sizes, extra, small):
+    near, far, moved, small = gather_parts(own, extra, small)
+    near_other = [swap(v, "core") for v in near]
+    far_other = [swap(v, "core") for v in far]
+    position, place = slot_places(tile_slot, own.shape[0])
+    rows, width = near[0].shape[1:]
+    anywhere = pl.BlockSpec(memory_space=pl.ANY)
+    smem = pl.BlockSpec(memory_space=pltpu.SMEM)
+    mats = pl.pallas_call(
+        lambda *refs: assemble_kernel(sizes, *refs),
+        in_specs=[smem, smem] + [anywhere] * 16,
+        out_specs=[anywhere] * len(sizes),
+        out_shape=[jax.ShapeDtypeStruct((2, n, 4, rows, width), own.dtype) for n in sizes],
+        scratch_shapes=[
+            pltpu.VMEM((DEPTH, 4, rows, width), own.dtype),
+            pltpu.SemaphoreType.DMA((DEPTH,)),
+            pltpu.SemaphoreType.DMA((DEPTH,)),
+        ],
+        compiler_params=pltpu.CompilerParams(vmem_limit_bytes=32 * 1024 * 1024),
+    )(position, place, *near, *far, *near_other, *far_other)
+    return [m.reshape(-1, width) for m in mats], moved, small
+
+
+def scatter_kernel(sizes, position_ref, place_ref, *refs):
+    sources, outs = refs[: len(sizes)], refs[len(sizes) : len(sizes) + 8]
+    buffer, in_sem, out_sem = refs[len(sizes) + 8 :]
+    items = [(g, j) for g, count in enumerate(sizes) for j in range(count)]
+
+    def in_copy(i):
+        g, j = items[i]
+        return pltpu.make_async_copy(
+            sources[g].at[j], buffer.at[i % DEPTH], in_sem.at[i % DEPTH]
+        )
+
+    def store(i):
+        for b in range(4):
+            when_placed(
+                position_ref,
+                place_ref,
+                i,
+                b,
+                lambda array, far, index: pltpu.make_async_copy(
+                    buffer.at[i % DEPTH, b],
+                    outs[far * 4 + array].at[index],
+                    out_sem.at[i % DEPTH],
+                ).start(),
+            )
+
+    def drain_out(i):
+        slot = buffer.at[i % DEPTH]
+        pltpu.make_async_copy(slot, slot, out_sem.at[i % DEPTH]).wait()
+
+    staged(
+        len(items),
+        DEPTH,
+        lambda i: in_copy(i).start(),
+        lambda i: in_copy(i).wait(),
+        store,
+        drain_out,
+    )
+
+
+def reduce_tiles_here(halves, tile_slot, slots, sizes, small):
+    rows, width = halves[0].shape[2:]
+    position, place = slot_places(tile_slot, slots)
+    anywhere = pl.BlockSpec(memory_space=pl.ANY)
+    smem = pl.BlockSpec(memory_space=pltpu.SMEM)
+    shapes = [jax.ShapeDtypeStruct((8 * len(parts), rows, width), bf16) for _, parts in LAST]
+    arrays = pl.pallas_call(
+        lambda *refs: scatter_kernel(sizes, *refs),
+        in_specs=[smem, smem] + [anywhere] * len(sizes),
+        out_specs=[anywhere] * 8,
+        out_shape=shapes + shapes,
+        scratch_shapes=[
+            pltpu.VMEM((DEPTH, 4, rows, width), bf16),
+            pltpu.SemaphoreType.DMA((DEPTH,)),
+            pltpu.SemaphoreType.DMA((DEPTH,)),
+        ],
+        compiler_params=pltpu.CompilerParams(vmem_limit_bytes=32 * 1024 * 1024),
+    )(position, place, *halves)
+    keep = {n: a for (n, _), a in zip(LAST, arrays[:4])}
+    send = {n: a for (n, _), a in zip(LAST, arrays[4:])}
+    state = [None] * 6
+    for step in range(3, -1, -1):
+        groups = step_groups(step, ORDERS)
+        if step < 3:
+            send, keep = {}, {}
+            size = 1 << step
+            for name, parts in groups.items():
+                send[name] = jnp.concatenate([state[p][size:] for p in parts]).astype(bf16)
+                keep[name] = jnp.concatenate([state[p][:size] for p in parts]).astype(bf16)
+        send, small = lax.optimization_barrier((send, small))
+        got = {name: swap(value, name) for name, value in send.items()}
+        small = small + swap(small, ("z2", "z1", "x", "y")[step])
+        got, small = lax.optimization_barrier((got, small))
+        size = 1 << step
+        for name, parts in groups.items():
+            for i, p in enumerate(parts):
+                cut = slice(i * size, (i + 1) * size)
+                state[p] = keep[name][cut].astype(f32) + got[name][cut].astype(f32)
+    return jnp.concatenate(state).reshape(slots, HALVES * rows, width), small
+
+
+def owned_mask(tile_slot, slots):
+    slot = lax.axis_index("dp") * slots + jnp.arange(slots, dtype=jnp.int32)
+    return jnp.any(slot[:, None] == tile_slot[None, :], axis=1)[:, None, None]
+
+
+def gather_tiles(own, tile_slot, sizes):
+    width = own.shape[2]
+    strips = lax.all_gather(own, "dp", axis=0, tiled=True)
+    strips = strips.at[tile_slot].get(mode="promise_in_bounds")
+    whole = lax.all_gather(strips, "chan", axis=1, tiled=True)
+    mats, first = [], 0
+    for n in sizes:
+        mats.append(whole[first : first + n].reshape(-1, width))
+        first += n
+    return mats
 
 
 def reduce_tiles(grads, tile_slot, slots):
-    tiles, full, width = grads.shape
-    chan_count, dp_count = lax.axis_size("chan"), lax.axis_size("dp")
-    rows = full // chan_count
-    slot = jnp.arange(dp_count * slots, dtype=jnp.int32)
-    hit = slot[:, None] == tile_slot[None, :]
-    tile_of = jnp.argmax(hit, axis=1).astype(jnp.int32).reshape(dp_count, 1, slots)
-    filled = jnp.any(hit, axis=1)
-    block = (tile_of * chan_count + jnp.arange(chan_count)[None, :, None]).reshape(-1)
-    placed = grads.reshape(tiles * chan_count, rows, width).at[block].get(mode="promise_in_bounds")
-    placed = placed.reshape(dp_count * chan_count * slots, rows, width)
-    total = lax.psum_scatter(placed, BOTH, scatter_dimension=0, tiled=True).astype(f32)
-    mine = lax.dynamic_slice_in_dim(filled, lax.axis_index("dp") * slots, slots)
-    return jnp.where(mine[:, None, None], total, 0.0)
+    slot = jnp.arange(lax.axis_size("dp") * slots, dtype=jnp.int32)
+    tile_of = jnp.argmax(slot[:, None] == tile_slot[None, :], axis=1).astype(jnp.int32)
+    strips = lax.psum_scatter(grads, "chan", scatter_dimension=1, tiled=True)
+    placed = strips.at[tile_of].get(mode="promise_in_bounds")
+    return lax.psum_scatter(placed, "dp", scatter_dimension=0, tiled=True).astype(f32)
 
 
 def norm_stats(stream):
@@ -183,12 +446,20 @@
     return (stream + 0.5 * dot_plain(active, w_out), (stats, normed, active, slope))
 
 
-def ffn_backward(upstream, stream, gain, kept, w_in, w_out):
+def weight_grad(left, right, local):
+    if not local:
+        return dot_cols(left, right).astype(bf16)
+    half = left.shape[1] // 2
+    other = swap(dot_cols(left[:, half:], right).astype(bf16), "core")
+    return (dot_cols(left[:, :half], right) + other.astype(f32)).astype(bf16)
+
+
+def ffn_backward(upstream, stream, gain, kept, w_in, w_out, local):
     stats, normed, active, slope = kept
     incoming = (0.5 * upstream).astype(bf16)
-    grad_out = dot_cols(active, incoming).astype(bf16)
+    grad_out = weight_grad(active, incoming, local)
     grad_hidden = (dot_rows(incoming, w_out) * slope.astype(f32)).astype(bf16)
-    grad_in = dot_cols(grad_hidden, normed).astype(bf16)
+    grad_in = weight_grad(grad_hidden, normed, local)
     back, grad_gain, grad_bias = norm_backward(stream, stats, gain, dot_plain(grad_hidden, w_in))
     return (upstream + back, grad_in, grad_out, grad_gain, grad_bias)
 
@@ -236,20 +507,33 @@
     quarter = (tile_count - 7) // 4
     base = 4 * quarter
 
-    tiles = gather_tiles(master.astype(bf16), tile_slot)
-    source = swap_blocks(inputs[:, 0], "chan").reshape(rows, width).astype(f32)
-    upstream = swap_blocks(cotangent[:, 0], "chan").reshape(rows, width).astype(f32)
-    convs = jnp.moveaxis(gather_small(conv_params, "chan"), 0, 1).reshape(-1, width)
+    sizes = (quarter,) * 4 + (1,) * 7
+    local = is_slice(dp_count, chan_count, slots)
+    both = jnp.stack([inputs[:, 0], cotangent[:, 0]], axis=1)
+    mine = both
+    if local:
+        extra = [
+            lax.dynamic_index_in_dim(both, chan_index ^ mask, 0, keepdims=True)
+            for mask in range(1, chan_count)
+        ]
+        mats, moved, convs = gather_tiles_here(
+            master.astype(bf16), tile_slot, sizes, extra, conv_params
+        )
+        for mask in range(1, chan_count):
+            mine = lax.dynamic_update_slice_in_dim(mine, moved[mask - 1], chan_index ^ mask, 0)
+        near = jnp.array([0, 2, 1, 3], jnp.int32)
+        position = near[jnp.arange(chan_count, dtype=jnp.int32) ^ chan_index]
+    else:
+        mats = gather_tiles(master.astype(bf16), tile_slot, sizes)
+        mine = swap_blocks(both, "chan")
+        convs = gather_small(conv_params, "chan")
+        position = jnp.arange(chan_count, dtype=jnp.int32)
+    source = mine[:, 0].reshape(rows, width).astype(f32)
+    upstream = mine[:, 1].reshape(rows, width).astype(f32)
+    convs = jnp.moveaxis(convs, 0, 1).reshape(-1, width)
     valid = lax.dynamic_slice_in_dim(lengths[:, 0], chan_index, 1)
-
-    def stack_rows(first):
-        return tiles[first : first + quarter].reshape(quarter * width, width)
-
-    in_first, out_first = stack_rows(0), stack_rows(quarter)
-    in_second, out_second = stack_rows(2 * quarter), stack_rows(3 * quarter)
-    w_query, w_key, w_value, w_output, p_value, p_gate, p_output = [
-        tiles[base + i] for i in range(7)
-    ]
+    in_first, out_first, in_second, out_second = mats[:4]
+    w_query, w_key, w_value, w_output, p_value, p_gate, p_output = mats[4:]
     gains, biases = norm_params[:5], norm_params[5:]
     taps = convs.shape[0] - 2
     margin = (taps - 1) // 2
@@ -298,11 +582,11 @@
 
     grad_four, gain_four, bias_four = norm_backward(stream_four, stats_last, gains[4], upstream)
     grad_three, gin_second, gout_second, gain_three, bias_three = ffn_backward(
-        grad_four, stream_three, gains[3], kept_four, in_second, out_second
+        grad_four, stream_three, gains[3], kept_four, in_second, out_second, local
     )
 
     incoming = grad_three.astype(bf16)
-    grad_po = dot_cols(conv_act, incoming).astype(bf16)
+    grad_po = weight_grad(conv_act, incoming, local)
     conv_slope = conv_sig * (1.0 + normal * (1.0 - conv_sig))
     grad_normal = dot_rows(incoming, p_output) * conv_slope
     own_sums = jnp.stack([jnp.sum(grad_normal, axis=0), jnp.sum(grad_normal * center, axis=0)])
@@ -319,8 +603,8 @@
     grad_glu = grad_glu * frame_mask
     grad_linear = (grad_glu * gate_sig).astype(bf16)
     grad_gating = (grad_glu * linear * gate_sig * (1.0 - gate_sig)).astype(bf16)
-    grad_pv = dot_cols(grad_linear, conv_in).astype(bf16)
-    grad_pg = dot_cols(grad_gating, conv_in).astype(bf16)
+    grad_pv = weight_grad(grad_linear, conv_in, local)
+    grad_pg = weight_grad(grad_gating, conv_in, local)
     back, gain_two, bias_two = norm_backward(
         stream_two,
         stats_conv,
@@ -330,14 +614,14 @@
     grad_two = grad_three + back
 
     incoming = grad_two.astype(bf16)
-    grad_wo = dot_cols(merged, incoming).astype(bf16)
+    grad_wo = weight_grad(merged, incoming, local)
     grad_merged = dot_rows(incoming, w_output).astype(bf16)
     grad_q, grad_k, grad_v = head_call(
         attend_back_kernel, valid, (queries, keys, values, grad_merged), 3, 10
     )
-    grad_wq = dot_cols(grad_q, att_in).astype(bf16)
-    grad_wk = dot_cols(grad_k, att_in).astype(bf16)
-    grad_wv = dot_cols(grad_v, att_in).astype(bf16)
+    grad_wq = weight_grad(grad_q, att_in, local)
+    grad_wk = weight_grad(grad_k, att_in, local)
+    grad_wv = weight_grad(grad_v, att_in, local)
     back, gain_one, bias_one = norm_backward(
         stream_one,
         stats_att,
@@ -347,22 +631,32 @@
     grad_one = grad_two + back
 
     grad_zero, gin_first, gout_first, gain_zero, bias_zero = ffn_backward(
-        grad_one, source, gains[0], kept_one, in_first, out_first
-    )
-
-    grads = jnp.concatenate(
-        [gin_first, gout_first, gin_second, gout_second]
-        + [grad_wq, grad_wk, grad_wv, grad_wo, grad_pv, grad_pg, grad_po]
-    ).reshape(tile_count, width, width)
-    owned = reduce_tiles(grads, tile_slot, slots)
-
-    small = jnp.stack(
-        [gain_zero, gain_one, gain_two, gain_three, gain_four]
-        + [bias_zero, bias_one, bias_two, bias_three, bias_four]
-        + tap_grads
-        + [own_sums[1] * inv_std, own_sums[0]]
-    )
-    small = butterfly_sum(butterfly_sum(small, "dp"), "chan")
+        grad_one, source, gains[0], kept_one, in_first, out_first, local
+    )
+
+    grads = [gin_first, gout_first, gin_second, gout_second]
+    grads += [grad_wq, grad_wk, grad_wv, grad_wo, grad_pv, grad_pg, grad_po]
+    conv_small = jnp.stack(tap_grads + [own_sums[1] * inv_std, own_sums[0]])
+    conv_small = conv_small.reshape(-1, chan_count, rows_tile)[:, position].reshape(-1, width)
+    small = jnp.concatenate(
+        [
+            jnp.stack(
+                [gain_zero, gain_one, gain_two, gain_three, gain_four]
+                + [bias_zero, bias_one, bias_two, bias_three, bias_four]
+            ),
+            conv_small,
+        ]
+    )
+    if local:
+        halves = [g.reshape(n, 4, -1, width) for g, n in zip(grads, sizes)]
+        small = small + swap(small, "core")
+        owned, small = reduce_tiles_here(halves, tile_slot, slots, sizes, small)
+    else:
+        owned = reduce_tiles(
+            jnp.concatenate(grads).reshape(tile_count, width, width), tile_slot, slots
+        )
+        small = butterfly_sum(butterfly_sum(small, "dp"), "chan")
+    owned = jnp.where(owned_mask(tile_slot, slots), owned, 0.0)
     norm_total = small[: norm_params.shape[0]]
     conv_grad = lax.dynamic_slice_in_dim(
         small[norm_params.shape[0] :], chan_index * rows_tile, rows_tile, 1

time: 1090 us -> 837 us (0.77)
  waiting for transfers between devices: 686 us -> 408 us
  local copies, waits for them, and re-layouts: 131 us -> 53 us
  Pallas kernels: 23.9 us -> 61.8 us
  starting transfers between devices: 23.7 us -> 57.1 us
  other arithmetic: 42.5 us -> 62.7 us
  matrix products: 161 us -> 181 us
  between operations: 16.4 us -> 3.91 us
    reduce_scatter x1 -> x0, waiting for transfers between devices: 394 us -> none  [reduce_tiles(): lax.psum_scatter(placed, BOTH, scatter_dimension=0, tiled=True).astype(f32)]
    ppermute x0 -> x52, waiting for transfers between devices: none -> 346 us  [swap(): return lax.ppermute(value, BOTH, [(i, i ^ BITS[name]) for i in range(size)])]
    all_gather x1 -> x0, waiting for transfers between devices: 238 us -> none  [gather_tiles(): everything = lax.all_gather(own, BOTH, axis=0, tiled=True)]
    gather x2, local copies, waits for them, and re-layouts: 67.5 us -> 1.19 us  [the longest x1 0.64 us: shards(): position = near[jnp.arange(chan_count, dtype=jnp.int32) ^ chan_index]]
    ppermute x0 -> x52, starting transfers between devices: none -> 48.5 us  [swap(): return lax.ppermute(value, BOTH, [(i, i ^ BITS[name]) for i in range(size)])]
    pallas_call x0 -> x2, Pallas kernels: none -> 37.8 us  [the longest x1 27 us: gather_tiles_here(): pl.pallas_call(lambda *refs: assemble_kernel(sizes, *refs), in_specs=[sme...]
    slice x3 -> x32, local copies, waits for them, and re-layouts: 32.1 us -> 8.94 us  [the longest x21 3.46 us: reduce_tiles_here(): send[name] = jnp.concatenate([state[p][size:] for p in parts]).astype(bf16)]
    another operation x1 -> x19, other arithmetic: 0.63 us -> 16.7 us  [reduce_tiles(): jnp.argmax(hit, axis=1).astype(jnp.int32).reshape(dp_count, 1, slots)]
  transfers between devices with their start and end apart: 28 -> 69, of which waited for: 16 -> 29; matrix products, arithmetic and copies ran while one was open for 11% -> 16% of each run, Pallas kernels for 1% -> 2%
where the time goes in v2:
time: 837 us; the launch traced here: 827 us
  waiting for transfers between devices  408 us (49%)
  matrix products  181 us (22%)
  other arithmetic  62.7 us (7%)
  Pallas kernels  61.8 us (7%)
  starting transfers between devices  57.1 us (7%)
  local copies, waits for them, and re-layouts  53 us (6%)
    ppermute x52, waiting for transfers between devices, swap(): return lax.ppermute(value, BOTH, [(i, i ^ BITS[name]) for i in range(size)])  346 us
    dot_general x22, matrix products, dot_cols(): lax.dot_general(left, right, (((0,), (0,)), ((), ())), preferred_element_...  64.7 us
    dot_general x11, matrix products, dot_rows(): lax.dot_general(left, right, (((1,), (1,)), ((), ())), preferred_element_...  64.6 us
    ppermute x17, waiting for transfers between devices, exchange(): return lax.ppermute(value, axis, [(i, i ^ mask) for i in range(size)])  61.5 us
    dot_general x11, matrix products, dot_plain(): return jnp.dot(left, right, preferred_element_type=f32)  51.5 us
    ppermute x52, starting transfers between devices, swap(): return lax.ppermute(value, BOTH, [(i, i ^ BITS[name]) for i in range(size)])  48.5 us
    unnamed x253, local copies, waits for them, and re-layouts  30.6 us
    pallas_call x1, Pallas kernels, gather_tiles_here(): pl.pallas_call(lambda *refs: assemble_kernel(sizes, *refs), in_specs=[sme...  27 us
  transfers between devices with their start and end apart: 69, of which 29 were waited for; matrix products, arithmetic and copies ran while one was open for 16% of the time, Pallas kernels for 2%

profile of v2, /device:TPU:0, one launch (start us, length us, event | category | flops | bytes accessed | tf_op | source)
XLA Modules:
  0.0 826.9 jit_solution(3335233240957963404)
XLA Ops:
  16.2 12.7 %collective-permute-done.3 = bf16[1,2,128,1024]{3,2,1,0:T(8,128)(2,1)S(1)} collective-permute-done((bf16[1,2,128,1024]{3,2,1,0:T(8,128)(2,1)S(1)}, bf16[1,2,128,1024]{3,2,1,0:T(8,128)(2,1)S(1)}, u32[]{:S(2)}, u32[]{:S(2)}) %collective-permute-start.3) | collective-permute-done | bytes 524320 | tf_op jit(solution)/shard_map/ppermute | solution.py:48
  28.9 10.5 %collective-permute-done.4 = bf16[1,2,128,1024]{3,2,1,0:T(8,128)(2,1)S(1)} collective-permute-done((bf16[1,2,128,1024]{3,2,1,0:T(8,128)(2,1)S(1)}, bf16[1,2,128,1024]{3,2,1,0:T(8,128)(2,1)S(1)}, u32[]{:S(2)}, u32[]{:S(2)}) %collective-permute-start.4) | collective-permute-done | bytes 524320 | tf_op jit(solution)/shard_map/ppermute | solution.py:48
  55.6 16.5 %collective-permute-done.9 = f32[7,256]{1,0:T(8,128)S(1)} collective-permute-done((f32[7,256]{1,0:T(8,128)S(1)}, f32[7,256]{1,0:T(8,128)S(1)}, u32[]{:S(2)}, u32[]{:S(2)}) %collective-permute-start.9) | collective-permute-done | bytes 7200 | tf_op jit(solution)/shard_map/ppermute | solution.py:48
  84.0 38.7 %collective-permute-done.12 = bf16[4,128,1024]{2,1,0:T(8,128)(2,1)S(1)} collective-permute-done((bf16[4,128,1024]{2,1,0:T(8,128)(2,1)S(1)}, bf16[4,128,1024]{2,1,0:T(8,128)(2,1)S(1)}, u32[]{:S(2)}, u32[]{:S(2)}) %collective-permute-start.12) | collective-permute-done | bytes 1048608 | tf_op jit(solution)/shard_map/ppermute | solution.py:101
  141.0 77.8 %collective-permute-done.16.refs_7_ = bf16[8,128,1024]{2,1,0:T(8,128)(2,1)S(1)} collective-permute-done((bf16[8,128,1024]{2,1,0:T(8,128)(2,1)S(1)}, bf16[8,128,1024]{2,1,0:T(8,128)(2,1)S(1)}, u32[]{:S(2)}, u32[]{:S(2)}) %collective-permute-start.16) | collective-permute-done | bytes 2097184 | tf_op jit(solution)/shard_map/ppermute | solution.py:101
  218.8 8.2 collective-permute-done.17.refs_8_
  241.5 11.0 %collective-permute-done.24.refs_15_ = bf16[8,128,1024]{2,1,0:T(8,128)(2,1)} collective-permute-done((bf16[8,128,1024]{2,1,0:T(8,128)(2,1)}, bf16[8,128,1024]{2,1,0:T(8,128)(2,1)}, u32[]{:S(2)}, u32[]{:S(2)}) %collective-permute-start.24) | collective-permute-done | bytes 2097184 | tf_op jit(solution)/shard_map/ppermute | solution.py:101
  255.5 27.0 %shard_map.229 = (bf16[2,4,4,128,1024]{4,3,2,1,0:T(8,128)(2,1)}, bf16[2,4,4,128,1024]{4,3,2,1,0:T(8,128)(2,1)}, bf16[2,4,4,128,1024]{4,3,2,1,0:T(8,128)(2,1)}, b...) custom-call(s32[23]{0:T(128)S(1)} %get-tuple-element.265.refs_0_, ...), custom_call_target="tpu_custom_call" | custom-call | tf_op jit(solution)/shard_map/pallas_call | solution.py:251
  285.1 13.3 %multiply_convert_fusion.5 = (bf16[512,4096]{1,0:T(8,128)(2,1)}, f32[512,4096]{1,0:T(8,128)}) fusion(bf16[512,1024]{1,0:T(8,128)(2,1)S(1)} %bitcast.256, bf16[4096,1024]{1,0:T(8,128)(2,1)} %bitcast.339), kind=kOutput, calls=%fused_computation.12 | convolution fusion | flops 4305453056 | bytes 22020096 | tf_op jit(solution)/shard_map/dot_general | solution.py:26
  298.4 8.3 %fusion.123 = (f32[512]{0:T(512)S(1)}, f32[512,1024]{1,0:T(8,128)S(1)}) fusion(bf16[512,4096]{1,0:T(8,128)(2,1)} %get-tuple-element.368, bf16[4096,1024]{1,0:T(8,128)(2,1)} %bitcast.341, bf16[4,1,128,1024]{3,2,1,0:T(8,128)(2,1)S(1)} %slice.655), kind=kOutput, calls=%fused_computation.356 | convolution fusion | flops 4297063936 | bytes 15730688 | tf_op jit(solution)/shard_map/dot_general | solution.py:30
  311.6 9.7 %shard_map.230 = bf16[512,1024]{1,0:T(8,128)(2,1)S(1)} custom-call(s32[1]{0:T(128)} %bitcast.15.valid_ref, bf16[512,1024]{1,0:T(8,128)(2,1)S(1)} %convolution_convert_fusion.7.q_ref, bf16[512,1024]{1,0:T(8,128)(2,1)S(1)} %convolution_convert_fusion.6.k_ref, bf16[512,1024]{1,0:T(8,128)(2,1)S(1)} %convolution_convert_fusion.5.v_ref), custom_call_target="tpu_custom_call" | custom-call | flops 1073741824 | bytes 4194304 | tf_op jit(solution)/shard_map/pallas_call | solution.py:424
  352.1 14.4 %multiply_convert_fusion.4 = (bf16[512,4096]{1,0:T(8,128)(2,1)}, f32[512,4096]{1,0:T(8,128)}) fusion(bf16[4096,1024]{1,0:T(8,128)(2,1)} %bitcast.343, f32[512,1024]{1,0:T(8,128)} %get-tuple-element.377, f32[1024]{0:T(1024)S(1)} %bitcast.330, f32[1024]{0:T(1024)S(1)} %bitcast.305, f32[512]{0:T(512)S(1)} %add_rsqrt_fusion.2, f32[512]{0:T(512)S(1)} %broadcast_multiply_fusion.10), kind=kOutput, calls=%fused_computation.10 | convolution fusion | flops 4308074496 | bytes 23080960 | tf_op jit(solution)/shard_map/dot_general | solution.py:26
  366.5 9.7 %fusion.126 = (f32[512]{0:T(512)S(1)}, f32[512,1024]{1,0:T(8,128)S(1)}) fusion(f32[512,1024]{1,0:T(8,128)} %get-tuple-element.377, bf16[512,4096]{1,0:T(8,128)(2,1)} %get-tuple-element.378, bf16[4096,1024]{1,0:T(8,128)(2,1)} %bitcast.345), kind=kOutput, calls=%fused_computation.359 | convolution fusion | flops 4296539648 | bytes 16779264 | tf_op jit(solution)/shard_map/dot_general | solution.py:30
  380.5 12.3 %multiply_convert_fusion.2 = bf16[512,4096]{1,0:T(8,128)(2,1)} fusion(bf16[4096,1024]{1,0:T(8,128)(2,1)} %bitcast.346, f32[512,4096]{1,0:T(8,128)} %get-tuple-element.379, f32[512,1024]{1,0:T(8,128)S(1)} %get-tuple-element.271), kind=kOutput, calls=%fused_computation.8 | convolution fusion | flops 4319084544 | bytes 23068672 | tf_op jit(solution)/shard_map/dot_general | solution.py:26
  392.8 10.1 %multiply_reduce_fusion.5 = (f32[1024]{0:T(1024)S(1)}, f32[512]{0:T(512)S(1)}, f32[512]{0:T(512)S(1)}, f32[1024]{0:T(1024)S(1)}, f32[512,1024]{1,0:T(8,128)S(1)}) fusion(f32[512,1024]{1,0:T(8,128)} %get-tuple-element.377, f32[512]{0:T(512)S(1)} %add_rsqrt_fusion.2, f32[512]{0:T(512)S(1)} %broadcast_multiply_fusion.10, f32[1024]{0:T(1024)S(1)} %bitcast.306, ...), kind=kOutput, calls=%fused_computation.90 | convolution fusion | flops 4299682816 | bytes 16797696 | tf_op jit(solution)/shard_map/dot_general | solution.py:30
  447.5 14.3 %shard_map.231 = (bf16[512,1024]{1,0:T(8,128)(2,1)S(1)}, bf16[512,1024]{1,0:T(8,128)(2,1)S(1)}, bf16[512,1024]{1,0:T(8,128)(2,1)S(1)}) custom-call(s32[1]{0:T(128)} %bitcast.15.valid_ref, bf16[512,1024]{1,0:T(8,128)(2,1)S(1)} %convolution_convert_fusion.7.q_ref, bf16[512,1024]{1,0:T(8,128)(2,1)S(1)} %convolution_convert_fusion.6.k_ref, ...), custom_call_target="tpu_custom_call" | custom-call | flops 2684354560 | bytes 7340032 | tf_op jit(solution)/shard_map/pallas_call | solution.py:424
  469.4 12.1 %multiply_convert_fusion = bf16[512,4096]{1,0:T(8,128)(2,1)} fusion(bf16[4096,1024]{1,0:T(8,128)(2,1)} %bitcast.342, f32[512,4096]{1,0:T(8,128)} %get-tuple-element.369, f32[512,1024]{1,0:T(8,128)S(1)} %multiply_add_fusion.1), kind=kOutput, calls=%fused_computation.6 | convolution fusion | flops 4319084544 | bytes 23068672 | tf_op jit(solution)/shard_map/dot_general | solution.py:26
  482.3 11.5 %fusion.46 = (f32[1024]{0:T(1024)S(1)}, f32[512]{0:T(512)S(1)}, f32[512]{0:T(512)S(1)}, f32[1024]{0:T(1024)S(1)}, bf16[512,1024]{1,0:T(8,128)(2,1)}, /*index=5*/f32[512,1024]{1,0:T(8,128)}) fusion(f32[512]{0:T(512)S(1)} %copy-done.107, f32[512]{0:T(512)S(1)} %copy-done.106, bf16[4,2,128,1024]{3,2,1,0:T(8,128)(2,1)} %constant_dynamic-update-slice_fusion.28, ...), kind=kOutput, calls=%fused_computation.78 | convolution fusion | flops 4301779968 | bytes 16801792 | tf_op jit(solution)/shard_map/dot_general | solution.py:30
  532.7 8.2 add_convert_fusion.1
  554.3 10.8 %shard_map.232 = (bf16[16,128,1024]{2,1,0:T(8,128)(2,1)S(1)}, bf16[8,128,1024]{2,1,0:T(8,128)(2,1)S(1)}, bf16[8,128,1024]{2,1,0:T(8,128)(2,1)S(1)}, bf16[16,128,...) custom-call(s32[23]{0:T(128)S(1)} %get-tuple-element.265.refs_0_, ...), custom_call_target="tpu_custom_call" | custom-call | tf_op jit(solution)/shard_map/pallas_call | solution.py:311
  572.2 89.5 %collective-permute-done.55 = f32[17,1024]{1,0:T(8,128)S(1)} collective-permute-done((f32[17,1024]{1,0:T(8,128)S(1)}, f32[17,1024]{1,0:T(8,128)S(1)}, u32[]{:S(2)}, u32[]{:S(2)}) %collective-permute-start.55) | collective-permute-done | bytes 69664 | tf_op jit(solution)/shard_map/ppermute | solution.py:101
  684.8 41.7 %collective-permute-done.60 = f32[17,1024]{1,0:T(8,128)S(1)} collective-permute-done((f32[17,1024]{1,0:T(8,128)S(1)}, f32[17,1024]{1,0:T(8,128)S(1)}, u32[]{:S(2)}, u32[]{:S(2)}) %collective-permute-start.60) | collective-permute-done | bytes 69664 | tf_op jit(solution)/shard_map/ppermute | solution.py:101
  745.4 24.1 %collective-permute-done.65 = f32[17,1024]{1,0:T(8,128)S(1)} collective-permute-done((f32[17,1024]{1,0:T(8,128)S(1)}, f32[17,1024]{1,0:T(8,128)S(1)}, u32[]{:S(2)}, u32[]{:S(2)}) %collective-permute-start.65) | collective-permute-done | bytes 69664 | tf_op jit(solution)/shard_map/ppermute | solution.py:101
  789.6 27.8 %collective-permute-done.68 = f32[17,1024]{1,0:T(8,128)S(1)} collective-permute-done((f32[17,1024]{1,0:T(8,128)S(1)}, f32[17,1024]{1,0:T(8,128)S(1)}, u32[]{:S(2)}, u32[]{:S(2)}) %collective-permute-start.68) | collective-permute-done | bytes 69664 | tf_op jit(solution)/shard_map/ppermute | solution.py:101
  (585 shorter events, 302.8 us)
Async XLA Ops:
  8.6 37.3 %collective-permute-start = (bf16[3,128,1024]{2,1,0:T(8,128)(2,1)S(1)}, bf16[3,128,1024]{2,1,0:T(8,128)(2,1)S(1)}, u32[]{:S(2)}, u32[]{:S(2)}) collective-permute-start(bf16[3,128,1024]{2,1,0:T(8,128)(2,1)S(1)} %copy-done.90), channel_id=1, source_target_pairs={{0,8},{1,9},{2,10},{3,11},{4,12},{5,13},{6,14},{7,15},{8,0},{9,1},... | collective-permute-start | bytes 2359304 | tf_op jit(solution)/shard_map/ppermute | solution.py:101
  79.9 45.7 %collective-permute-start.10 = (bf16[8,128,1024]{2,1,0:T(8,128)(2,1)S(1)}, bf16[8,128,1024]{2,1,0:T(8,128)(2,1)S(1)}, u32[]{:S(2)}, u32[]{:S(2)}) collective-permute-start(bf16[8,128,1024]{2,1,0:T(8,128)(2,1)S(1)} %get-tuple-element.133), channel_id=1, source_target_pairs={{0,4},{1,5},{2,6},{3,7},{4,0},{5,1},{6,2},{7,3},{8,12},{9,13},{10,... | collective-permute-start | bytes 6291464 | tf_op jit(solution)/shard_map/ppermute | solution.py:101
  80.4 45.2 %collective-permute-start.11 = (bf16[8,128,1024]{2,1,0:T(8,128)(2,1)S(1)}, bf16[8,128,1024]{2,1,0:T(8,128)(2,1)S(1)}, u32[]{:S(2)}, u32[]{:S(2)}) collective-permute-start(bf16[8,128,1024]{2,1,0:T(8,128)(2,1)S(1)} %get-tuple-element.134), channel_id=1, source_target_pairs={{0,2},{1,3},{2,0},{3,1},{4,6},{5,7},{6,4},{7,5},{8,10},{9,11},{10,... | collective-permute-start | bytes 6291464 | tf_op jit(solution)/shard_map/ppermute | solution.py:101
  80.9 41.8 %collective-permute-start.12 = (bf16[4,128,1024]{2,1,0:T(8,128)(2,1)S(1)}, bf16[4,128,1024]{2,1,0:T(8,128)(2,1)S(1)}, u32[]{:S(2)}, u32[]{:S(2)}) collective-permute-start(bf16[4,128,1024]{2,1,0:T(8,128)(2,1)S(1)} %pad_maximum_fusion.7), channel_id=1, source_target_pairs={{0,8},{1,9},{2,10},{3,11},{4,12},{5,13},{6,14},{7,15},{8,0},{9,1},... | collective-permute-start | bytes 3145736 | tf_op jit(solution)/shard_map/ppermute | solution.py:101
  80.9 44.7 %collective-permute-start.13 = (bf16[4,128,1024]{2,1,0:T(8,128)(2,1)S(1)}, bf16[4,128,1024]{2,1,0:T(8,128)(2,1)S(1)}, u32[]{:S(2)}, u32[]{:S(2)}) collective-permute-start(bf16[4,128,1024]{2,1,0:T(8,128)(2,1)S(1)} %pad_maximum_fusion.8), channel_id=1, source_target_pairs={{0,16},{1,17},{2,18},{3,19},{4,20},{5,21},{6,22},{7,23},{8,24},{9,... | collective-permute-start | bytes 3145736 | tf_op jit(solution)/shard_map/ppermute | solution.py:101
  135.3 83.5 %collective-permute-start.16 = (bf16[8,128,1024]{2,1,0:T(8,128)(2,1)S(1)}, bf16[8,128,1024]{2,1,0:T(8,128)(2,1)S(1)}, u32[]{:S(2)}, u32[]{:S(2)}) collective-permute-start(bf16[8,128,1024]{2,1,0:T(8,128)(2,1)S(1)} %pad_maximum_fusion.refs_3_), channel_id=1, source_target_pairs={{0,8},{1,9},{2,10},{3,11},{4,12},{5,13},{6,14},{7,15},{8,0},{9,1},... | collective-permute-start | bytes 6291464 | tf_op jit(solution)/shard_map/ppermute | solution.py:101
  135.4 92.9 %collective-permute-start.15 = (bf16[16,128,1024]{2,1,0:T(8,128)(2,1)}, bf16[16,128,1024]{2,1,0:T(8,128)(2,1)}, u32[]{:S(2)}, u32[]{:S(2)}) collective-permute-start(bf16[16,128,1024]{2,1,0:T(8,128)(2,1)} %get-tuple-element.149.refs_2_), channel_id=1, source_target_pairs={{0,4},{1,5},{2,6},{3,7},{4,0},{5,1},{6,2},{7,3},{8,12},{9,13},{10,... | collective-permute-start | bytes 12582920 | tf_op jit(solution)/shard_map/ppermute | solution.py:101
  136.9 92.1 %collective-permute-start.18 = (bf16[16,128,1024]{2,1,0:T(8,128)(2,1)}, bf16[16,128,1024]{2,1,0:T(8,128)(2,1)}, u32[]{:S(2)}, u32[]{:S(2)}) collective-permute-start(bf16[16,128,1024]{2,1,0:T(8,128)(2,1)} %constant_dynamic-update-slice_fusion.21.refs_5_), channel_id=1, source_target_pairs={{0,2},{1,3},{2,0},{3,1},{4,6},{5,7},{6,4},{7,5},{8,10},{9,11},{10,... | collective-permute-start | bytes 12582920 | tf_op jit(solution)/shard_map/ppermute | solution.py:101
  138.3 88.7 %collective-permute-start.17 = (bf16[8,128,1024]{2,1,0:T(8,128)(2,1)}, bf16[8,128,1024]{2,1,0:T(8,128)(2,1)S(1)}, u32[]{:S(2)}, u32[]{:S(2)}) collective-permute-start(bf16[8,128,1024]{2,1,0:T(8,128)(2,1)} %pad_maximum_fusion.1.refs_4_), channel_id=1, source_target_pairs={{0,16},{1,17},{2,18},{3,19},{4,20},{5,21},{6,22},{7,23},{8,24},{9,... | collective-permute-start | bytes 6291464 | tf_op jit(solution)/shard_map/ppermute | solution.py:101
  141.0 90.6 %collective-permute-start.19 = (bf16[16,128,1024]{2,1,0:T(8,128)(2,1)}, bf16[16,128,1024]{2,1,0:T(8,128)(2,1)}, u32[]{:S(2)}, u32[]{:S(2)}) collective-permute-start(bf16[16,128,1024]{2,1,0:T(8,128)(2,1)} %get-tuple-element.149.refs_2_), channel_id=1, source_target_pairs={{0,1},{1,0},{2,3},{3,2},{4,5},{5,4},{6,7},{7,6},{8,9},{9,8},{10,11... | collective-permute-start | bytes 12582920 | tf_op jit(solution)/shard_map/ppermute | solution.py:101
  423.1 102.4 %collective-permute-start.42 = (bf16[2048,1024]{1,0:T(8,128)(2,1)}, bf16[2048,1024]{1,0:T(8,128)(2,1)}, u32[]{:S(2)}, u32[]{:S(2)}) collective-permute-start(bf16[2048,1024]{1,0:T(8,128)(2,1)} %convolution_convert_fusion), channel_id=1, source_target_pairs={{0,1},{1,0},{2,3},{3,2},{4,5},{5,4},{6,7},{7,6},{8,9},{9,8},{10,11... | collective-permute-start | bytes 12582920 | tf_op jit(solution)/shard_map/ppermute | solution.py:101
  423.1 79.2 %collective-permute-start.49 = (bf16[512,1024]{1,0:T(8,128)(2,1)}, bf16[512,1024]{1,0:T(8,128)(2,1)}, u32[]{:S(2)}, u32[]{:S(2)}) collective-permute-start(bf16[512,1024]{1,0:T(8,128)(2,1)} %convolution_convert_fusion.8), channel_id=1, source_target_pairs={{0,1},{1,0},{2,3},{3,2},{4,5},{5,4},{6,7},{7,6},{8,9},{9,8},{10,11... | collective-permute-start | bytes 3145736 | tf_op jit(solution)/shard_map/ppermute | solution.py:101
  565.2 97.2 %collective-permute-start.51 = (bf16[16,128,1024]{2,1,0:T(8,128)(2,1)}, bf16[16,128,1024]{2,1,0:T(8,128)(2,1)S(1)}, u32[]{:S(2)}, u32[]{:S(2)}) collective-permute-start(bf16[16,128,1024]{2,1,0:T(8,128)(2,1)} %get-tuple-element.173), channel_id=1, source_target_pairs={{0,4},{1,5},{2,6},{3,7},{4,0},{5,1},{6,2},{7,3},{8,12},{9,13},{10,... | collective-permute-start | bytes 12582920 | tf_op jit(solution)/shard_map/ppermute | solution.py:101
  567.1 95.3 %collective-permute-start.52 = (bf16[16,128,1024]{2,1,0:T(8,128)(2,1)}, bf16[16,128,1024]{2,1,0:T(8,128)(2,1)S(1)}, u32[]{:S(2)}, u32[]{:S(2)}) collective-permute-start(bf16[16,128,1024]{2,1,0:T(8,128)(2,1)} %get-tuple-element.174), channel_id=1, source_target_pairs={{0,2},{1,3},{2,0},{3,1},{4,6},{5,7},{6,4},{7,5},{8,10},{9,11},{10,... | collective-permute-start | bytes 12582920 | tf_op jit(solution)/shard_map/ppermute | solution.py:101
  567.8 93.9 %collective-permute-start.53 = (bf16[8,128,1024]{2,1,0:T(8,128)(2,1)S(1)}, bf16[8,128,1024]{2,1,0:T(8,128)(2,1)S(1)}, u32[]{:S(2)}, u32[]{:S(2)}) collective-permute-start(bf16[8,128,1024]{2,1,0:T(8,128)(2,1)S(1)} %get-tuple-element.175), channel_id=1, source_target_pairs={{0,8},{1,9},{2,10},{3,11},{4,12},{5,13},{6,14},{7,15},{8,0},{9,1},... | collective-permute-start | bytes 6291464 | tf_op jit(solution)/shard_map/ppermute | solution.py:101
  569.7 92.7 %collective-permute-start.54 = (bf16[8,128,1024]{2,1,0:T(8,128)(2,1)S(1)}, bf16[8,128,1024]{2,1,0:T(8,128)(2,1)S(1)}, u32[]{:S(2)}, u32[]{:S(2)}) collective-permute-start(bf16[8,128,1024]{2,1,0:T(8,128)(2,1)S(1)} %get-tuple-element.176), channel_id=1, source_target_pairs={{0,16},{1,17},{2,18},{3,19},{4,20},{5,21},{6,22},{7,23},{8,24},{9,... | collective-permute-start | bytes 6291464 | tf_op jit(solution)/shard_map/ppermute | solution.py:101
  570.7 91.0 %collective-permute-start.55 = (f32[17,1024]{1,0:T(8,128)S(1)}, f32[17,1024]{1,0:T(8,128)S(1)}, u32[]{:S(2)}, u32[]{:S(2)}) collective-permute-start(f32[17,1024]{1,0:T(8,128)S(1)} %add.796), channel_id=1, source_target_pairs={{0,2},{1,3},{2,0},{3,1},{4,6},{5,7},{6,4},{7,5},{8,10},{9,11},{10,... | collective-permute-start | bytes 208904 | tf_op jit(solution)/shard_map/ppermute | solution.py:101
  678.3 49.9 %collective-permute-start.56 = (bf16[8,128,1024]{2,1,0:T(8,128)(2,1)}, bf16[8,128,1024]{2,1,0:T(8,128)(2,1)}, u32[]{:S(2)}, u32[]{:S(2)}) collective-permute-start(bf16[8,128,1024]{2,1,0:T(8,128)(2,1)} %pad_maximum_fusion.2), channel_id=1, source_target_pairs={{0,4},{1,5},{2,6},{3,7},{4,0},{5,1},{6,2},{7,3},{8,12},{9,13},{10,... | collective-permute-start | bytes 6291464 | tf_op jit(solution)/shard_map/ppermute | solution.py:101
  678.6 49.5 %collective-permute-start.57 = (bf16[8,128,1024]{2,1,0:T(8,128)(2,1)}, bf16[8,128,1024]{2,1,0:T(8,128)(2,1)}, u32[]{:S(2)}, u32[]{:S(2)}) collective-permute-start(bf16[8,128,1024]{2,1,0:T(8,128)(2,1)} %pad_maximum_fusion.3), channel_id=1, source_target_pairs={{0,2},{1,3},{2,0},{3,1},{4,6},{5,7},{6,4},{7,5},{8,10},{9,11},{10,... | collective-permute-start | bytes 6291464 | tf_op jit(solution)/shard_map/ppermute | solution.py:101
  680.1 46.4 %collective-permute-start.58 = (bf16[4,128,1024]{2,1,0:T(8,128)(2,1)}, bf16[4,128,1024]{2,1,0:T(8,128)(2,1)S(1)}, u32[]{:S(2)}, u32[]{:S(2)}) collective-permute-start(bf16[4,128,1024]{2,1,0:T(8,128)(2,1)} %slice.702), channel_id=1, source_target_pairs={{0,8},{1,9},{2,10},{3,11},{4,12},{5,13},{6,14},{7,15},{8,0},{9,1},... | collective-permute-start | bytes 3145736 | tf_op jit(solution)/shard_map/ppermute | solution.py:101
  680.6 47.5 %collective-permute-start.59 = (bf16[4,128,1024]{2,1,0:T(8,128)(2,1)}, bf16[4,128,1024]{2,1,0:T(8,128)(2,1)}, u32[]{:S(2)}, u32[]{:S(2)}) collective-permute-start(bf16[4,128,1024]{2,1,0:T(8,128)(2,1)} %slice.703), channel_id=1, source_target_pairs={{0,16},{1,17},{2,18},{3,19},{4,20},{5,21},{6,22},{7,23},{8,24},{9,... | collective-permute-start | bytes 3145736 | tf_op jit(solution)/shard_map/ppermute | solution.py:101
  683.0 43.5 %collective-permute-start.60 = (f32[17,1024]{1,0:T(8,128)S(1)}, f32[17,1024]{1,0:T(8,128)S(1)}, u32[]{:S(2)}, u32[]{:S(2)}) collective-permute-start(f32[17,1024]{1,0:T(8,128)S(1)} %add.797), channel_id=1, source_target_pairs={{0,4},{1,5},{2,6},{3,7},{4,0},{5,1},{6,2},{7,3},{8,12},{9,13},{10,... | collective-permute-start | bytes 208904 | tf_op jit(solution)/shard_map/ppermute | solution.py:101
  773.2 44.1 %collective-permute-start.66 = (bf16[3,128,1024]{2,1,0:T(8,128)(2,1)S(1)}, bf16[3,128,1024]{2,1,0:T(8,128)(2,1)S(1)}, u32[]{:S(2)}, u32[]{:S(2)}) collective-permute-start(bf16[3,128,1024]{2,1,0:T(8,128)(2,1)S(1)} %pad_maximum_fusion.11), channel_id=1, source_target_pairs={{0,8},{1,9},{2,10},{3,11},{4,12},{5,13},{6,14},{7,15},{8,0},{9,1},... | collective-permute-start | bytes 2359304 | tf_op jit(solution)/shard_map/ppermute | solution.py:101
  778.1 39.3 %collective-permute-start.67 = (bf16[3,128,1024]{2,1,0:T(8,128)(2,1)S(1)}, bf16[3,128,1024]{2,1,0:T(8,128)(2,1)S(1)}, u32[]{:S(2)}, u32[]{:S(2)}) collective-permute-start(bf16[3,128,1024]{2,1,0:T(8,128)(2,1)S(1)} %pad_maximum_fusion.12), channel_id=1, source_target_pairs={{0,16},{1,17},{2,18},{3,19},{4,20},{5,21},{6,22},{7,23},{8,24},{9,... | collective-permute-start | bytes 2359304 | tf_op jit(solution)/shard_map/ppermute | solution.py:101
  (168 other events, 2344.4 us)

commit v3 on v2

--- a/solution.py
+++ b/solution.py
@@ -56,6 +56,28 @@
         sent = lax.dynamic_index_in_dim(value, me ^ mask, 0, keepdims=True)
         result = lax.dynamic_update_slice_in_dim(result, exchange(sent, axis, mask), me ^ mask, 0)
     return result
+
+
+def swap_in_hops(value):
+    me = lax.axis_index("chan")
+    pairs = value.reshape((2, 2) + value.shape[1:])
+    core, y = lax.rem(me, 2), lax.div(me, 2)
+    keep = lax.dynamic_index_in_dim(pairs, core, 1, keepdims=False)
+    sent = lax.dynamic_index_in_dim(pairs, 1 - core, 1, keepdims=False)
+    got = exchange(sent, "chan", 1)
+    low = jnp.where(core == 0, keep, got)
+    high = jnp.where(core == 0, got, keep)
+    mixed = jnp.stack([low, high], axis=1)
+    there = lax.dynamic_index_in_dim(mixed, 1 - y, 0, keepdims=False)
+    here = lax.dynamic_index_in_dim(mixed, y, 0, keepdims=False)
+    return here, there
+
+
+def finish_hops(here, arrived_there):
+    y = lax.div(lax.axis_index("chan"), 2)
+    low = jnp.where(y == 0, here, arrived_there)
+    high = jnp.where(y == 0, arrived_there, here)
+    return jnp.concatenate([low, high])
 
 
 def gather_small(value, axis):
@@ -108,14 +130,11 @@
     return groups
 
 
-def block_rows(own):
-    half = own.shape[1] // HALVES
-    return [own[p // HALVES, (p % HALVES) * half : (p % HALVES + 1) * half][None] for p in range(6)]
-
-
-def gather_parts(own, extra, small):
+def gather_parts(master, extra, small):
+    half = master.shape[1] // HALVES
+    own = [master[:, h * half : (h + 1) * half].astype(bf16) for h in range(HALVES)]
     own = lax.optimization_barrier(own)
-    state = block_rows(own)
+    state = [own[p % HALVES][p // HALVES][None] for p in range(6)]
     moved = []
     for step in range(4):
         groups = step_groups(step, ORDERS)
@@ -124,8 +143,7 @@
             for name, parts in groups.items()
         }
         if step == 0:
-            half = own.shape[1] // HALVES
-            sent = {ORDERS[h][0]: own[:, h * half : (h + 1) * half] for h in range(HALVES)}
+            sent = {ORDERS[h][0]: own[h] for h in range(HALVES)}
             sent, extra = lax.optimization_barrier((sent, extra))
             moved = [exchange(value, "chan", mask + 1) for mask, value in enumerate(extra)]
         elif step == 1:
@@ -154,24 +172,33 @@
             return (bits[order[3]], index + 8 * parts.index(part))
 
 
+def array_of(position, h):
+    part = position * HALVES + h
+    return [i for i, (_, parts) in enumerate(LAST) if part in parts][0]
+
+
 def slot_places(slot, slots):
-    owner = slot // slots
+    owner, position = slot // slots, slot % slots
     gap = owner ^ lax.axis_index("dp")
     bits = {"x": gap & 1, "z1": (gap >> 1) & 1, "z2": (gap >> 2) & 1}
     rows = []
     for dy in range(2):
         for h in range(HALVES):
-            at = [place_of(s * HALVES + h, dict(bits, y=jnp.full_like(gap, dy))) for s in range(slots)]
-            position = slot % slots
-            far = jnp.select([position == s for s in range(slots)], [a[0] for a in at])
-            index = jnp.select([position == s for s in range(slots)], [a[1] for a in at])
-            rows.append((far * 16 + index).astype(jnp.int32))
-    return (slot % slots).astype(jnp.int32), jnp.stack(rows)
-
-
-def array_of(position, h):
-    part = position * HALVES + h
-    return [i for i, (_, parts) in enumerate(LAST) if part in parts][0]
+            codes = []
+            for s in range(slots):
+                far, index = place_of(s * HALVES + h, dict(bits, y=jnp.full_like(gap, dy)))
+                codes.append((far * 4 + array_of(s, h)) * 16 + index)
+            rows.append(jnp.select([position == s for s in range(slots)], codes))
+    return jnp.stack(rows).astype(jnp.int32)
+
+
+def at_place(place, arrays, act):
+    which, index = lax.div(place, 16), lax.rem(place, 16)
+    for i, array in enumerate(arrays):
+
+        @pl.when(which == i)
+        def _():
+            act(array, index)
 
 
 def staged(count, depth, load, drain_in, store, drain_out):
@@ -191,37 +218,30 @@
 DEPTH = 8
 
 
-def when_placed(position_ref, place_ref, tile, b, act):
-    place = place_ref[b, tile]
-    index = lax.rem(place, 16)
-    for s in range(3):
-        for far in range(2):
-
-            @pl.when((position_ref[tile] == s) & (place // 16 == far))
-            def _():
-                act(array_of(s, b % HALVES), far, index)
-
-
-def assemble_kernel(sizes, position_ref, place_ref, *refs):
-    sources, outs = refs[:16], refs[16 : 16 + len(sizes)]
-    buffer, in_sem, out_sem = refs[16 + len(sizes) :]
-    items, first = [], 0
-    for g, count in enumerate(sizes):
-        items += [(core, g, j, first + j) for core in range(2) for j in range(count)]
-        first += count
+SOURCES = 13
+
+
+def sixteen(refs):
+    near, at = [], 0
+    for _, parts in LAST:
+        near.append(refs[8].at[pl.ds(at, 8 * len(parts))])
+        at += 8 * len(parts)
+    return list(refs[:8]) + near + list(refs[9:SOURCES])
+
+
+def assemble_kernel(first, place_ref, *refs):
+    sources, outs = sixteen(refs), refs[SOURCES:-3]
+    buffer, in_sem, out_sem = refs[-3:]
+    items = [(core, g) for core in range(2) for g in range(len(outs))]
 
     def load(i):
-        core, _, _, tile = items[i]
+        core, g = items[i]
         for b in range(4):
-            when_placed(
-                position_ref,
-                place_ref,
-                tile,
-                b,
-                lambda array, far, index: pltpu.make_async_copy(
-                    sources[core * 8 + far * 4 + array].at[index],
-                    buffer.at[i % DEPTH, b],
-                    in_sem.at[i % DEPTH],
+            at_place(
+                place_ref[b, first + g],
+                sources[core * 8 : core * 8 + 8],
+                lambda array, index: pltpu.make_async_copy(
+                    array.at[index], buffer.at[i % DEPTH, b], in_sem.at[i % DEPTH]
                 ).start(),
             )
 
@@ -230,96 +250,316 @@
         pltpu.make_async_copy(slot, slot, in_sem.at[i % DEPTH]).wait()
 
     def out_copy(i):
-        core, g, j, _ = items[i]
-        return pltpu.make_async_copy(
-            buffer.at[i % DEPTH], outs[g].at[core, j], out_sem.at[i % DEPTH]
-        )
+        core, g = items[i]
+        return pltpu.make_async_copy(buffer.at[i % DEPTH], outs[g].at[core], out_sem.at[i % DEPTH])
 
     staged(
         len(items), DEPTH, load, drain_in, lambda i: out_copy(i).start(), lambda i: out_copy(i).wait()
     )
 
 
-def gather_tiles_here(own, tile_slot, sizes, extra, small):
-    near, far, moved, small = gather_parts(own, extra, small)
-    near_other = [swap(v, "core") for v in near]
-    far_other = [swap(v, "core") for v in far]
-    position, place = slot_places(tile_slot, own.shape[0])
-    rows, width = near[0].shape[1:]
-    anywhere = pl.BlockSpec(memory_space=pl.ANY)
-    smem = pl.BlockSpec(memory_space=pltpu.SMEM)
+ANYWHERE = pl.BlockSpec(memory_space=pl.ANY)
+IN_SMEM = pl.BlockSpec(memory_space=pltpu.SMEM)
+IN_VMEM = pl.BlockSpec(memory_space=pltpu.VMEM)
+
+
+def assemble(place, sources, first, count):
+    rows, width = sources[0].shape[1:]
     mats = pl.pallas_call(
-        lambda *refs: assemble_kernel(sizes, *refs),
-        in_specs=[smem, smem] + [anywhere] * 16,
-        out_specs=[anywhere] * len(sizes),
-        out_shape=[jax.ShapeDtypeStruct((2, n, 4, rows, width), own.dtype) for n in sizes],
-        scratch_shapes=[
-            pltpu.VMEM((DEPTH, 4, rows, width), own.dtype),
-            pltpu.SemaphoreType.DMA((DEPTH,)),
-            pltpu.SemaphoreType.DMA((DEPTH,)),
-        ],
-        compiler_params=pltpu.CompilerParams(vmem_limit_bytes=32 * 1024 * 1024),
-    )(position, place, *near, *far, *near_other, *far_other)
-    return [m.reshape(-1, width) for m in mats], moved, small
-
-
-def scatter_kernel(sizes, position_ref, place_ref, *refs):
-    sources, outs = refs[: len(sizes)], refs[len(sizes) : len(sizes) + 8]
-    buffer, in_sem, out_sem = refs[len(sizes) + 8 :]
-    items = [(g, j) for g, count in enumerate(sizes) for j in range(count)]
-
-    def in_copy(i):
-        g, j = items[i]
-        return pltpu.make_async_copy(
-            sources[g].at[j], buffer.at[i % DEPTH], in_sem.at[i % DEPTH]
-        )
-
-    def store(i):
-        for b in range(4):
-            when_placed(
-                position_ref,
-                place_ref,
-                i,
-                b,
-                lambda array, far, index: pltpu.make_async_copy(
-                    buffer.at[i % DEPTH, b],
-                    outs[far * 4 + array].at[index],
-                    out_sem.at[i % DEPTH],
-                ).start(),
-            )
-
-    def drain_out(i):
-        slot = buffer.at[i % DEPTH]
-        pltpu.make_async_copy(slot, slot, out_sem.at[i % DEPTH]).wait()
-
-    staged(
-        len(items),
-        DEPTH,
-        lambda i: in_copy(i).start(),
-        lambda i: in_copy(i).wait(),
-        store,
-        drain_out,
-    )
-
-
-def reduce_tiles_here(halves, tile_slot, slots, sizes, small):
-    rows, width = halves[0].shape[2:]
-    position, place = slot_places(tile_slot, slots)
-    anywhere = pl.BlockSpec(memory_space=pl.ANY)
-    smem = pl.BlockSpec(memory_space=pltpu.SMEM)
-    shapes = [jax.ShapeDtypeStruct((8 * len(parts), rows, width), bf16) for _, parts in LAST]
-    arrays = pl.pallas_call(
-        lambda *refs: scatter_kernel(sizes, *refs),
-        in_specs=[smem, smem] + [anywhere] * len(sizes),
-        out_specs=[anywhere] * 8,
-        out_shape=shapes + shapes,
+        lambda *refs: assemble_kernel(first, *refs),
+        in_specs=[IN_SMEM] + [ANYWHERE] * SOURCES,
+        out_specs=[ANYWHERE] * count,
+        out_shape=[jax.ShapeDtypeStruct((2, 4, rows, width), bf16)] * count,
         scratch_shapes=[
             pltpu.VMEM((DEPTH, 4, rows, width), bf16),
             pltpu.SemaphoreType.DMA((DEPTH,)),
             pltpu.SemaphoreType.DMA((DEPTH,)),
         ],
         compiler_params=pltpu.CompilerParams(vmem_limit_bytes=32 * 1024 * 1024),
-    )(position, place, *halves)
+        cost_estimate=pl.CostEstimate(
+            flops=0, bytes_accessed=count * 32 * rows * width, transcendentals=0
+        ),
+    )(place, *sources)
+    return [m.reshape(-1, width) for m in mats]
+
+
+def gather_sources(master, extra, small):
+    near, far, moved, small = gather_parts(master, extra, small)
+    near_other = swap(jnp.concatenate(near), "core")
+    far_other = [swap(v, "core") for v in far]
+    return near + far + [near_other] + far_other, moved, small
+
+
+BPS = 2
+STEPS = 4 // BPS
+
+
+def fetch_rows(at, item, firsts, count, place_ref, sources, buffers, sems):
+    core, step = item
+    rows = sources[0].shape[1]
+    for m, first in enumerate(firsts):
+        for i in range(BPS):
+            for j in range(count):
+                at_place(
+                    place_ref[step * BPS + i, first + j],
+                    sources[core * 8 : core * 8 + 8],
+                    lambda array, index: pltpu.make_async_copy(
+                        array.at[index],
+                        buffers[m].at[at, pl.ds((i * count + j) * rows, rows)],
+                        sems.at[m, at],
+                    ).start(),
+                )
+
+
+def arrived(m, at, buffers, sems):
+    pltpu.make_async_copy(buffers[m].at[at], buffers[m].at[at], sems.at[m, at]).wait()
+    return buffers[m][at]
+
+
+def ffn_kernel(firsts, count, place_ref, normed_ref, base_ref, *refs):
+    sources = sixteen(refs)
+    out_ref, act_ref, slope_ref, in_buf, out_buf, sems = refs[SOURCES:]
+    buffers = (in_buf, out_buf)
+    size = in_buf.shape[1]
+    items = [(core, q) for core in range(2) for q in range(STEPS)]
+    for i in range(2):
+        fetch_rows(i, items[i], firsts, count, place_ref, sources, buffers, sems)
+    for i, (core, q) in enumerate(items):
+        cut = slice(i * size, (i + 1) * size)
+        hidden = dot_rows(normed_ref[...], arrived(0, i % 2, buffers, sems))
+        sig = jax.nn.sigmoid(hidden)
+        active = (hidden * sig).astype(bf16)
+        act_ref[:, cut] = active
+        slope_ref[:, cut] = (sig * (1.0 + hidden * (1.0 - sig))).astype(bf16)
+        before = base_ref[...] if i == 0 else out_ref[...]
+        out_ref[...] = before + 0.5 * dot_plain(active, arrived(1, i % 2, buffers, sems))
+        if i + 2 < len(items):
+            fetch_rows(i % 2, items[i + 2], firsts, count, place_ref, sources, buffers, sems)
+
+
+def ffn_back_kernel(cores, based, firsts, count, place_ref, e_ref, act_ref, slope_ref, normed_ref, *refs):
+    base_ref, refs = (refs[0], refs[1:]) if based else (None, refs)
+    sources, refs = sixteen(refs), refs[SOURCES:]
+    dx_ref, grads, refs = refs[0], refs[1 : 1 + 2 * len(cores)], refs[1 + 2 * len(cores) :]
+    in_grads, out_grads, put_sems, in_buf, out_buf, sems = refs
+    buffers = (in_buf, out_buf)
+    size = in_buf.shape[1]
+    items = [(core, q) for core in cores for q in range(STEPS)]
+    for i in range(2):
+        fetch_rows(i, items[i], firsts, count, place_ref, sources, buffers, sems)
+
+    def copy(m, i):
+        core, q = items[i]
+        target = grads[2 * cores.index(core) + m].at[pl.ds(q * size, size)]
+        buffer = (in_grads, out_grads)[m]
+        return pltpu.make_async_copy(buffer.at[i % 2], target, put_sems.at[m, i % 2])
+
+    for i, (core, q) in enumerate(items):
+        cut = slice((core * STEPS + q) * size, (core * STEPS + q + 1) * size)
+        incoming = e_ref[...]
+        grad = dot_rows(incoming, arrived(1, i % 2, buffers, sems)) * slope_ref[:, cut].astype(f32)
+        grad = grad.astype(bf16)
+        change = dot_plain(grad, arrived(0, i % 2, buffers, sems))
+        if i + 2 < len(items):
+            fetch_rows(i % 2, items[i + 2], firsts, count, place_ref, sources, buffers, sems)
+        if i > 0:
+            dx_ref[...] += change
+        elif based:
+            dx_ref[...] = base_ref[...] + change
+        else:
+            dx_ref[...] = change
+        if i >= 2:
+            copy(1, i - 2).wait()
+        out_grads[i % 2] = dot_cols(act_ref[:, cut], incoming).astype(bf16)
+        copy(1, i).start()
+        if i >= 2:
+            copy(0, i - 2).wait()
+        in_grads[i % 2] = dot_cols(grad, normed_ref[...]).astype(bf16)
+        copy(0, i).start()
+    for i in range(len(items) - 2, len(items)):
+        for m in range(2):
+            copy(m, i).wait()
+
+
+def grads_kernel(pairs, lefts, rights, *refs):
+    left_refs, right_refs = refs[:lefts], refs[lefts : lefts + rights]
+    other, own, buffer, sems = refs[lefts + rights :]
+    half = own.shape[1]
+    for k, (i, j) in enumerate(pairs):
+        slot = k % 2
+        if k >= 2:
+            pltpu.make_async_copy(buffer.at[slot], buffer.at[slot], sems.at[slot]).wait()
+        buffer[slot] = dot_cols(left_refs[i][...], right_refs[j][...]).astype(bf16)
+        pltpu.make_async_copy(buffer.at[slot, pl.ds(0, half)], own.at[k], sems.at[slot]).start()
+        pltpu.make_async_copy(buffer.at[slot, pl.ds(half, half)], other.at[k], sems.at[slot]).start()
+    for slot in range(2):
+        pltpu.make_async_copy(buffer.at[slot], buffer.at[slot], sems.at[slot]).wait()
+
+
+def single_grads(pairs, lefts, rights):
+    rows, width = lefts[0].shape
+    shape = jax.ShapeDtypeStruct((len(pairs), width // 2, width), bf16)
+    return pl.pallas_call(
+        lambda *refs: grads_kernel(pairs, len(lefts), len(rights), *refs),
+        in_specs=[IN_VMEM] * (len(lefts) + len(rights)),
+        out_specs=[ANYWHERE] * 2,
+        out_shape=[shape] * 2,
+        scratch_shapes=[pltpu.VMEM((2, width, width), bf16), pltpu.SemaphoreType.DMA((2,))],
+        compiler_params=pltpu.CompilerParams(vmem_limit_bytes=32 * 1024 * 1024),
+        cost_estimate=pl.CostEstimate(
+            flops=2 * len(pairs) * rows * width * width,
+            bytes_accessed=2 * len(pairs) * width * (width + 2 * rows),
+            transcendentals=0,
+        ),
+    )(*lefts, *rights)
+
+
+def ffn_scratch(count, rows, width):
+    return [
+        pltpu.VMEM((2, BPS * count * rows, width), bf16),
+        pltpu.VMEM((2, BPS * count * rows, width), bf16),
+        pltpu.SemaphoreType.DMA((2, 2)),
+    ]
+
+
+def ffn_forward_here(stream, gain, bias, firsts, count, place, sources):
+    rows, width = stream.shape
+    block = sources[0].shape[1]
+    hidden = 8 * count * block
+    shape = jax.ShapeDtypeStruct
+    stats = norm_stats(stream)
+    normed = norm_apply(stream, stats, gain, bias).astype(bf16)
+    result, active, slope = pl.pallas_call(
+        lambda *refs: ffn_kernel(firsts, count, *refs),
+        in_specs=[IN_SMEM] + [IN_VMEM] * 2 + [ANYWHERE] * SOURCES,
+        out_specs=[IN_VMEM] * 3,
+        out_shape=[
+            shape((rows, width), f32),
+            shape((rows, hidden), bf16),
+            shape((rows, hidden), bf16),
+        ],
+        scratch_shapes=ffn_scratch(count, block, width),
+        compiler_params=pltpu.CompilerParams(vmem_limit_bytes=FORWARD_MB * 1024 * 1024),
+        cost_estimate=pl.CostEstimate(
+            flops=4 * rows * width * hidden,
+            bytes_accessed=4 * hidden * (width + rows),
+            transcendentals=rows * hidden,
+        ),
+    )(place, normed, stream, *sources)
+    return (result, (stats, normed, active, slope))
+
+
+FORWARD_MB = 40
+BACKWARD_MB = 48
+
+
+def ffn_backward_here(upstream, stream, gain, kept, firsts, count, place, sources, calls):
+    stats, normed, active, slope = kept
+    rows, width = stream.shape
+    block = sources[0].shape[1]
+    half = 4 * count * block
+    size = BPS * count * block
+    shape = jax.ShapeDtypeStruct
+    incoming = (0.5 * upstream).astype(bf16)
+    base, grads = [], []
+    for cores in calls:
+        dx, *some = pl.pallas_call(
+            lambda *refs, cores=cores: ffn_back_kernel(cores, bool(base), firsts, count, *refs),
+            in_specs=[IN_SMEM] + [IN_VMEM] * (4 + len(base)) + [ANYWHERE] * SOURCES,
+            out_specs=[IN_VMEM] + [ANYWHERE] * (2 * len(cores)),
+            out_shape=[shape((rows, width), f32)]
+            + [shape((half, width), bf16)] * (2 * len(cores)),
+            scratch_shapes=[
+                pltpu.VMEM((2, size, width), bf16),
+                pltpu.VMEM((2, size, width), bf16),
+                pltpu.SemaphoreType.DMA((2, 2)),
+            ]
+            + ffn_scratch(count, block, width),
+            compiler_params=pltpu.CompilerParams(vmem_limit_bytes=BACKWARD_MB * 1024 * 1024),
+            cost_estimate=pl.CostEstimate(
+                flops=8 * rows * width * half * len(cores),
+                bytes_accessed=8 * half * (width + rows) * len(cores),
+                transcendentals=0,
+            ),
+        )(place, incoming, active, slope, normed, *base, *sources)
+        base = [dx]
+        if not grads:
+            some = [swap(v, "core") for v in some[:2]] + some[2:]
+        grads += some
+    other_in, other_out, own_in, own_out = grads
+    back, grad_gain, grad_bias = norm_backward(stream, stats, gain, dx)
+    return (upstream + back, (own_in, other_in), (own_out, other_out), grad_gain, grad_bias)
+
+
+SCATTER = 6
+
+
+def scatter_kernel(groups, place_ref, *refs):
+    owns, others = refs[: len(groups)], refs[len(groups) : 2 * len(groups)]
+    outs = refs[2 * len(groups) : 2 * len(groups) + 8]
+    own_buf, other_buf, in_sem, out_sem = refs[2 * len(groups) + 8 :]
+    items = []
+    for g, (first, count, whole) in enumerate(groups):
+        if whole:
+            items += [(g, k, [(b, first + k) for b in range(4)]) for k in range(count)]
+        else:
+            items += [(g, b, [(b, first + j) for j in range(count)]) for b in range(4)]
+
+    def in_copies(i):
+        g, k, _ = items[i]
+        slot = i % SCATTER
+        return (
+            pltpu.make_async_copy(owns[g].at[k], own_buf.at[slot], in_sem.at[0, slot]),
+            pltpu.make_async_copy(others[g].at[k], other_buf.at[slot], in_sem.at[1, slot]),
+        )
+
+    def load(i):
+        for copy in in_copies(i):
+            copy.start()
+
+    def drain_in(i):
+        for copy in in_copies(i):
+            copy.wait()
+
+    def store(i):
+        slot = i % SCATTER
+        own_buf[slot] = (own_buf[slot].astype(f32) + other_buf[slot].astype(f32)).astype(bf16)
+        for at, (b, tile) in enumerate(items[i][2]):
+            at_place(
+                place_ref[b, tile],
+                outs,
+                lambda array, index: pltpu.make_async_copy(
+                    own_buf.at[slot, at], array.at[index], out_sem.at[slot]
+                ).start(),
+            )
+
+    def drain_out(i):
+        slot = own_buf.at[i % SCATTER]
+        pltpu.make_async_copy(slot, slot, out_sem.at[i % SCATTER]).wait()
+
+    staged(len(items), SCATTER, load, drain_in, store, drain_out)
+
+
+def reduce_tiles_here(groups, owns, others, place, slots, small, ahead):
+    rows, width = owns[0].shape[2:]
+    shapes = [jax.ShapeDtypeStruct((8 * len(parts), rows, width), bf16) for _, parts in LAST]
+    arrays = pl.pallas_call(
+        lambda *refs: scatter_kernel(groups, *refs),
+        in_specs=[IN_SMEM] + [ANYWHERE] * (2 * len(groups)),
+        out_specs=[ANYWHERE] * 8,
+        out_shape=shapes + shapes,
+        scratch_shapes=[
+            pltpu.VMEM((SCATTER, 4, rows, width), bf16),
+            pltpu.VMEM((SCATTER, 4, rows, width), bf16),
+            pltpu.SemaphoreType.DMA((2, SCATTER)),
+            pltpu.SemaphoreType.DMA((SCATTER,)),
+        ],
+        compiler_params=pltpu.CompilerParams(vmem_limit_bytes=32 * 1024 * 1024),
+        cost_estimate=pl.CostEstimate(
+            flops=0, bytes_accessed=6 * 92 * rows * width, transcendentals=0
+        ),
+    )(place, *owns, *others)
+    arrays, ahead = lax.optimization_barrier((arrays, ahead))
     keep = {n: a for (n, _), a in zip(LAST, arrays[:4])}
     send = {n: a for (n, _), a in zip(LAST, arrays[4:])}
     state = [None] * 6
@@ -335,17 +575,52 @@
         got = {name: swap(value, name) for name, value in send.items()}
         small = small + swap(small, ("z2", "z1", "x", "y")[step])
         got, small = lax.optimization_barrier((got, small))
+        if step == 0:
+            return [keep[n] for n in groups], [got[n] for n in groups], small, ahead
         size = 1 << step
         for name, parts in groups.items():
             for i, p in enumerate(parts):
                 cut = slice(i * size, (i + 1) * size)
                 state[p] = keep[name][cut].astype(f32) + got[name][cut].astype(f32)
-    return jnp.concatenate(state).reshape(slots, HALVES * rows, width), small
+
+
+def update_kernel(filled_ref, k0, g0, k1, g1, w_ref, m_ref, v_ref, m_new, v_new, w_new, b_new):
+    half = pl.program_id(1)
+    first = k0[...].astype(f32) + g0[...].astype(f32)
+    second = k1[...].astype(f32) + g1[...].astype(f32)
+    gradient = jnp.where(half == 0, first, second)
+    gradient = jnp.where(filled_ref[pl.program_id(0)] > 0, gradient, 0.0)
+    moment, square, weight = adamw_step(
+        w_ref[...], gradient, m_ref[...], v_ref[...], tile_rate, weight_decay
+    )
+    m_new[...], v_new[...], w_new[...] = moment, square, weight
+    b_new[...] = weight.astype(bf16)
+
+
+def update_tiles_here(keep, got, filled, master, tile_first, tile_second):
+    slots, full, width = master.shape
+    rows = full // HALVES
+    part = pl.BlockSpec((1, rows, width), lambda s, h: (s, 0, 0))
+    here = pl.BlockSpec((1, rows, width), lambda s, h: (s, h, 0))
+    shape = jax.ShapeDtypeStruct(master.shape, f32)
+    return pl.pallas_call(
+        update_kernel,
+        grid=(slots, HALVES),
+        in_specs=[IN_SMEM] + [part] * 4 + [here] * 3,
+        out_specs=[here] * 4,
+        out_shape=[shape] * 3 + [jax.ShapeDtypeStruct(master.shape, bf16)],
+        compiler_params=pltpu.CompilerParams(vmem_limit_bytes=32 * 1024 * 1024),
+        cost_estimate=pl.CostEstimate(
+            flops=20 * slots * full * width,
+            bytes_accessed=30 * slots * full * width,
+            transcendentals=slots * full * width,
+        ),
+    )(filled, keep[0], got[0], keep[1], got[1], master, tile_first, tile_second)
 
 
 def owned_mask(tile_slot, slots):
     slot = lax.axis_index("dp") * slots + jnp.arange(slots, dtype=jnp.int32)
-    return jnp.any(slot[:, None] == tile_slot[None, :], axis=1)[:, None, None]
+    return jnp.any(slot[:, None] == tile_slot[None, :], axis=1)
 
 
 def gather_tiles(own, tile_slot, sizes):
@@ -393,11 +668,11 @@
 
 
 def masked_probs(query, key, valid):
-    scores = dot_rows(query, key) * HEAD_DIM ** (-0.5)
+    scores = dot_rows(query, key)
     column = lax.broadcasted_iota(jnp.int32, scores.shape, 1)
-    scores = jnp.where(column < valid, scores, masked_score)
+    scores = jnp.where(column < valid, scores * HEAD_DIM ** (-0.5), masked_score)
     exponent = jnp.exp(scores - jnp.max(scores, axis=-1, keepdims=True))
-    return exponent / jnp.sum(exponent, axis=-1, keepdims=True)
+    return exponent * (1.0 / jnp.sum(exponent, axis=-1, keepdims=True))
 
 
 def attend_kernel(valid_ref, q_ref, k_ref, v_ref, out_ref):
@@ -446,20 +721,16 @@
     return (stream + 0.5 * dot_plain(active, w_out), (stats, normed, active, slope))
 
 
-def weight_grad(left, right, local):
-    if not local:
-        return dot_cols(left, right).astype(bf16)
-    half = left.shape[1] // 2
-    other = swap(dot_cols(left[:, half:], right).astype(bf16), "core")
-    return (dot_cols(left[:, :half], right) + other.astype(f32)).astype(bf16)
-
-
-def ffn_backward(upstream, stream, gain, kept, w_in, w_out, local):
+def weight_grad(left, right):
+    return dot_cols(left, right).astype(bf16)
+
+
+def ffn_backward(upstream, stream, gain, kept, w_in, w_out):
     stats, normed, active, slope = kept
     incoming = (0.5 * upstream).astype(bf16)
-    grad_out = weight_grad(active, incoming, local)
+    grad_out = weight_grad(active, incoming)
     grad_hidden = (dot_rows(incoming, w_out) * slope.astype(f32)).astype(bf16)
-    grad_in = weight_grad(grad_hidden, normed, local)
+    grad_in = weight_grad(grad_hidden, normed)
     back, grad_gain, grad_bias = norm_backward(stream, stats, gain, dot_plain(grad_hidden, w_in))
     return (upstream + back, grad_in, grad_out, grad_gain, grad_bias)
 
@@ -516,9 +787,9 @@
             lax.dynamic_index_in_dim(both, chan_index ^ mask, 0, keepdims=True)
             for mask in range(1, chan_count)
         ]
-        mats, moved, convs = gather_tiles_here(
-            master.astype(bf16), tile_slot, sizes, extra, conv_params
-        )
+        sources, moved, convs = gather_sources(master, extra, conv_params)
+        place = slot_places(tile_slot, slots)
+        mats = [None] * 4 + assemble(place, sources, base, tile_count - base)
         for mask in range(1, chan_count):
             mine = lax.dynamic_update_slice_in_dim(mine, moved[mask - 1], chan_index ^ mask, 0)
         near = jnp.array([0, 2, 1, 3], jnp.int32)
@@ -540,7 +811,30 @@
     bn_gain, bn_bias = convs[taps], convs[taps + 1]
     frame_mask = (jnp.arange(rows, dtype=jnp.int32) < valid[0]).astype(f32)[:, None]
 
-    stream_one, kept_one = ffn_forward(source, gains[0], biases[0], in_first, out_first)
+    def forward(stream, norm, first, w_in, w_out):
+        if local:
+            firsts = (first, first + quarter)
+            return ffn_forward_here(
+                stream, gains[norm], biases[norm], firsts, quarter, place, sources
+            )
+        return ffn_forward(stream, gains[norm], biases[norm], w_in, w_out)
+
+    def send_home(value):
+        value = value.astype(bf16).reshape(chan_count, seg_rows, width)
+        if not local:
+            return swap_blocks(value, "chan")
+        here, there = swap_in_hops(value)
+        return (here, exchange(there, "chan", 2))
+
+    def backward(upstream, stream, norm, kept, first, w_in, w_out, calls):
+        if local:
+            firsts = (first, first + quarter)
+            return ffn_backward_here(
+                upstream, stream, gains[norm], kept, firsts, quarter, place, sources, calls
+            )
+        return ffn_backward(upstream, stream, gains[norm], kept, w_in, w_out)
+
+    stream_one, kept_one = forward(source, 0, 0, in_first, out_first)
 
     stats_att = norm_stats(stream_one)
     att_in = norm_apply(stream_one, stats_att, gains[1], biases[1]).astype(bf16)
@@ -576,21 +870,29 @@
     conv_act = (normal * conv_sig).astype(bf16)
     stream_three = stream_two + dot_plain(conv_act, p_output)
 
-    stream_four, kept_four = ffn_forward(stream_three, gains[3], biases[3], in_second, out_second)
+    stream_four, kept_four = forward(stream_three, 3, 2 * quarter, in_second, out_second)
     stats_last = norm_stats(stream_four)
     result = norm_apply(stream_four, stats_last, gains[4], biases[4]).astype(bf16)
 
     grad_four, gain_four, bias_four = norm_backward(stream_four, stats_last, gains[4], upstream)
-    grad_three, gin_second, gout_second, gain_three, bias_three = ffn_backward(
-        grad_four, stream_three, gains[3], kept_four, in_second, out_second, local
+    grad_three, gin_second, gout_second, gain_three, bias_three = backward(
+        grad_four, stream_three, 3, kept_four, 2 * quarter, in_second, out_second, ((1, 0),)
     )
 
     incoming = grad_three.astype(bf16)
-    grad_po = weight_grad(conv_act, incoming, local)
+    incoming_three = incoming
+    grad_po = None if local else weight_grad(conv_act, incoming)
     conv_slope = conv_sig * (1.0 + normal * (1.0 - conv_sig))
     grad_normal = dot_rows(incoming, p_output) * conv_slope
     own_sums = jnp.stack([jnp.sum(grad_normal, axis=0), jnp.sum(grad_normal * center, axis=0)])
-    sum_plain, sum_center = butterfly_sum(own_sums, "dp")
+    sums = butterfly_sum(own_sums, "dp")
+    if local:
+        block_out = send_home(result)
+        sums, block_out = lax.optimization_barrier((sums, block_out))
+        block_out = finish_hops(*block_out)
+    else:
+        block_out = send_home(result)
+    sum_plain, sum_center = sums
     bn_scale = bn_gain * inv_std
     grad_depth = bn_scale * grad_normal - frame_mask * bn_scale * (
         sum_plain + inv_std * inv_std * sum_center * center
@@ -603,8 +905,9 @@
     grad_glu = grad_glu * frame_mask
     grad_linear = (grad_glu * gate_sig).astype(bf16)
     grad_gating = (grad_glu * linear * gate_sig * (1.0 - gate_sig)).astype(bf16)
-    grad_pv = weight_grad(grad_linear, conv_in, local)
-    grad_pg = weight_grad(grad_gating, conv_in, local)
+    if not local:
+        grad_pv = weight_grad(grad_linear, conv_in)
+        grad_pg = weight_grad(grad_gating, conv_in)
     back, gain_two, bias_two = norm_backward(
         stream_two,
         stats_conv,
@@ -614,14 +917,25 @@
     grad_two = grad_three + back
 
     incoming = grad_two.astype(bf16)
-    grad_wo = weight_grad(merged, incoming, local)
+    grad_wo = None if local else weight_grad(merged, incoming)
     grad_merged = dot_rows(incoming, w_output).astype(bf16)
+    if local:
+        grad_merged, gin_second, gout_second = lax.optimization_barrier(
+            (grad_merged, gin_second, gout_second)
+        )
     grad_q, grad_k, grad_v = head_call(
         attend_back_kernel, valid, (queries, keys, values, grad_merged), 3, 10
     )
-    grad_wq = weight_grad(grad_q, att_in, local)
-    grad_wk = weight_grad(grad_k, att_in, local)
-    grad_wv = weight_grad(grad_v, att_in, local)
+    if local:
+        singles_other, singles_own = single_grads(
+            ((0, 0), (1, 0), (2, 0), (3, 1), (4, 2), (5, 2), (6, 3)),
+            (grad_q, grad_k, grad_v, merged, grad_linear, grad_gating, conv_act),
+            (att_in, incoming, conv_in, incoming_three),
+        )
+    else:
+        grad_wq = weight_grad(grad_q, att_in)
+        grad_wk = weight_grad(grad_k, att_in)
+        grad_wv = weight_grad(grad_v, att_in)
     back, gain_one, bias_one = norm_backward(
         stream_one,
         stats_att,
@@ -629,13 +943,15 @@
         dot_plain(grad_q, w_query) + dot_plain(grad_k, w_key) + dot_plain(grad_v, w_value),
     )
     grad_one = grad_two + back
-
-    grad_zero, gin_first, gout_first, gain_zero, bias_zero = ffn_backward(
-        grad_one, source, gains[0], kept_one, in_first, out_first, local
-    )
-
-    grads = [gin_first, gout_first, gin_second, gout_second]
-    grads += [grad_wq, grad_wk, grad_wv, grad_wo, grad_pv, grad_pg, grad_po]
+    if local:
+        grad_one, singles_other = lax.optimization_barrier((grad_one, singles_other))
+        singles_other = swap(singles_other, "core")
+
+    grad_zero, gin_first, gout_first, gain_zero, bias_zero = backward(
+        grad_one, source, 0, kept_one, 0, in_first, out_first, ((1,), (0,))
+    )
+    block_grad = send_home(grad_zero)
+
     conv_small = jnp.stack(tap_grads + [own_sums[1] * inv_std, own_sums[0]])
     conv_small = conv_small.reshape(-1, chan_count, rows_tile)[:, position].reshape(-1, width)
     small = jnp.concatenate(
@@ -648,40 +964,57 @@
         ]
     )
     if local:
-        halves = [g.reshape(n, 4, -1, width) for g, n in zip(grads, sizes)]
         small = small + swap(small, "core")
-        owned, small = reduce_tiles_here(halves, tile_slot, slots, sizes, small)
+        groups = [(i * quarter, quarter, False) for i in range(4)]
+        groups.append((base, tile_count - base, True))
+        pairs = [
+            tuple(v.reshape(4, quarter, -1, width) for v in pair)
+            for pair in (gin_first, gout_first, gin_second, gout_second)
+        ]
+        shape = (tile_count - base, 4) + pairs[0][0].shape[2:]
+        pairs.append((singles_own.reshape(shape), singles_other.reshape(shape)))
+        keep, got, small, block_grad = reduce_tiles_here(
+            groups, [p[0] for p in pairs], [p[1] for p in pairs], place, slots, small, block_grad
+        )
+        block_grad = finish_hops(*block_grad)
+        tile_m, tile_v, tile_w, tile_b = update_tiles_here(
+            keep,
+            got,
+            owned_mask(tile_slot, slots).astype(jnp.int32),
+            master,
+            tile_first,
+            tile_second,
+        )
     else:
+        grads = [gin_first, gout_first, gin_second, gout_second]
+        grads += [grad_wq, grad_wk, grad_wv, grad_wo, grad_pv, grad_pg, grad_po]
         owned = reduce_tiles(
             jnp.concatenate(grads).reshape(tile_count, width, width), tile_slot, slots
         )
         small = butterfly_sum(butterfly_sum(small, "dp"), "chan")
-    owned = jnp.where(owned_mask(tile_slot, slots), owned, 0.0)
+        owned = jnp.where(owned_mask(tile_slot, slots)[:, None, None], owned, 0.0)
+        tile_m, tile_v, tile_w = adamw_step(
+            master, owned, tile_first, tile_second, tile_rate, weight_decay
+        )
+        tile_b = tile_w.astype(bf16)
     norm_total = small[: norm_params.shape[0]]
     conv_grad = lax.dynamic_slice_in_dim(
         small[norm_params.shape[0] :], chan_index * rows_tile, rows_tile, 1
     )
 
-    tile_m, tile_v, tile_w = adamw_step(
-        master, owned, tile_first, tile_second, tile_rate, weight_decay
-    )
     norm_m, norm_v, norm_w = adamw_step(
         norm_params, norm_total, norm_first, norm_second, small_rate, 0.0
     )
     conv_m, conv_v, conv_w = adamw_step(
         conv_params, conv_grad, conv_first, conv_second, small_rate, 0.0
     )
-    block_out = swap_blocks(result.reshape(chan_count, seg_rows, width), "chan")
-    block_grad = swap_blocks(
-        grad_zero.astype(bf16).reshape(chan_count, seg_rows, width), "chan"
-    ).astype(f32)
     return (
         block_out[:, None],
-        block_grad[:, None],
+        block_grad[:, None].astype(f32),
         tile_m,
         tile_v,
         tile_w,
-        tile_w.astype(bf16),
+        tile_b,
         norm_m,
         norm_v,
         norm_w,

time: 837 us -> 766 us (0.915)
  matrix products: 181 us -> 24.8 us
  Pallas kernels: 61.8 us -> 160 us
  local copies, waits for them, and re-layouts: 53 us -> 39.7 us
  starting transfers between devices: 57.1 us -> 48.6 us
    pallas_call x2 -> x9, Pallas kernels: 37.8 us -> 136 us  [the longest x3 62.3 us: ffn_backward_here(): pl.pallas_call(lambda *refs, cores=cores: ffn_back_kernel(cores, bool(bas...]
    dot_general x22 -> x0, matrix products: 64.7 us -> none  [dot_cols(): lax.dot_general(left, right, (((0,), (0,)), ((), ())), preferred_element_...]
    dot_general x11 -> x7, matrix products: 64.6 us -> 12.3 us  [dot_rows(): lax.dot_general(left, right, (((1,), (1,)), ((), ())), preferred_element_...]
    dot_general x11 -> x7, matrix products: 51.5 us -> 12.4 us  [dot_plain(): return jnp.dot(left, right, preferred_element_type=f32)]
    concatenate x1 -> x4, other arithmetic: 0.06 us -> 10.5 us  [the longest x1 10.3 us: gather_sources(): near_other = swap(jnp.concatenate(near), 'core')]
    ppermute x52 -> x43, starting transfers between devices: 48.5 us -> 38.5 us  [swap(): return lax.ppermute(value, BOTH, [(i, i ^ BITS[name]) for i in range(size)])]
    unnamed x253 -> x243, local copies, waits for them, and re-layouts: 30.6 us -> 26.4 us
    ppermute x52 -> x43, waiting for transfers between devices: 346 us -> 349 us  [swap(): return lax.ppermute(value, BOTH, [(i, i ^ BITS[name]) for i in range(size)])]
  transfers between devices with their start and end apart: 69 -> 58, of which waited for: 29 -> 27; matrix products, arithmetic and copies ran while one was open for 16% -> 4% of each run, Pallas kernels for 2% -> 7%
where the time goes in v3:
time: 766 us; the launch traced here: 758 us
  waiting for transfers between devices  411 us (54%)
  Pallas kernels  160 us (21%)
  other arithmetic  70.6 us (9%)
  starting transfers between devices  48.6 us (6%)
  local copies, waits for them, and re-layouts  39.7 us (5%)
  matrix products  24.8 us (3%)
    ppermute x43, waiting for transfers between devices, swap(): return lax.ppermute(value, BOTH, [(i, i ^ BITS[name]) for i in range(size)])  349 us
    pallas_call x3, Pallas kernels, ffn_backward_here(): pl.pallas_call(lambda *refs, cores=cores: ffn_back_kernel(cores, bool(bas...  62.3 us
    ppermute x15, waiting for transfers between devices, exchange(): return lax.ppermute(value, axis, [(i, i ^ mask) for i in range(size)])  61.1 us
    ppermute x43, starting transfers between devices, swap(): return lax.ppermute(value, BOTH, [(i, i ^ BITS[name]) for i in range(size)])  38.5 us
    pallas_call x2, Pallas kernels, ffn_forward_here(): pl.pallas_call(lambda *refs: ffn_kernel(firsts, count, *refs), in_specs=[...  33.2 us
    unnamed x243, local copies, waits for them, and re-layouts  26.4 us
    pallas_call x2, Pallas kernels, head_call(): pl.pallas_call(kernel, grid=(width // HEAD_DIM,), in_specs=[pl.BlockSpec(...  23.7 us
    pallas_call x1, Pallas kernels, reduce_tiles_here(): pl.pallas_call(lambda *refs: scatter_kernel(groups, *refs), in_specs=[IN_...  17.7 us
  transfers between devices with their start and end apart: 58, of which 27 were waited for; matrix products, arithmetic and copies ran while one was open for 4% of the time, Pallas kernels for 7%

profile of v3, /device:TPU:0, one launch (start us, length us, event | category | flops | bytes accessed | tf_op | source)
XLA Modules:
  0.0 758.0 jit_solution(9828906496396245101)
XLA Ops:
  13.7 12.6 %collective-permute-done.3 = bf16[1,2,128,1024]{3,2,1,0:T(8,128)(2,1)S(1)} collective-permute-done((bf16[1,2,128,1024]{3,2,1,0:T(8,128)(2,1)S(1)}, bf16[1,2,128,1024]{3,2,1,0:T(8,128)(2,1)S(1)}, u32[]{:S(2)}, u32[]{:S(2)}) %collective-permute-start.3) | collective-permute-done | bytes 524320 | tf_op jit(solution)/shard_map/ppermute | solution.py:48
  26.3 10.5 %collective-permute-done.4 = bf16[1,2,128,1024]{3,2,1,0:T(8,128)(2,1)S(1)} collective-permute-done((bf16[1,2,128,1024]{3,2,1,0:T(8,128)(2,1)S(1)}, bf16[1,2,128,1024]{3,2,1,0:T(8,128)(2,1)S(1)}, u32[]{:S(2)}, u32[]{:S(2)}) %collective-permute-start.4) | collective-permute-done | bytes 524320 | tf_op jit(solution)/shard_map/ppermute | solution.py:48
  36.8 6.4 collective-permute-done
  54.4 15.0 %collective-permute-done.9 = f32[7,256]{1,0:T(8,128)S(1)} collective-permute-done((f32[7,256]{1,0:T(8,128)S(1)}, f32[7,256]{1,0:T(8,128)S(1)}, u32[]{:S(2)}, u32[]{:S(2)}) %collective-permute-start.9) | collective-permute-done | bytes 7200 | tf_op jit(solution)/shard_map/ppermute | solution.py:48
  81.7 38.0 %collective-permute-done.12 = bf16[4,128,1024]{2,1,0:T(8,128)(2,1)S(1)} collective-permute-done((bf16[4,128,1024]{2,1,0:T(8,128)(2,1)S(1)}, bf16[4,128,1024]{2,1,0:T(8,128)(2,1)S(1)}, u32[]{:S(2)}, u32[]{:S(2)}) %collective-permute-start.12) | collective-permute-done | bytes 1048608 | tf_op jit(solution)/shard_map/ppermute | solution.py:123
  126.2 10.3 %pad_maximum_fusion = bf16[48,128,1024]{2,1,0:T(8,128)(2,1)} fusion(bf16[16,128,1024]{2,1,0:T(8,128)(2,1)S(1)} %constant_dynamic-update-slice_fusion.21.refs_6_.refs_4_.refs_8_.refs_9_, bf16[8,128,1024]{2,1,0:T(8,128)(2,1)} %pad_maximum_fusion.2.refs_5_.refs_3_.refs_7_.refs_8_, bf16[8,128,1024]{2,1,0:T(8,128)(2,1)S(1)} %pad_maximum_fusion.1.refs_4_.refs_2_.refs_6_.refs_7_, ...), kind=kLoop, calls=%fused_computation.2 | loop fusion | flops 18874368 | bytes 25165824 | tf_op jit(solution)/shard_map/concatenate | solution.py:288
  139.9 89.6 %collective-permute-done.15.refs_7_.refs_5_.refs_9_.refs_10_ = bf16[16,128,1024]{2,1,0:T(8,128)(2,1)} collective-permute-done((bf16[16,128,1024]{2,1,0:T(8,128)(2,1)S(1)}, bf16[16,128,1024]{2,1,0:T(8,128)(2,1)}, u32[]{:S(2)}, u32[]{:S(2)}) %collective-permute-start.15) | collective-permute-done | bytes 4194336 | tf_op jit(solution)/shard_map/ppermute | solution.py:123
  240.6 5.4 collective-permute-done.21.refs_13_.refs_11_.refs_15_.refs_16_
  249.0 16.6 %shard_map.229 = (f32[512,1024]{1,0:T(8,128)S(1)}, bf16[512,4096]{1,0:T(8,128)(2,1)}, bf16[512,4096]{1,0:T(8,128)(2,1)}) custom-call(s32[4,23]{1,0:T(4,128)S(1)} %pad_add_fusion.refs_0_, bf16[512,1024]{1,0:T(8,128)(2,1)S(1)} %add_convert_fusion.17.refs_1_.refs_4_, f32[512,1024]{1,0:T(8,128)S(1)} %bitcast.196, bf16[16,128,1024]{2,1,0:T(8,128)(2,1)} %copy-done.49, ...), custom_call_target="tpu_custom_call" | custom-call | flops 8589934592 | bytes 25165824 | tf_op jit(solution)/shard_map/pallas_call | solution.py:432
  271.4 6.2 shard_map.230
  285.6 9.3 %shard_map.231.refs_3_ = bf16[512,1024]{1,0:T(8,128)(2,1)S(1)} custom-call(s32[1]{0:T(128)} %bitcast.17.valid_ref, bf16[512,1024]{1,0:T(8,128)(2,1)S(1)} %convolution_convert_fusion.3.q_ref, bf16[512,1024]{1,0:T(8,128)(2,1)S(1)} %convolution_convert_fusion.2.k_ref, bf16[512,1024]{1,0:T(8,128)(2,1)S(1)} %convolution_convert_fusion.1.v_ref), custom_call_target="tpu_custom_call" | custom-call | flops 1073741824 | bytes 4194304 | tf_op jit(solution)/shard_map/pallas_call | solution.py:699
  317.2 4.3 collective-permute-done.26
  328.5 16.6 %shard_map.232 = (f32[512,1024]{1,0:T(8,128)S(1)}, bf16[512,4096]{1,0:T(8,128)(2,1)}, bf16[512,4096]{1,0:T(8,128)(2,1)}) custom-call(s32[4,23]{1,0:T(4,128)S(1)} %pad_add_fusion.refs_0_, bf16[512,1024]{1,0:T(8,128)(2,1)S(1)} %add_convert_fusion.14.refs_1_.refs_4_, f32[512,1024]{1,0:T(8,128)S(1)} %get-tuple-element.472.refs_2_, ...), custom_call_target="tpu_custom_call" | custom-call | flops 8589934592 | bytes 25165824 | tf_op jit(solution)/shard_map/pallas_call | solution.py:432
  352.0 27.4 %shard_map.233 = (f32[512,1024]{1,0:T(8,128)S(1)}, bf16[2048,1024]{1,0:T(8,128)(2,1)}, bf16[2048,1024]{1,0:T(8,128)(2,1)}, bf16[2048,1024]{1,0:T(8,128)(2,1)}, bf16[2048,1024]{1,0:T(8,128)(2,1)}) custom-call(s32[4,23]{1,0:T(4,128)S(1)} %pad_add_fusion.refs_0_, bf16[512,1024]{1,0:T(8,128)(2,1)S(1)} %get-tuple-element.353.refs_1_, ...), custom_call_target="tpu_custom_call" | custom-call | flops 17179869184 | bytes 50331648 | tf_op jit(solution)/shard_map/pallas_call | solution.py:466
  417.0 14.4 %shard_map.234 = (bf16[512,1024]{1,0:T(8,128)(2,1)S(1)}, bf16[512,1024]{1,0:T(8,128)(2,1)S(1)}, bf16[512,1024]{1,0:T(8,128)(2,1)S(1)}) custom-call(s32[1]{0:T(128)} %bitcast.17.valid_ref, bf16[512,1024]{1,0:T(8,128)(2,1)S(1)} %copy-done.28, bf16[512,1024]{1,0:T(8,128)(2,1)S(1)} %copy-done.30, bf16[512,1024]{1,0:T(8,128)(2,1)} %copy-done.31, ...), custom_call_target="tpu_custom_call" | custom-call | flops 2684354560 | bytes 7340032 | tf_op jit(solution)/shard_map/pallas_call | solution.py:699
  435.2 10.5 %shard_map.235 = (bf16[7,512,1024]{2,1,0:T(8,128)(2,1)}, bf16[7,512,1024]{2,1,0:T(8,128)(2,1)}) custom-call(bf16[512,1024]{1,0:T(8,128)(2,1)S(1)} %get-tuple-element.217.refs_0_, bf16[512,1024]{1,0:T(8,128)(2,1)S(1)} %get-tuple-element.218.refs_1_, bf16[512,1024]{1,0:T(8,128)(2,1)S(1)} %get-tuple-element.219.refs_2_, bf16[512,1024]{1,0:T(8,128)(2,1)S(1)} %copy-done.26, ...), custom_call_target="tpu_custom_call" | custom-call | flops 7516192768 | bytes 29360128 | tf_op jit(solution)/shard_map/pallas_call | solution.py:402
  448.9 17.0 %shard_map.236 = (f32[512,1024]{1,0:T(8,128)S(1)}, bf16[2048,1024]{1,0:T(8,128)(2,1)}, bf16[2048,1024]{1,0:T(8,128)(2,1)}) custom-call(s32[4,23]{1,0:T(4,128)S(1)} %pad_add_fusion.refs_0_, bf16[512,1024]{1,0:T(8,128)(2,1)S(1)} %multiply_convert_fusion.refs_1_, bf16[512,4096]{1,0:T(8,128)(2,1)} %get-tuple-element.222.refs_2_, ...), custom_call_target="tpu_custom_call" | custom-call | flops 8589934592 | bytes 25165824 | tf_op jit(solution)/shard_map/pallas_call | solution.py:466
  467.8 17.9 %shard_map.237 = (f32[512,1024]{1,0:T(8,128)S(1)}, bf16[2048,1024]{1,0:T(8,128)(2,1)}, bf16[2048,1024]{1,0:T(8,128)(2,1)}) custom-call(s32[4,23]{1,0:T(4,128)S(1)} %pad_add_fusion.refs_0_, bf16[512,1024]{1,0:T(8,128)(2,1)S(1)} %multiply_convert_fusion.refs_1_, bf16[512,4096]{1,0:T(8,128)(2,1)} %get-tuple-element.222.refs_2_, ...), custom_call_target="tpu_custom_call" | custom-call | flops 8589934592 | bytes 25165824 | tf_op jit(solution)/shard_map/pallas_call | solution.py:466
  495.0 17.7 %shard_map.238 = (bf16[16,128,1024]{2,1,0:T(8,128)(2,1)S(1)}, bf16[8,128,1024]{2,1,0:T(8,128)(2,1)S(1)}, bf16[8,128,1024]{2,1,0:T(8,128)(2,1)S(1)}, bf16[16,128,...) custom-call(s32[4,23]{1,0:T(4,128)S(1)} %pad_add_fusion.refs_0_, ...), custom_call_target="tpu_custom_call" | custom-call | bytes 72351744 | tf_op jit(solution)/shard_map/pallas_call | solution.py:546
  517.2 91.8 %collective-permute-done.44 = f32[17,1024]{1,0:T(8,128)S(1)} collective-permute-done((f32[17,1024]{1,0:T(8,128)S(1)}, f32[17,1024]{1,0:T(8,128)S(1)}, u32[]{:S(2)}, u32[]{:S(2)}) %collective-permute-start.44) | collective-permute-done | bytes 69664 | tf_op jit(solution)/shard_map/ppermute | solution.py:123
  623.4 44.0 %collective-permute-done.49 = f32[17,1024]{1,0:T(8,128)S(1)} collective-permute-done((f32[17,1024]{1,0:T(8,128)S(1)}, f32[17,1024]{1,0:T(8,128)S(1)}, u32[]{:S(2)}, u32[]{:S(2)}) %collective-permute-start.49) | collective-permute-done | bytes 69664 | tf_op jit(solution)/shard_map/ppermute | solution.py:123
  681.1 21.8 %collective-permute-done.54 = f32[17,1024]{1,0:T(8,128)S(1)} collective-permute-done((f32[17,1024]{1,0:T(8,128)S(1)}, f32[17,1024]{1,0:T(8,128)S(1)}, u32[]{:S(2)}, u32[]{:S(2)}) %collective-permute-start.54) | collective-permute-done | bytes 69664 | tf_op jit(solution)/shard_map/ppermute | solution.py:123
  715.6 34.5 %collective-permute-done.57 = f32[17,1024]{1,0:T(8,128)S(1)} collective-permute-done((f32[17,1024]{1,0:T(8,128)S(1)}, f32[17,1024]{1,0:T(8,128)S(1)}, u32[]{:S(2)}, u32[]{:S(2)}) %collective-permute-start.57) | collective-permute-done | bytes 69664 | tf_op jit(solution)/shard_map/ppermute | solution.py:123
  751.5 6.2 shard_map.239
  (531 shorter events, 210.1 us)
Async XLA Ops:
  5.9 37.2 %collective-permute-start = (bf16[3,128,1024]{2,1,0:T(8,128)(2,1)S(1)}, bf16[3,128,1024]{2,1,0:T(8,128)(2,1)S(1)}, u32[]{:S(2)}, u32[]{:S(2)}) collective-permute-start(bf16[3,128,1024]{2,1,0:T(8,128)(2,1)S(1)} %get-tuple-element.155), channel_id=1, source_target_pairs={{0,8},{1,9},{2,10},{3,11},{4,12},{5,13},{6,14},{7,15},{8,0},{9,1},... | collective-permute-start | bytes 2359304 | tf_op jit(solution)/shard_map/ppermute | solution.py:123
  9.0 36.9 %collective-permute-start.1 = (bf16[3,128,1024]{2,1,0:T(8,128)(2,1)S(1)}, bf16[3,128,1024]{2,1,0:T(8,128)(2,1)S(1)}, u32[]{:S(2)}, u32[]{:S(2)}) collective-permute-start(bf16[3,128,1024]{2,1,0:T(8,128)(2,1)S(1)} %copy-done.76), channel_id=1, source_target_pairs={{0,16},{1,17},{2,18},{3,19},{4,20},{5,21},{6,22},{7,23},{8,24},{9,... | collective-permute-start | bytes 2359304 | tf_op jit(solution)/shard_map/ppermute | solution.py:123
  76.5 46.8 %collective-permute-start.10 = (bf16[8,128,1024]{2,1,0:T(8,128)(2,1)S(1)}, bf16[8,128,1024]{2,1,0:T(8,128)(2,1)S(1)}, u32[]{:S(2)}, u32[]{:S(2)}) collective-permute-start(bf16[8,128,1024]{2,1,0:T(8,128)(2,1)S(1)} %get-tuple-element.176), channel_id=1, source_target_pairs={{0,4},{1,5},{2,6},{3,7},{4,0},{5,1},{6,2},{7,3},{8,12},{9,13},{10,... | collective-permute-start | bytes 6291464 | tf_op jit(solution)/shard_map/ppermute | solution.py:123
  77.1 46.2 %collective-permute-start.11 = (bf16[8,128,1024]{2,1,0:T(8,128)(2,1)S(1)}, bf16[8,128,1024]{2,1,0:T(8,128)(2,1)S(1)}, u32[]{:S(2)}, u32[]{:S(2)}) collective-permute-start(bf16[8,128,1024]{2,1,0:T(8,128)(2,1)S(1)} %get-tuple-element.177), channel_id=1, source_target_pairs={{0,2},{1,3},{2,0},{3,1},{4,6},{5,7},{6,4},{7,5},{8,10},{9,11},{10,... | collective-permute-start | bytes 6291464 | tf_op jit(solution)/shard_map/ppermute | solution.py:123
  77.6 42.1 %collective-permute-start.12 = (bf16[4,128,1024]{2,1,0:T(8,128)(2,1)S(1)}, bf16[4,128,1024]{2,1,0:T(8,128)(2,1)S(1)}, u32[]{:S(2)}, u32[]{:S(2)}) collective-permute-start(bf16[4,128,1024]{2,1,0:T(8,128)(2,1)S(1)} %pad_maximum_fusion.8), channel_id=1, source_target_pairs={{0,8},{1,9},{2,10},{3,11},{4,12},{5,13},{6,14},{7,15},{8,0},{9,1},... | collective-permute-start | bytes 3145736 | tf_op jit(solution)/shard_map/ppermute | solution.py:123
  77.9 45.4 %collective-permute-start.13 = (bf16[4,128,1024]{2,1,0:T(8,128)(2,1)S(1)}, bf16[4,128,1024]{2,1,0:T(8,128)(2,1)S(1)}, u32[]{:S(2)}, u32[]{:S(2)}) collective-permute-start(bf16[4,128,1024]{2,1,0:T(8,128)(2,1)S(1)} %pad_maximum_fusion.9), channel_id=1, source_target_pairs={{0,16},{1,17},{2,18},{3,19},{4,20},{5,21},{6,22},{7,23},{8,24},{9,... | collective-permute-start | bytes 3145736 | tf_op jit(solution)/shard_map/ppermute | solution.py:123
  136.4 112.6 %collective-permute-start.19 = (bf16[48,128,1024]{2,1,0:T(8,128)(2,1)}, bf16[48,128,1024]{2,1,0:T(8,128)(2,1)}, u32[]{:S(2)}, u32[]{:S(2)}) collective-permute-start(bf16[48,128,1024]{2,1,0:T(8,128)(2,1)} %pad_maximum_fusion), channel_id=1, source_target_pairs={{0,1},{1,0},{2,3},{3,2},{4,5},{5,4},{6,7},{7,6},{8,9},{9,8},{10,11... | collective-permute-start | bytes 37748744 | tf_op jit(solution)/shard_map/ppermute | solution.py:123
  136.4 93.1 %collective-permute-start.15 = (bf16[16,128,1024]{2,1,0:T(8,128)(2,1)S(1)}, bf16[16,128,1024]{2,1,0:T(8,128)(2,1)}, u32[]{:S(2)}, u32[]{:S(2)}) collective-permute-start(bf16[16,128,1024]{2,1,0:T(8,128)(2,1)S(1)} %get-tuple-element.192.refs_3_.refs_1_.refs_5_.refs_6_), channel_id=1, source_target_pairs={{0,4},{1,5},{2,6},{3,7},{4,0},{5,1},{6,2},{7,3},{8,12},{9,13},{10,... | collective-permute-start | bytes 12582920 | tf_op jit(solution)/shard_map/ppermute | solution.py:123
  137.9 92.8 %collective-permute-start.18 = (bf16[16,128,1024]{2,1,0:T(8,128)(2,1)S(1)}, bf16[16,128,1024]{2,1,0:T(8,128)(2,1)}, u32[]{:S(2)}, u32[]{:S(2)}) collective-permute-start(bf16[16,128,1024]{2,1,0:T(8,128)(2,1)S(1)} %constant_dynamic-update-slice_fusion.21.refs_6_.refs_4_.refs_8_.refs_9_), channel_id=1, source_target_pairs={{0,2},{1,3},{2,0},{3,1},{4,6},{5,7},{6,4},{7,5},{8,10},{9,11},{10,... | collective-permute-start | bytes 12582920 | tf_op jit(solution)/shard_map/ppermute | solution.py:123
  139.5 93.3 %collective-permute-start.16 = (bf16[8,128,1024]{2,1,0:T(8,128)(2,1)S(1)}, bf16[8,128,1024]{2,1,0:T(8,128)(2,1)}, u32[]{:S(2)}, u32[]{:S(2)}) collective-permute-start(bf16[8,128,1024]{2,1,0:T(8,128)(2,1)S(1)} %pad_maximum_fusion.1.refs_4_.refs_2_.refs_6_.refs_7_), channel_id=1, source_target_pairs={{0,8},{1,9},{2,10},{3,11},{4,12},{5,13},{6,14},{7,15},{8,0},{9,1},... | collective-permute-start | bytes 6291464 | tf_op jit(solution)/shard_map/ppermute | solution.py:123
  139.5 93.9 %collective-permute-start.17 = (bf16[8,128,1024]{2,1,0:T(8,128)(2,1)}, bf16[8,128,1024]{2,1,0:T(8,128)(2,1)}, u32[]{:S(2)}, u32[]{:S(2)}) collective-permute-start(bf16[8,128,1024]{2,1,0:T(8,128)(2,1)} %pad_maximum_fusion.2.refs_5_.refs_3_.refs_7_.refs_8_), channel_id=1, source_target_pairs={{0,16},{1,17},{2,18},{3,19},{4,20},{5,21},{6,22},{7,23},{8,24},{9,... | collective-permute-start | bytes 6291464 | tf_op jit(solution)/shard_map/ppermute | solution.py:123
  448.6 46.4 %collective-permute-start.36 = (bf16[7,512,1024]{2,1,0:T(8,128)(2,1)}, bf16[7,512,1024]{2,1,0:T(8,128)(2,1)}, u32[]{:S(2)}, u32[]{:S(2)}) collective-permute-start(bf16[7,512,1024]{2,1,0:T(8,128)(2,1)} %get-tuple-element.234), channel_id=1, source_target_pairs={{0,1},{1,0},{2,3},{3,2},{4,5},{5,4},{6,7},{7,6},{8,9},{9,8},{10,11... | collective-permute-start | bytes 22020104 | tf_op jit(solution)/shard_map/ppermute | solution.py:123
  512.8 96.3 %collective-permute-start.40 = (bf16[16,128,1024]{2,1,0:T(8,128)(2,1)S(1)}, bf16[16,128,1024]{2,1,0:T(8,128)(2,1)S(1)}, u32[]{:S(2)}, u32[]{:S(2)}) collective-permute-start(bf16[16,128,1024]{2,1,0:T(8,128)(2,1)S(1)} %get-tuple-element.251), channel_id=1, source_target_pairs={{0,4},{1,5},{2,6},{3,7},{4,0},{5,1},{6,2},{7,3},{8,12},{9,13},{10,... | collective-permute-start | bytes 12582920 | tf_op jit(solution)/shard_map/ppermute | solution.py:123
  514.3 94.7 %collective-permute-start.41 = (bf16[16,128,1024]{2,1,0:T(8,128)(2,1)}, bf16[16,128,1024]{2,1,0:T(8,128)(2,1)S(1)}, u32[]{:S(2)}, u32[]{:S(2)}) collective-permute-start(bf16[16,128,1024]{2,1,0:T(8,128)(2,1)} %get-tuple-element.252), channel_id=1, source_target_pairs={{0,2},{1,3},{2,0},{3,1},{4,6},{5,7},{6,4},{7,5},{8,10},{9,11},{10,... | collective-permute-start | bytes 12582920 | tf_op jit(solution)/shard_map/ppermute | solution.py:123
  514.8 94.2 %collective-permute-start.42 = (bf16[8,128,1024]{2,1,0:T(8,128)(2,1)S(1)}, bf16[8,128,1024]{2,1,0:T(8,128)(2,1)S(1)}, u32[]{:S(2)}, u32[]{:S(2)}) collective-permute-start(bf16[8,128,1024]{2,1,0:T(8,128)(2,1)S(1)} %get-tuple-element.253), channel_id=1, source_target_pairs={{0,8},{1,9},{2,10},{3,11},{4,12},{5,13},{6,14},{7,15},{8,0},{9,1},... | collective-permute-start | bytes 6291464 | tf_op jit(solution)/shard_map/ppermute | solution.py:123
  514.9 94.1 %collective-permute-start.43 = (bf16[8,128,1024]{2,1,0:T(8,128)(2,1)S(1)}, bf16[8,128,1024]{2,1,0:T(8,128)(2,1)S(1)}, u32[]{:S(2)}, u32[]{:S(2)}) collective-permute-start(bf16[8,128,1024]{2,1,0:T(8,128)(2,1)S(1)} %get-tuple-element.254), channel_id=1, source_target_pairs={{0,16},{1,17},{2,18},{3,19},{4,20},{5,21},{6,22},{7,23},{8,24},{9,... | collective-permute-start | bytes 6291464 | tf_op jit(solution)/shard_map/ppermute | solution.py:123
  516.9 92.1 %collective-permute-start.44 = (f32[17,1024]{1,0:T(8,128)S(1)}, f32[17,1024]{1,0:T(8,128)S(1)}, u32[]{:S(2)}, u32[]{:S(2)}) collective-permute-start(f32[17,1024]{1,0:T(8,128)S(1)} %add.681), channel_id=1, source_target_pairs={{0,2},{1,3},{2,0},{3,1},{4,6},{5,7},{6,4},{7,5},{8,10},{9,11},{10,... | collective-permute-start | bytes 208904 | tf_op jit(solution)/shard_map/ppermute | solution.py:123
  618.8 48.8 %collective-permute-start.45 = (bf16[8,128,1024]{2,1,0:T(8,128)(2,1)S(1)}, bf16[8,128,1024]{2,1,0:T(8,128)(2,1)S(1)}, u32[]{:S(2)}, u32[]{:S(2)}) collective-permute-start(bf16[8,128,1024]{2,1,0:T(8,128)(2,1)S(1)} %pad_maximum_fusion.3), channel_id=1, source_target_pairs={{0,4},{1,5},{2,6},{3,7},{4,0},{5,1},{6,2},{7,3},{8,12},{9,13},{10,... | collective-permute-start | bytes 6291464 | tf_op jit(solution)/shard_map/ppermute | solution.py:123
  619.4 48.2 %collective-permute-start.46 = (bf16[8,128,1024]{2,1,0:T(8,128)(2,1)S(1)}, bf16[8,128,1024]{2,1,0:T(8,128)(2,1)S(1)}, u32[]{:S(2)}, u32[]{:S(2)}) collective-permute-start(bf16[8,128,1024]{2,1,0:T(8,128)(2,1)S(1)} %pad_maximum_fusion.4), channel_id=1, source_target_pairs={{0,2},{1,3},{2,0},{3,1},{4,6},{5,7},{6,4},{7,5},{8,10},{9,11},{10,... | collective-permute-start | bytes 6291464 | tf_op jit(solution)/shard_map/ppermute | solution.py:123
  619.9 47.6 %collective-permute-start.47 = (bf16[4,128,1024]{2,1,0:T(8,128)(2,1)S(1)}, bf16[4,128,1024]{2,1,0:T(8,128)(2,1)S(1)}, u32[]{:S(2)}, u32[]{:S(2)}) collective-permute-start(bf16[4,128,1024]{2,1,0:T(8,128)(2,1)S(1)} %slice.564), channel_id=1, source_target_pairs={{0,8},{1,9},{2,10},{3,11},{4,12},{5,13},{6,14},{7,15},{8,0},{9,1},... | collective-permute-start | bytes 3145736 | tf_op jit(solution)/shard_map/ppermute | solution.py:123
  620.0 47.5 %collective-permute-start.48 = (bf16[4,128,1024]{2,1,0:T(8,128)(2,1)S(1)}, bf16[4,128,1024]{2,1,0:T(8,128)(2,1)S(1)}, u32[]{:S(2)}, u32[]{:S(2)}) collective-permute-start(bf16[4,128,1024]{2,1,0:T(8,128)(2,1)S(1)} %slice.565), channel_id=1, source_target_pairs={{0,16},{1,17},{2,18},{3,19},{4,20},{5,21},{6,22},{7,23},{8,24},{9,... | collective-permute-start | bytes 3145736 | tf_op jit(solution)/shard_map/ppermute | solution.py:123
  622.0 45.5 %collective-permute-start.49 = (f32[17,1024]{1,0:T(8,128)S(1)}, f32[17,1024]{1,0:T(8,128)S(1)}, u32[]{:S(2)}, u32[]{:S(2)}) collective-permute-start(f32[17,1024]{1,0:T(8,128)S(1)} %add.682), channel_id=1, source_target_pairs={{0,4},{1,5},{2,6},{3,7},{4,0},{5,1},{6,2},{7,3},{8,12},{9,13},{10,... | collective-permute-start | bytes 208904 | tf_op jit(solution)/shard_map/ppermute | solution.py:123
  709.3 40.8 %collective-permute-start.55 = (bf16[3,128,1024]{2,1,0:T(8,128)(2,1)S(1)}, bf16[3,128,1024]{2,1,0:T(8,128)(2,1)S(1)}, u32[]{:S(2)}, u32[]{:S(2)}) collective-permute-start(bf16[3,128,1024]{2,1,0:T(8,128)(2,1)S(1)} %pad_maximum_fusion.13), channel_id=1, source_target_pairs={{0,8},{1,9},{2,10},{3,11},{4,12},{5,13},{6,14},{7,15},{8,0},{9,1},... | collective-permute-start | bytes 2359304 | tf_op jit(solution)/shard_map/ppermute | solution.py:123
  709.7 40.4 %collective-permute-start.56 = (bf16[3,128,1024]{2,1,0:T(8,128)(2,1)S(1)}, bf16[3,128,1024]{2,1,0:T(8,128)(2,1)S(1)}, u32[]{:S(2)}, u32[]{:S(2)}) collective-permute-start(bf16[3,128,1024]{2,1,0:T(8,128)(2,1)S(1)} %pad_maximum_fusion.14), channel_id=1, source_target_pairs={{0,16},{1,17},{2,18},{3,19},{4,20},{5,21},{6,22},{7,23},{8,24},{9,... | collective-permute-start | bytes 2359304 | tf_op jit(solution)/shard_map/ppermute | solution.py:123
  (151 other events, 2452.3 us)

commit v4 on v3

--- a/solution.py
+++ b/solution.py
@@ -316,9 +316,41 @@
     return buffers[m][at]
 
 
-def ffn_kernel(firsts, count, place_ref, normed_ref, base_ref, *refs):
+def tail_next(out_ref, ins, outs):
+    gain_ref, bias_ref = ins
+    next_ref, stats_ref = outs
+    lanes = stats_ref.shape[1] // 2
+    for r in range(4):
+        rows = pl.ds(r * (out_ref.shape[0] // 4), out_ref.shape[0] // 4)
+        stream = out_ref[rows, :]
+        mean, inv = norm_stats(stream)
+        next_ref[rows, :] = norm_apply(
+            stream, (mean, inv), gain_ref[...], bias_ref[...]
+        ).astype(bf16)
+        stats_ref[rows, :lanes] = jnp.broadcast_to(mean, (stream.shape[0], lanes))
+        stats_ref[rows, lanes:] = jnp.broadcast_to(inv, (stream.shape[0], lanes))
+
+
+def tail_last(out_ref, ins, outs):
+    gain_ref, bias_ref, up_ref = ins
+    result_ref, grad_ref, half_ref, sums_ref = outs
+    for r in range(4):
+        rows = pl.ds(r * (out_ref.shape[0] // 4), out_ref.shape[0] // 4)
+        stream, upstream = out_ref[rows, :], up_ref[rows, :].astype(f32)
+        stats = norm_stats(stream)
+        result_ref[rows, :] = norm_apply(stream, stats, gain_ref[...], bias_ref[...]).astype(bf16)
+        back, grad_gain, grad_bias = norm_backward(stream, stats, gain_ref[...], upstream)
+        grad_ref[rows, :] = back
+        half_ref[rows, :] = (0.5 * back).astype(bf16)
+        sums = jnp.concatenate([grad_gain[None], grad_bias[None]])
+        sums_ref[...] = sums if r == 0 else sums_ref[...] + sums
+
+
+def ffn_kernel(firsts, count, tail, tail_ins, place_ref, normed_ref, base_ref, *refs):
+    ins, refs = refs[:tail_ins], refs[tail_ins:]
     sources = sixteen(refs)
-    out_ref, act_ref, slope_ref, in_buf, out_buf, sems = refs[SOURCES:]
+    out_ref, act_ref, slope_ref = refs[SOURCES : SOURCES + 3]
+    outs, (in_buf, out_buf, sems) = refs[SOURCES + 3 : -3], refs[-3:]
     buffers = (in_buf, out_buf)
     size = in_buf.shape[1]
     items = [(core, q) for core in range(2) for q in range(STEPS)]
@@ -335,6 +367,7 @@
         out_ref[...] = before + 0.5 * dot_plain(active, arrived(1, i % 2, buffers, sems))
         if i + 2 < len(items):
             fetch_rows(i % 2, items[i + 2], firsts, count, place_ref, sources, buffers, sems)
+    tail(out_ref, ins, outs)
 
 
 def ffn_back_kernel(cores, based, firsts, count, place_ref, e_ref, act_ref, slope_ref, normed_ref, *refs):
@@ -422,22 +455,35 @@
     ]
 
 
-def ffn_forward_here(stream, gain, bias, firsts, count, place, sources):
+LANES = 128
+
+
+def ffn_forward_here(stream, gain, bias, firsts, count, place, sources, tail, tail_ins):
     rows, width = stream.shape
     block = sources[0].shape[1]
     hidden = 8 * count * block
     shape = jax.ShapeDtypeStruct
     stats = norm_stats(stream)
     normed = norm_apply(stream, stats, gain, bias).astype(bf16)
-    result, active, slope = pl.pallas_call(
-        lambda *refs: ffn_kernel(firsts, count, *refs),
-        in_specs=[IN_SMEM] + [IN_VMEM] * 2 + [ANYWHERE] * SOURCES,
-        out_specs=[IN_VMEM] * 3,
+    if tail is tail_next:
+        more = [shape((rows, width), bf16), shape((rows, 2 * LANES), f32)]
+    else:
+        more = [
+            shape((rows, width), bf16),
+            shape((rows, width), f32),
+            shape((rows, width), bf16),
+            shape((2, width), f32),
+        ]
+    result, active, slope, *more = pl.pallas_call(
+        lambda *refs: ffn_kernel(firsts, count, tail, len(tail_ins), *refs),
+        in_specs=[IN_SMEM] + [IN_VMEM] * (2 + len(tail_ins)) + [ANYWHERE] * SOURCES,
+        out_specs=[IN_VMEM] * (3 + len(more)),
         out_shape=[
             shape((rows, width), f32),
             shape((rows, hidden), bf16),
             shape((rows, hidden), bf16),
-        ],
+        ]
+        + more,
         scratch_shapes=ffn_scratch(count, block, width),
         compiler_params=pltpu.CompilerParams(vmem_limit_bytes=FORWARD_MB * 1024 * 1024),
         cost_estimate=pl.CostEstimate(
@@ -445,22 +491,23 @@
             bytes_accessed=4 * hidden * (width + rows),
             transcendentals=rows * hidden,
         ),
-    )(place, normed, stream, *sources)
-    return (result, (stats, normed, active, slope))
-
-
-FORWARD_MB = 40
-BACKWARD_MB = 48
-
-
-def ffn_backward_here(upstream, stream, gain, kept, firsts, count, place, sources, calls):
+    )(place, normed, stream, *tail_ins, *sources)
+    return (result, (stats, normed, active, slope), more)
+
+
+FORWARD_MB = 36
+BACKWARD_MB = 40
+
+
+def ffn_backward_here(
+    upstream, incoming, stream, gain, kept, firsts, count, place, sources, calls
+):
     stats, normed, active, slope = kept
     rows, width = stream.shape
     block = sources[0].shape[1]
     half = 4 * count * block
     size = BPS * count * block
     shape = jax.ShapeDtypeStruct
-    incoming = (0.5 * upstream).astype(bf16)
     base, grads = [], []
     for cores in calls:
         dx, *some = pl.pallas_call(
@@ -540,6 +587,57 @@
     staged(len(items), SCATTER, load, drain_in, store, drain_out)
 
 
+def combine_kernel(plan, count, *refs):
+    keeps, gots, outs = refs[:count], refs[count : 2 * count], refs[2 * count :]
+    rows = 16
+
+    def body(r, carry):
+        cut = pl.ds(pl.multiple_of(r * rows, rows), rows)
+        for out, at, array, index in plan:
+            total = keeps[array][index, cut, :].astype(f32) + gots[array][index, cut, :].astype(f32)
+            outs[out][at, cut, :] = total.astype(bf16)
+        return carry
+
+    lax.fori_loop(0, keeps[0].shape[1] // rows, body, 0)
+
+
+def combine(step, keep, got):
+    before, now = step_groups(step + 1, ORDERS), step_groups(step, ORDERS)
+    size = 1 << step
+    lies = {
+        p: (a, 2 * i * size)
+        for a, parts in enumerate(before.values())
+        for i, p in enumerate(parts)
+    }
+    plan, shapes = [], []
+    for half in (1, 0):
+        for parts in now.values():
+            for i, p in enumerate(parts):
+                array, first = lies[p]
+                plan += [
+                    (len(shapes), i * size + k, array, first + half * size + k)
+                    for k in range(size)
+                ]
+            some = next(iter(keep.values()))
+            shapes.append(jax.ShapeDtypeStruct((size * len(parts),) + some.shape[1:], bf16))
+    blocks = sum(s.shape[0] for s in shapes)
+    outs = pl.pallas_call(
+        lambda *refs: combine_kernel(plan, len(before), *refs),
+        in_specs=[IN_VMEM] * (2 * len(before)),
+        out_specs=[IN_VMEM] * len(shapes),
+        out_shape=shapes,
+        compiler_params=pltpu.CompilerParams(
+            vmem_limit_bytes=(3 * blocks * 2 * some.shape[1] * some.shape[2]) + (4 << 20)
+        ),
+        cost_estimate=pl.CostEstimate(
+            flops=blocks * some.shape[1] * some.shape[2],
+            bytes_accessed=6 * blocks * some.shape[1] * some.shape[2],
+            transcendentals=0,
+        ),
+    )(*[keep[n] for n in before], *[got[n] for n in before])
+    return dict(zip(now, outs[: len(now)])), dict(zip(now, outs[len(now) :]))
+
+
 def reduce_tiles_here(groups, owns, others, place, slots, small, ahead):
     rows, width = owns[0].shape[2:]
     shapes = [jax.ShapeDtypeStruct((8 * len(parts), rows, width), bf16) for _, parts in LAST]
@@ -562,26 +660,31 @@
     arrays, ahead = lax.optimization_barrier((arrays, ahead))
     keep = {n: a for (n, _), a in zip(LAST, arrays[:4])}
     send = {n: a for (n, _), a in zip(LAST, arrays[4:])}
-    state = [None] * 6
     for step in range(3, -1, -1):
-        groups = step_groups(step, ORDERS)
-        if step < 3:
-            send, keep = {}, {}
+        if step == 2:
             size = 1 << step
-            for name, parts in groups.items():
-                send[name] = jnp.concatenate([state[p][size:] for p in parts]).astype(bf16)
-                keep[name] = jnp.concatenate([state[p][:size] for p in parts]).astype(bf16)
+            state = {}
+            for name, parts in step_groups(step + 1, ORDERS).items():
+                for i, p in enumerate(parts):
+                    cut = slice(2 * i * size, 2 * (i + 1) * size)
+                    state[p] = keep[name][cut].astype(f32) + got[name][cut].astype(f32)
+            halves = []
+            for cut in (slice(size, None), slice(0, size)):
+                halves.append(
+                    {
+                        name: jnp.concatenate([state[p][cut] for p in parts]).astype(bf16)
+                        for name, parts in step_groups(step, ORDERS).items()
+                    }
+                )
+            send, keep = halves
+        elif step < 2:
+            send, keep = combine(step, keep, got)
         send, small = lax.optimization_barrier((send, small))
         got = {name: swap(value, name) for name, value in send.items()}
         small = small + swap(small, ("z2", "z1", "x", "y")[step])
         got, small = lax.optimization_barrier((got, small))
-        if step == 0:
-            return [keep[n] for n in groups], [got[n] for n in groups], small, ahead
-        size = 1 << step
-        for name, parts in groups.items():
-            for i, p in enumerate(parts):
-                cut = slice(i * size, (i + 1) * size)
-                state[p] = keep[name][cut].astype(f32) + got[name][cut].astype(f32)
+    order = step_groups(0, ORDERS)
+    return [keep[n] for n in order], [got[n] for n in order], small, ahead
 
 
 def update_kernel(filled_ref, k0, g0, k1, g1, w_ref, m_ref, v_ref, m_new, v_new, w_new, b_new):
@@ -668,38 +771,47 @@
 
 
 def masked_probs(query, key, valid):
-    scores = dot_rows(query, key)
-    column = lax.broadcasted_iota(jnp.int32, scores.shape, 1)
-    scores = jnp.where(column < valid, scores * HEAD_DIM ** (-0.5), masked_score)
+    scores = dot_rows(query, key) * HEAD_DIM ** (-0.5)
+    column = lax.broadcasted_iota(jnp.int32, (1, scores.shape[1]), 1)
+    scores = jnp.where(column < valid, scores, masked_score)
     exponent = jnp.exp(scores - jnp.max(scores, axis=-1, keepdims=True))
-    return exponent * (1.0 / jnp.sum(exponent, axis=-1, keepdims=True))
+    return exponent, 1.0 / jnp.sum(exponent, axis=-1, keepdims=True)
+
+
+TOGETHER = 4
 
 
 def attend_kernel(valid_ref, q_ref, k_ref, v_ref, out_ref):
-    probs = masked_probs(q_ref[...], k_ref[...], valid_ref[0]).astype(bf16)
-    out_ref[...] = dot_plain(probs, v_ref[...]).astype(bf16)
+    for i in range(TOGETHER):
+        cut = slice(i * HEAD_DIM, (i + 1) * HEAD_DIM)
+        exponent, inverse = masked_probs(q_ref[:, cut], k_ref[:, cut], valid_ref[0])
+        probs = (exponent * inverse).astype(bf16)
+        out_ref[:, cut] = dot_plain(probs, v_ref[:, cut]).astype(bf16)
 
 
 def attend_back_kernel(valid_ref, q_ref, k_ref, v_ref, g_ref, dq_ref, dk_ref, dv_ref):
-    query, key, grad = q_ref[...], k_ref[...], g_ref[...]
-    probs = masked_probs(query, key, valid_ref[0])
-    grad_probs = dot_rows(grad, v_ref[...])
-    row_dot = jnp.sum(probs * grad_probs, axis=-1, keepdims=True)
-    grad_scores = (probs * (grad_probs - row_dot)).astype(bf16)
     scale = HEAD_DIM ** (-0.5)
-    dq_ref[...] = (dot_plain(grad_scores, key) * scale).astype(bf16)
-    dk_ref[...] = (dot_cols(grad_scores, query) * scale).astype(bf16)
-    dv_ref[...] = dot_cols(probs.astype(bf16), grad).astype(bf16)
+    for i in range(TOGETHER):
+        cut = slice(i * HEAD_DIM, (i + 1) * HEAD_DIM)
+        query, key, grad = q_ref[:, cut], k_ref[:, cut], g_ref[:, cut]
+        exponent, inverse = masked_probs(query, key, valid_ref[0])
+        probs = exponent * inverse
+        grad_probs = dot_rows(grad, v_ref[:, cut])
+        row_dot = jnp.sum(probs * grad_probs, axis=-1, keepdims=True)
+        grad_scores = (probs * (grad_probs - row_dot)).astype(bf16)
+        dq_ref[:, cut] = (dot_plain(grad_scores, key) * scale).astype(bf16)
+        dk_ref[:, cut] = (dot_cols(grad_scores, query) * scale).astype(bf16)
+        dv_ref[:, cut] = dot_cols(probs.astype(bf16), grad).astype(bf16)
 
 
 def head_call(kernel, valid, operands, out_count, flops):
     rows, width = operands[0].shape
-    spec = pl.BlockSpec((rows, HEAD_DIM), lambda h: (0, h))
+    spec = pl.BlockSpec((rows, TOGETHER * HEAD_DIM), lambda h: (0, h))
     shape = jax.ShapeDtypeStruct((rows, width), bf16)
     return pl.pallas_call(
         kernel,
-        grid=(width // HEAD_DIM,),
-        in_specs=[pl.BlockSpec(memory_space=pltpu.SMEM)] + [spec] * len(operands),
+        grid=(width // HEAD_DIM // TOGETHER,),
+        in_specs=[IN_SMEM] + [spec] * len(operands),
         out_specs=[spec] * out_count,
         out_shape=[shape] * out_count,
         cost_estimate=pl.CostEstimate(
@@ -707,7 +819,7 @@
             bytes_accessed=2 * rows * width * (len(operands) + out_count),
             transcendentals=rows * rows * width // HEAD_DIM,
         ),
-        compiler_params=pltpu.CompilerParams(vmem_limit_bytes=48 * 1024 * 1024),
+        compiler_params=pltpu.CompilerParams(vmem_limit_bytes=32 * 1024 * 1024),
     )(valid, *operands)
 
 
@@ -789,7 +901,7 @@
         ]
         sources, moved, convs = gather_sources(master, extra, conv_params)
         place = slot_places(tile_slot, slots)
-        mats = [None] * 4 + assemble(place, sources, base, tile_count - base)
+        mats = [None] * tile_count
         for mask in range(1, chan_count):
             mine = lax.dynamic_update_slice_in_dim(mine, moved[mask - 1], chan_index ^ mask, 0)
         near = jnp.array([0, 2, 1, 3], jnp.int32)
@@ -800,24 +912,15 @@
         convs = gather_small(conv_params, "chan")
         position = jnp.arange(chan_count, dtype=jnp.int32)
     source = mine[:, 0].reshape(rows, width).astype(f32)
-    upstream = mine[:, 1].reshape(rows, width).astype(f32)
+    cotangent_rows = mine[:, 1].reshape(rows, width)
     convs = jnp.moveaxis(convs, 0, 1).reshape(-1, width)
     valid = lax.dynamic_slice_in_dim(lengths[:, 0], chan_index, 1)
     in_first, out_first, in_second, out_second = mats[:4]
-    w_query, w_key, w_value, w_output, p_value, p_gate, p_output = mats[4:]
     gains, biases = norm_params[:5], norm_params[5:]
     taps = convs.shape[0] - 2
     margin = (taps - 1) // 2
     bn_gain, bn_bias = convs[taps], convs[taps + 1]
     frame_mask = (jnp.arange(rows, dtype=jnp.int32) < valid[0]).astype(f32)[:, None]
-
-    def forward(stream, norm, first, w_in, w_out):
-        if local:
-            firsts = (first, first + quarter)
-            return ffn_forward_here(
-                stream, gains[norm], biases[norm], firsts, quarter, place, sources
-            )
-        return ffn_forward(stream, gains[norm], biases[norm], w_in, w_out)
 
     def send_home(value):
         value = value.astype(bf16).reshape(chan_count, seg_rows, width)
@@ -826,18 +929,26 @@
         here, there = swap_in_hops(value)
         return (here, exchange(there, "chan", 2))
 
-    def backward(upstream, stream, norm, kept, first, w_in, w_out, calls):
-        if local:
-            firsts = (first, first + quarter)
-            return ffn_backward_here(
-                upstream, stream, gains[norm], kept, firsts, quarter, place, sources, calls
-            )
-        return ffn_backward(upstream, stream, gains[norm], kept, w_in, w_out)
-
-    stream_one, kept_one = forward(source, 0, 0, in_first, out_first)
-
-    stats_att = norm_stats(stream_one)
-    att_in = norm_apply(stream_one, stats_att, gains[1], biases[1]).astype(bf16)
+    if local:
+        stream_one, kept_one, (att_in, stats_att) = ffn_forward_here(
+            source,
+            gains[0],
+            biases[0],
+            (0, quarter),
+            quarter,
+            place,
+            sources,
+            tail_next,
+            (gains[1:2], biases[1:2]),
+        )
+        stats_att = (stats_att[:, :1], stats_att[:, LANES : LANES + 1])
+        stream_one, place_after = lax.optimization_barrier((stream_one, place))
+        mats[4:] = assemble(place_after, sources, base, tile_count - base)
+    else:
+        stream_one, kept_one = ffn_forward(source, gains[0], biases[0], in_first, out_first)
+        stats_att = norm_stats(stream_one)
+        att_in = norm_apply(stream_one, stats_att, gains[1], biases[1]).astype(bf16)
+    w_query, w_key, w_value, w_output, p_value, p_gate, p_output = mats[4:]
     queries = dot_rows(att_in, w_query).astype(bf16)
     keys = dot_rows(att_in, w_key).astype(bf16)
     values = dot_rows(att_in, w_value).astype(bf16)
@@ -870,14 +981,43 @@
     conv_act = (normal * conv_sig).astype(bf16)
     stream_three = stream_two + dot_plain(conv_act, p_output)
 
-    stream_four, kept_four = forward(stream_three, 3, 2 * quarter, in_second, out_second)
-    stats_last = norm_stats(stream_four)
-    result = norm_apply(stream_four, stats_last, gains[4], biases[4]).astype(bf16)
-
-    grad_four, gain_four, bias_four = norm_backward(stream_four, stats_last, gains[4], upstream)
-    grad_three, gin_second, gout_second, gain_three, bias_three = backward(
-        grad_four, stream_three, 3, kept_four, 2 * quarter, in_second, out_second, ((1, 0),)
-    )
+    if local:
+        _, kept_four, (result, grad_four, half_four, sums_four) = ffn_forward_here(
+            stream_three,
+            gains[3],
+            biases[3],
+            (2 * quarter, 3 * quarter),
+            quarter,
+            place,
+            sources,
+            tail_last,
+            (gains[4:5], biases[4:5], cotangent_rows),
+        )
+        gain_four, bias_four = sums_four[0], sums_four[1]
+        grad_three, gin_second, gout_second, gain_three, bias_three = ffn_backward_here(
+            grad_four,
+            half_four,
+            stream_three,
+            gains[3],
+            kept_four,
+            (2 * quarter, 3 * quarter),
+            quarter,
+            place,
+            sources,
+            ((1, 0),),
+        )
+    else:
+        stream_four, kept_four = ffn_forward(
+            stream_three, gains[3], biases[3], in_second, out_second
+        )
+        stats_last = norm_stats(stream_four)
+        result = norm_apply(stream_four, stats_last, gains[4], biases[4]).astype(bf16)
+        grad_four, gain_four, bias_four = norm_backward(
+            stream_four, stats_last, gains[4], cotangent_rows.astype(f32)
+        )
+        grad_three, gin_second, gout_second, gain_three, bias_three = ffn_backward(
+            grad_four, stream_three, gains[3], kept_four, in_second, out_second
+        )
 
     incoming = grad_three.astype(bf16)
     incoming_three = incoming
@@ -947,9 +1087,23 @@
         grad_one, singles_other = lax.optimization_barrier((grad_one, singles_other))
         singles_other = swap(singles_other, "core")
 
-    grad_zero, gin_first, gout_first, gain_zero, bias_zero = backward(
-        grad_one, source, 0, kept_one, 0, in_first, out_first, ((1,), (0,))
-    )
+    if local:
+        grad_zero, gin_first, gout_first, gain_zero, bias_zero = ffn_backward_here(
+            grad_one,
+            (0.5 * grad_one).astype(bf16),
+            source,
+            gains[0],
+            kept_one,
+            (0, quarter),
+            quarter,
+            place,
+            sources,
+            ((1,), (0,)),
+        )
+    else:
+        grad_zero, gin_first, gout_first, gain_zero, bias_zero = ffn_backward(
+            grad_one, source, gains[0], kept_one, in_first, out_first
+        )
     block_grad = send_home(grad_zero)
 
     conv_small = jnp.stack(tap_grads + [own_sums[1] * inv_std, own_sums[0]])

time: 766 us -> 750 us (0.979)
  other arithmetic: 70.6 us -> 52 us
  Pallas kernels: 160 us -> 171 us
  local copies, waits for them, and re-layouts: 39.7 us -> 30.1 us
    pallas_call x1, Pallas kernels: 6.18 us -> 18.1 us  [assemble(): pl.pallas_call(lambda *refs: assemble_kernel(first, *refs), in_specs=[IN_...]
    unnamed x243 -> x203, local copies, waits for them, and re-layouts: 26.4 us -> 17.1 us
    another operation x13 -> x5, other arithmetic: 16.8 us -> 8.29 us
    pallas_call x4 -> x6, Pallas kernels: 56.9 us -> 54.9 us  [the longest x2 33.8 us: ffn_forward_here(): pl.pallas_call(lambda *refs: ffn_kernel(firsts, count, tail, len(tail_ins...]
  transfers between devices with their start and end apart: 58 -> 58, of which waited for: 27 -> 26; matrix products, arithmetic and copies ran while one was open for 4% -> 5% of each run, Pallas kernels for 7% -> 11%
where the time goes in v4:
time: 750 us; the launch traced here: 742 us
  waiting for transfers between devices  410 us (55%)
  Pallas kernels  171 us (23%)
  other arithmetic  52 us (7%)
  starting transfers between devices  49 us (7%)
  local copies, waits for them, and re-layouts  30.1 us (4%)
  matrix products  26.6 us (4%)
    ppermute x43, waiting for transfers between devices, swap(): return lax.ppermute(value, BOTH, [(i, i ^ BITS[name]) for i in range(size)])  348 us
    pallas_call x3, Pallas kernels, ffn_backward_here(): pl.pallas_call(lambda *refs, cores=cores: ffn_back_kernel(cores, bool(bas...  61.9 us
    ppermute x15, waiting for transfers between devices, exchange(): return lax.ppermute(value, axis, [(i, i ^ mask) for i in range(size)])  61.5 us
    ppermute x43, starting transfers between devices, swap(): return lax.ppermute(value, BOTH, [(i, i ^ BITS[name]) for i in range(size)])  39 us
    pallas_call x2, Pallas kernels, ffn_forward_here(): pl.pallas_call(lambda *refs: ffn_kernel(firsts, count, tail, len(tail_ins...  33.8 us
    pallas_call x1, Pallas kernels, reduce_tiles_here(): pl.pallas_call(lambda *refs: scatter_kernel(groups, *refs), in_specs=[IN_...  19.2 us
    pallas_call x1, Pallas kernels, assemble(): pl.pallas_call(lambda *refs: assemble_kernel(first, *refs), in_specs=[IN_...  18.1 us
    unnamed x203, local copies, waits for them, and re-layouts  17.1 us
  transfers between devices with their start and end apart: 58, of which 26 were waited for; matrix products, arithmetic and copies ran while one was open for 5% of the time, Pallas kernels for 11%

profile of v4, /device:TPU:0, one launch (start us, length us, event | category | flops | bytes accessed | tf_op | source)
XLA Modules:
  0.0 741.9 jit_solution(5665321848460106450)
XLA Ops:
  13.7 12.6 %collective-permute-done.3 = bf16[1,2,128,1024]{3,2,1,0:T(8,128)(2,1)S(1)} collective-permute-done((bf16[1,2,128,1024]{3,2,1,0:T(8,128)(2,1)S(1)}, bf16[1,2,128,1024]{3,2,1,0:T(8,128)(2,1)S(1)}, u32[]{:S(2)}, u32[]{:S(2)}) %collective-permute-start.3) | collective-permute-done | bytes 524320 | tf_op jit(solution)/shard_map/ppermute | solution.py:48
  26.3 10.5 %collective-permute-done.4 = bf16[1,2,128,1024]{3,2,1,0:T(8,128)(2,1)S(1)} collective-permute-done((bf16[1,2,128,1024]{3,2,1,0:T(8,128)(2,1)S(1)}, bf16[1,2,128,1024]{3,2,1,0:T(8,128)(2,1)S(1)}, u32[]{:S(2)}, u32[]{:S(2)}) %collective-permute-start.4) | collective-permute-done | bytes 524320 | tf_op jit(solution)/shard_map/ppermute | solution.py:48
  36.7 6.4 collective-permute-done
  54.4 15.0 %collective-permute-done.9 = f32[7,256]{1,0:T(8,128)S(1)} collective-permute-done((f32[7,256]{1,0:T(8,128)S(1)}, f32[7,256]{1,0:T(8,128)S(1)}, u32[]{:S(2)}, u32[]{:S(2)}) %collective-permute-start.9) | collective-permute-done | bytes 7200 | tf_op jit(solution)/shard_map/ppermute | solution.py:48
  81.6 38.0 %collective-permute-done.12 = bf16[4,128,1024]{2,1,0:T(8,128)(2,1)S(1)} collective-permute-done((bf16[4,128,1024]{2,1,0:T(8,128)(2,1)S(1)}, bf16[4,128,1024]{2,1,0:T(8,128)(2,1)S(1)}, u32[]{:S(2)}, u32[]{:S(2)}) %collective-permute-start.12) | collective-permute-done | bytes 1048608 | tf_op jit(solution)/shard_map/ppermute | solution.py:123
  126.0 10.3 %pad_maximum_fusion = bf16[48,128,1024]{2,1,0:T(8,128)(2,1)} fusion(bf16[16,128,1024]{2,1,0:T(8,128)(2,1)S(1)} %constant_dynamic-update-slice_fusion.21.refs_8_.refs_4_.refs_9_, bf16[8,128,1024]{2,1,0:T(8,128)(2,1)} %pad_maximum_fusion.2.refs_7_.refs_3_.refs_8_, bf16[8,128,1024]{2,1,0:T(8,128)(2,1)S(1)} %pad_maximum_fusion.1.refs_6_.refs_2_.refs_7_, ...), kind=kLoop, calls=%fused_computation.2 | loop fusion | flops 18874368 | bytes 25165824 | tf_op jit(solution)/shard_map/concatenate | solution.py:288
  139.7 89.6 %collective-permute-done.15.refs_9_.refs_5_.refs_10_ = bf16[16,128,1024]{2,1,0:T(8,128)(2,1)} collective-permute-done((bf16[16,128,1024]{2,1,0:T(8,128)(2,1)S(1)}, bf16[16,128,1024]{2,1,0:T(8,128)(2,1)}, u32[]{:S(2)}, u32[]{:S(2)}) %collective-permute-start.15) | collective-permute-done | bytes 4194336 | tf_op jit(solution)/shard_map/ppermute | solution.py:123
  241.4 4.4 collective-permute-done.21.refs_15_.refs_11_.refs_16_
  248.9 16.6 %shard_map.229 = (f32[512,1024]{1,0:T(8,128)S(1)}, bf16[512,4096]{1,0:T(8,128)(2,1)}, bf16[512,4096]{1,0:T(8,128)(2,1)}, bf16[512,1024]{1,0:T(8,128)(2,1)S(1)}, f32[512,256]{1,0:T(8,128)S(1)}) custom-call(s32[4,23]{1,0:T(4,128)S(1)} %pad_add_fusion.refs_0_, bf16[512,1024]{1,0:T(8,128)(2,1)S(1)} %add_convert_fusion.9.refs_1_.refs_4_, ...), custom_call_target="tpu_custom_call" | custom-call | flops 8589934592 | bytes 25165824 | tf_op jit(solution)/shard_map/pallas_call | solution.py:477
  265.5 18.1 %shard_map.230 = (bf16[2,4,128,1024]{3,2,1,0:T(8,128)(2,1)S(1)}, bf16[2,4,128,1024]{3,2,1,0:T(8,128)(2,1)S(1)}, bf16[2,4,128,1024]{3,2,1,0:T(8,128)(2,1)S(1)}, b...) custom-call(s32[4,23]{1,0:T(4,128)S(1)} %pad_add_fusion.refs_0_, ...), custom_call_target="tpu_custom_call" | custom-call | bytes 29360128 | tf_op jit(solution)/shard_map/pallas_call | solution.py:268
  289.9 5.1 shard_map.231.refs_3_
  316.4 4.3 collective-permute-done.26
  327.5 17.2 %shard_map.232 = (f32[512,1024]{1,0:T(8,128)}, bf16[512,4096]{1,0:T(8,128)(2,1)}, bf16[512,4096]{1,0:T(8,128)(2,1)}, bf16[512,1024]{1,0:T(8,128)(2,1)S(1)}, f32[...) custom-call(s32[4,23]{1,0:T(4,128)S(1)} %pad_add_fusion.refs_0_, ...), custom_call_target="tpu_custom_call" | custom-call | flops 8589934592 | bytes 25165824 | tf_op jit(solution)/shard_map/pallas_call | solution.py:477
  344.9 28.0 %shard_map.233 = (f32[512,1024]{1,0:T(8,128)S(1)}, bf16[2048,1024]{1,0:T(8,128)(2,1)}, bf16[2048,1024]{1,0:T(8,128)(2,1)}, bf16[2048,1024]{1,0:T(8,128)(2,1)}, bf16[2048,1024]{1,0:T(8,128)(2,1)}) custom-call(s32[4,23]{1,0:T(4,128)S(1)} %pad_add_fusion.refs_0_, bf16[512,1024]{1,0:T(8,128)(2,1)S(1)} %get-tuple-element.228.refs_1_, ...), custom_call_target="tpu_custom_call" | custom-call | flops 17179869184 | bytes 50331648 | tf_op jit(solution)/shard_map/pallas_call | solution.py:513
  412.4 10.6 %shard_map.234 = (bf16[512,1024]{1,0:T(8,128)(2,1)S(1)}, bf16[512,1024]{1,0:T(8,128)(2,1)S(1)}, bf16[512,1024]{1,0:T(8,128)(2,1)S(1)}) custom-call(s32[1]{0:T(128)} %bitcast.14.valid_ref, bf16[512,1024]{1,0:T(8,128)(2,1)S(1)} %copy-done.21, bf16[512,1024]{1,0:T(8,128)(2,1)S(1)} %copy-done.19, bf16[512,1024]{1,0:T(8,128)(2,1)S(1)} %copy-done.23, ...), custom_call_target="tpu_custom_call" | custom-call | flops 2684354560 | bytes 7340032 | tf_op jit(solution)/shard_map/pallas_call | solution.py:811
  427.1 10.5 %shard_map.235 = (bf16[7,512,1024]{2,1,0:T(8,128)(2,1)}, bf16[7,512,1024]{2,1,0:T(8,128)(2,1)}) custom-call(bf16[512,1024]{1,0:T(8,128)(2,1)S(1)} %get-tuple-element.241.refs_0_, bf16[512,1024]{1,0:T(8,128)(2,1)S(1)} %get-tuple-element.242.refs_1_, bf16[512,1024]{1,0:T(8,128)(2,1)S(1)} %get-tuple-element.243.refs_2_, bf16[512,1024]{1,0:T(8,128)(2,1)S(1)} %copy-done.17, ...), custom_call_target="tpu_custom_call" | custom-call | flops 7516192768 | bytes 29360128 | tf_op jit(solution)/shard_map/pallas_call | solution.py:435
  442.4 17.0 %shard_map.236 = (f32[512,1024]{1,0:T(8,128)S(1)}, bf16[2048,1024]{1,0:T(8,128)(2,1)}, bf16[2048,1024]{1,0:T(8,128)(2,1)}) custom-call(s32[4,23]{1,0:T(4,128)S(1)} %pad_add_fusion.refs_0_, bf16[512,1024]{1,0:T(8,128)(2,1)S(1)} %multiply_convert_fusion.refs_1_, bf16[512,4096]{1,0:T(8,128)(2,1)} %get-tuple-element.247.refs_2_, ...), custom_call_target="tpu_custom_call" | custom-call | flops 8589934592 | bytes 25165824 | tf_op jit(solution)/shard_map/pallas_call | solution.py:513
  460.0 17.0 %shard_map.237 = (f32[512,1024]{1,0:T(8,128)S(1)}, bf16[2048,1024]{1,0:T(8,128)(2,1)}, bf16[2048,1024]{1,0:T(8,128)(2,1)}) custom-call(s32[4,23]{1,0:T(4,128)S(1)} %pad_add_fusion.refs_0_, bf16[512,1024]{1,0:T(8,128)(2,1)S(1)} %multiply_convert_fusion.refs_1_, bf16[512,4096]{1,0:T(8,128)(2,1)} %get-tuple-element.247.refs_2_, ...), custom_call_target="tpu_custom_call" | custom-call | flops 8589934592 | bytes 25165824 | tf_op jit(solution)/shard_map/pallas_call | solution.py:513
  485.6 19.2 %shard_map.238 = (bf16[16,128,1024]{2,1,0:T(8,128)(2,1)S(1)}, bf16[8,128,1024]{2,1,0:T(8,128)(2,1)S(1)}, bf16[8,128,1024]{2,1,0:T(8,128)(2,1)S(1)}, bf16[16,128,...) custom-call(s32[4,23]{1,0:T(4,128)S(1)} %pad_add_fusion.refs_0_, ...), custom_call_target="tpu_custom_call" | custom-call | bytes 72351744 | tf_op jit(solution)/shard_map/pallas_call | solution.py:644
  508.6 91.9 %collective-permute-done.44 = f32[17,1024]{1,0:T(8,128)S(1)} collective-permute-done((f32[17,1024]{1,0:T(8,128)S(1)}, f32[17,1024]{1,0:T(8,128)S(1)}, u32[]{:S(2)}, u32[]{:S(2)}) %collective-permute-start.44) | collective-permute-done | bytes 69664 | tf_op jit(solution)/shard_map/ppermute | solution.py:123
  613.9 43.8 %collective-permute-done.49 = f32[17,1024]{1,0:T(8,128)S(1)} collective-permute-done((f32[17,1024]{1,0:T(8,128)S(1)}, f32[17,1024]{1,0:T(8,128)S(1)}, u32[]{:S(2)}, u32[]{:S(2)}) %collective-permute-start.49) | collective-permute-done | bytes 69664 | tf_op jit(solution)/shard_map/ppermute | solution.py:123
  667.3 21.3 %collective-permute-done.54 = f32[17,1024]{1,0:T(8,128)S(1)} collective-permute-done((f32[17,1024]{1,0:T(8,128)S(1)}, f32[17,1024]{1,0:T(8,128)S(1)}, u32[]{:S(2)}, u32[]{:S(2)}) %collective-permute-start.54) | collective-permute-done | bytes 69664 | tf_op jit(solution)/shard_map/ppermute | solution.py:123
  699.3 34.6 %collective-permute-done.57 = f32[17,1024]{1,0:T(8,128)S(1)} collective-permute-done((f32[17,1024]{1,0:T(8,128)S(1)}, f32[17,1024]{1,0:T(8,128)S(1)}, u32[]{:S(2)}, u32[]{:S(2)}) %collective-permute-start.57) | collective-permute-done | bytes 69664 | tf_op jit(solution)/shard_map/ppermute | solution.py:123
  735.3 6.2 shard_map.241
  (455 shorter events, 190.3 us)
Async XLA Ops:
  5.9 37.2 %collective-permute-start = (bf16[3,128,1024]{2,1,0:T(8,128)(2,1)S(1)}, bf16[3,128,1024]{2,1,0:T(8,128)(2,1)S(1)}, u32[]{:S(2)}, u32[]{:S(2)}) collective-permute-start(bf16[3,128,1024]{2,1,0:T(8,128)(2,1)S(1)} %get-tuple-element.175), channel_id=1, source_target_pairs={{0,8},{1,9},{2,10},{3,11},{4,12},{5,13},{6,14},{7,15},{8,0},{9,1},... | collective-permute-start | bytes 2359304 | tf_op jit(solution)/shard_map/ppermute | solution.py:123
  76.4 46.8 %collective-permute-start.10 = (bf16[8,128,1024]{2,1,0:T(8,128)(2,1)S(1)}, bf16[8,128,1024]{2,1,0:T(8,128)(2,1)S(1)}, u32[]{:S(2)}, u32[]{:S(2)}) collective-permute-start(bf16[8,128,1024]{2,1,0:T(8,128)(2,1)S(1)} %get-tuple-element.196), channel_id=1, source_target_pairs={{0,4},{1,5},{2,6},{3,7},{4,0},{5,1},{6,2},{7,3},{8,12},{9,13},{10,... | collective-permute-start | bytes 6291464 | tf_op jit(solution)/shard_map/ppermute | solution.py:123
  77.0 46.2 %collective-permute-start.11 = (bf16[8,128,1024]{2,1,0:T(8,128)(2,1)S(1)}, bf16[8,128,1024]{2,1,0:T(8,128)(2,1)S(1)}, u32[]{:S(2)}, u32[]{:S(2)}) collective-permute-start(bf16[8,128,1024]{2,1,0:T(8,128)(2,1)S(1)} %get-tuple-element.197), channel_id=1, source_target_pairs={{0,2},{1,3},{2,0},{3,1},{4,6},{5,7},{6,4},{7,5},{8,10},{9,11},{10,... | collective-permute-start | bytes 6291464 | tf_op jit(solution)/shard_map/ppermute | solution.py:123
  77.5 42.1 %collective-permute-start.12 = (bf16[4,128,1024]{2,1,0:T(8,128)(2,1)S(1)}, bf16[4,128,1024]{2,1,0:T(8,128)(2,1)S(1)}, u32[]{:S(2)}, u32[]{:S(2)}) collective-permute-start(bf16[4,128,1024]{2,1,0:T(8,128)(2,1)S(1)} %pad_maximum_fusion.10), channel_id=1, source_target_pairs={{0,8},{1,9},{2,10},{3,11},{4,12},{5,13},{6,14},{7,15},{8,0},{9,1},... | collective-permute-start | bytes 3145736 | tf_op jit(solution)/shard_map/ppermute | solution.py:123
  77.8 45.4 %collective-permute-start.13 = (bf16[4,128,1024]{2,1,0:T(8,128)(2,1)S(1)}, bf16[4,128,1024]{2,1,0:T(8,128)(2,1)S(1)}, u32[]{:S(2)}, u32[]{:S(2)}) collective-permute-start(bf16[4,128,1024]{2,1,0:T(8,128)(2,1)S(1)} %pad_maximum_fusion.11), channel_id=1, source_target_pairs={{0,16},{1,17},{2,18},{3,19},{4,20},{5,21},{6,22},{7,23},{8,24},{9,... | collective-permute-start | bytes 3145736 | tf_op jit(solution)/shard_map/ppermute | solution.py:123
  136.3 112.6 %collective-permute-start.19 = (bf16[48,128,1024]{2,1,0:T(8,128)(2,1)}, bf16[48,128,1024]{2,1,0:T(8,128)(2,1)}, u32[]{:S(2)}, u32[]{:S(2)}) collective-permute-start(bf16[48,128,1024]{2,1,0:T(8,128)(2,1)} %pad_maximum_fusion), channel_id=1, source_target_pairs={{0,1},{1,0},{2,3},{3,2},{4,5},{5,4},{6,7},{7,6},{8,9},{9,8},{10,11... | collective-permute-start | bytes 37748744 | tf_op jit(solution)/shard_map/ppermute | solution.py:123
  136.3 93.1 %collective-permute-start.15 = (bf16[16,128,1024]{2,1,0:T(8,128)(2,1)S(1)}, bf16[16,128,1024]{2,1,0:T(8,128)(2,1)}, u32[]{:S(2)}, u32[]{:S(2)}) collective-permute-start(bf16[16,128,1024]{2,1,0:T(8,128)(2,1)S(1)} %get-tuple-element.211.refs_5_.refs_1_.refs_6_), channel_id=1, source_target_pairs={{0,4},{1,5},{2,6},{3,7},{4,0},{5,1},{6,2},{7,3},{8,12},{9,13},{10,... | collective-permute-start | bytes 12582920 | tf_op jit(solution)/shard_map/ppermute | solution.py:123
  137.8 92.8 %collective-permute-start.18 = (bf16[16,128,1024]{2,1,0:T(8,128)(2,1)S(1)}, bf16[16,128,1024]{2,1,0:T(8,128)(2,1)}, u32[]{:S(2)}, u32[]{:S(2)}) collective-permute-start(bf16[16,128,1024]{2,1,0:T(8,128)(2,1)S(1)} %constant_dynamic-update-slice_fusion.21.refs_8_.refs_4_.refs_9_), channel_id=1, source_target_pairs={{0,2},{1,3},{2,0},{3,1},{4,6},{5,7},{6,4},{7,5},{8,10},{9,11},{10,... | collective-permute-start | bytes 12582920 | tf_op jit(solution)/shard_map/ppermute | solution.py:123
  139.3 93.3 %collective-permute-start.16 = (bf16[8,128,1024]{2,1,0:T(8,128)(2,1)S(1)}, bf16[8,128,1024]{2,1,0:T(8,128)(2,1)}, u32[]{:S(2)}, u32[]{:S(2)}) collective-permute-start(bf16[8,128,1024]{2,1,0:T(8,128)(2,1)S(1)} %pad_maximum_fusion.1.refs_6_.refs_2_.refs_7_), channel_id=1, source_target_pairs={{0,8},{1,9},{2,10},{3,11},{4,12},{5,13},{6,14},{7,15},{8,0},{9,1},... | collective-permute-start | bytes 6291464 | tf_op jit(solution)/shard_map/ppermute | solution.py:123
  139.3 93.9 %collective-permute-start.17 = (bf16[8,128,1024]{2,1,0:T(8,128)(2,1)}, bf16[8,128,1024]{2,1,0:T(8,128)(2,1)}, u32[]{:S(2)}, u32[]{:S(2)}) collective-permute-start(bf16[8,128,1024]{2,1,0:T(8,128)(2,1)} %pad_maximum_fusion.2.refs_7_.refs_3_.refs_8_), channel_id=1, source_target_pairs={{0,16},{1,17},{2,18},{3,19},{4,20},{5,21},{6,22},{7,23},{8,24},{9,... | collective-permute-start | bytes 6291464 | tf_op jit(solution)/shard_map/ppermute | solution.py:123
  442.0 43.6 %collective-permute-start.36 = (bf16[7,512,1024]{2,1,0:T(8,128)(2,1)}, bf16[7,512,1024]{2,1,0:T(8,128)(2,1)}, u32[]{:S(2)}, u32[]{:S(2)}) collective-permute-start(bf16[7,512,1024]{2,1,0:T(8,128)(2,1)} %get-tuple-element.259), channel_id=1, source_target_pairs={{0,1},{1,0},{2,3},{3,2},{4,5},{5,4},{6,7},{7,6},{8,9},{9,8},{10,11... | collective-permute-start | bytes 22020104 | tf_op jit(solution)/shard_map/ppermute | solution.py:123
  504.8 95.8 %collective-permute-start.40 = (bf16[16,128,1024]{2,1,0:T(8,128)(2,1)S(1)}, bf16[16,128,1024]{2,1,0:T(8,128)(2,1)S(1)}, u32[]{:S(2)}, u32[]{:S(2)}) collective-permute-start(bf16[16,128,1024]{2,1,0:T(8,128)(2,1)S(1)} %get-tuple-element.277), channel_id=1, source_target_pairs={{0,4},{1,5},{2,6},{3,7},{4,0},{5,1},{6,2},{7,3},{8,12},{9,13},{10,... | collective-permute-start | bytes 12582920 | tf_op jit(solution)/shard_map/ppermute | solution.py:123
  505.6 95.0 %collective-permute-start.41 = (bf16[16,128,1024]{2,1,0:T(8,128)(2,1)}, bf16[16,128,1024]{2,1,0:T(8,128)(2,1)S(1)}, u32[]{:S(2)}, u32[]{:S(2)}) collective-permute-start(bf16[16,128,1024]{2,1,0:T(8,128)(2,1)} %get-tuple-element.278), channel_id=1, source_target_pairs={{0,2},{1,3},{2,0},{3,1},{4,6},{5,7},{6,4},{7,5},{8,10},{9,11},{10,... | collective-permute-start | bytes 12582920 | tf_op jit(solution)/shard_map/ppermute | solution.py:123
  506.1 94.4 %collective-permute-start.42 = (bf16[8,128,1024]{2,1,0:T(8,128)(2,1)S(1)}, bf16[8,128,1024]{2,1,0:T(8,128)(2,1)S(1)}, u32[]{:S(2)}, u32[]{:S(2)}) collective-permute-start(bf16[8,128,1024]{2,1,0:T(8,128)(2,1)S(1)} %get-tuple-element.279), channel_id=1, source_target_pairs={{0,8},{1,9},{2,10},{3,11},{4,12},{5,13},{6,14},{7,15},{8,0},{9,1},... | collective-permute-start | bytes 6291464 | tf_op jit(solution)/shard_map/ppermute | solution.py:123
  506.2 94.4 %collective-permute-start.43 = (bf16[8,128,1024]{2,1,0:T(8,128)(2,1)S(1)}, bf16[8,128,1024]{2,1,0:T(8,128)(2,1)S(1)}, u32[]{:S(2)}, u32[]{:S(2)}) collective-permute-start(bf16[8,128,1024]{2,1,0:T(8,128)(2,1)S(1)} %get-tuple-element.280), channel_id=1, source_target_pairs={{0,16},{1,17},{2,18},{3,19},{4,20},{5,21},{6,22},{7,23},{8,24},{9,... | collective-permute-start | bytes 6291464 | tf_op jit(solution)/shard_map/ppermute | solution.py:123
  508.3 92.2 %collective-permute-start.44 = (f32[17,1024]{1,0:T(8,128)S(1)}, f32[17,1024]{1,0:T(8,128)S(1)}, u32[]{:S(2)}, u32[]{:S(2)}) collective-permute-start(f32[17,1024]{1,0:T(8,128)S(1)} %add.601), channel_id=1, source_target_pairs={{0,2},{1,3},{2,0},{3,1},{4,6},{5,7},{6,4},{7,5},{8,10},{9,11},{10,... | collective-permute-start | bytes 208904 | tf_op jit(solution)/shard_map/ppermute | solution.py:123
  608.7 49.1 %collective-permute-start.45 = (bf16[8,128,1024]{2,1,0:T(8,128)(2,1)S(1)}, bf16[8,128,1024]{2,1,0:T(8,128)(2,1)S(1)}, u32[]{:S(2)}, u32[]{:S(2)}) collective-permute-start(bf16[8,128,1024]{2,1,0:T(8,128)(2,1)S(1)} %pad_maximum_fusion.5), channel_id=1, source_target_pairs={{0,4},{1,5},{2,6},{3,7},{4,0},{5,1},{6,2},{7,3},{8,12},{9,13},{10,... | collective-permute-start | bytes 6291464 | tf_op jit(solution)/shard_map/ppermute | solution.py:123
  609.8 48.0 %collective-permute-start.46 = (bf16[8,128,1024]{2,1,0:T(8,128)(2,1)S(1)}, bf16[8,128,1024]{2,1,0:T(8,128)(2,1)S(1)}, u32[]{:S(2)}, u32[]{:S(2)}) collective-permute-start(bf16[8,128,1024]{2,1,0:T(8,128)(2,1)S(1)} %pad_maximum_fusion.6), channel_id=1, source_target_pairs={{0,2},{1,3},{2,0},{3,1},{4,6},{5,7},{6,4},{7,5},{8,10},{9,11},{10,... | collective-permute-start | bytes 6291464 | tf_op jit(solution)/shard_map/ppermute | solution.py:123
  610.3 47.4 %collective-permute-start.47 = (bf16[4,128,1024]{2,1,0:T(8,128)(2,1)S(1)}, bf16[4,128,1024]{2,1,0:T(8,128)(2,1)S(1)}, u32[]{:S(2)}, u32[]{:S(2)}) collective-permute-start(bf16[4,128,1024]{2,1,0:T(8,128)(2,1)S(1)} %get-tuple-element.292), channel_id=1, source_target_pairs={{0,8},{1,9},{2,10},{3,11},{4,12},{5,13},{6,14},{7,15},{8,0},{9,1},... | collective-permute-start | bytes 3145736 | tf_op jit(solution)/shard_map/ppermute | solution.py:123
  610.4 47.3 %collective-permute-start.48 = (bf16[4,128,1024]{2,1,0:T(8,128)(2,1)S(1)}, bf16[4,128,1024]{2,1,0:T(8,128)(2,1)S(1)}, u32[]{:S(2)}, u32[]{:S(2)}) collective-permute-start(bf16[4,128,1024]{2,1,0:T(8,128)(2,1)S(1)} %get-tuple-element.293), channel_id=1, source_target_pairs={{0,16},{1,17},{2,18},{3,19},{4,20},{5,21},{6,22},{7,23},{8,24},{9,... | collective-permute-start | bytes 3145736 | tf_op jit(solution)/shard_map/ppermute | solution.py:123
  612.5 45.2 %collective-permute-start.49 = (f32[17,1024]{1,0:T(8,128)S(1)}, f32[17,1024]{1,0:T(8,128)S(1)}, u32[]{:S(2)}, u32[]{:S(2)}) collective-permute-start(f32[17,1024]{1,0:T(8,128)S(1)} %add.602), channel_id=1, source_target_pairs={{0,4},{1,5},{2,6},{3,7},{4,0},{5,1},{6,2},{7,3},{8,12},{9,13},{10,... | collective-permute-start | bytes 208904 | tf_op jit(solution)/shard_map/ppermute | solution.py:123
  693.1 40.8 %collective-permute-start.55 = (bf16[3,128,1024]{2,1,0:T(8,128)(2,1)S(1)}, bf16[3,128,1024]{2,1,0:T(8,128)(2,1)S(1)}, u32[]{:S(2)}, u32[]{:S(2)}) collective-permute-start(bf16[3,128,1024]{2,1,0:T(8,128)(2,1)S(1)} %get-tuple-element.321), channel_id=1, source_target_pairs={{0,8},{1,9},{2,10},{3,11},{4,12},{5,13},{6,14},{7,15},{8,0},{9,1},... | collective-permute-start | bytes 2359304 | tf_op jit(solution)/shard_map/ppermute | solution.py:123
  693.5 40.4 %collective-permute-start.56 = (bf16[3,128,1024]{2,1,0:T(8,128)(2,1)S(1)}, bf16[3,128,1024]{2,1,0:T(8,128)(2,1)S(1)}, u32[]{:S(2)}, u32[]{:S(2)}) collective-permute-start(bf16[3,128,1024]{2,1,0:T(8,128)(2,1)S(1)} %get-tuple-element.322), channel_id=1, source_target_pairs={{0,16},{1,17},{2,18},{3,19},{4,20},{5,21},{6,22},{7,23},{8,24},{9,... | collective-permute-start | bytes 2359304 | tf_op jit(solution)/shard_map/ppermute | solution.py:123
  696.7 37.2 %collective-permute-start.57 = (f32[17,1024]{1,0:T(8,128)S(1)}, f32[17,1024]{1,0:T(8,128)S(1)}, u32[]{:S(2)}, u32[]{:S(2)}) collective-permute-start(f32[17,1024]{1,0:T(8,128)S(1)} %add.610), channel_id=1, source_target_pairs={{0,16},{1,17},{2,18},{3,19},{4,20},{5,21},{6,22},{7,23},{8,24},{9,... | collective-permute-start | bytes 208904 | tf_op jit(solution)/shard_map/ppermute | solution.py:123
  (128 other events, 2164.0 us)

commit v5 on v4

--- a/solution.py
+++ b/solution.py
@@ -275,7 +275,7 @@
             pltpu.SemaphoreType.DMA((DEPTH,)),
             pltpu.SemaphoreType.DMA((DEPTH,)),
         ],
-        compiler_params=pltpu.CompilerParams(vmem_limit_bytes=32 * 1024 * 1024),
+        compiler_params=pltpu.CompilerParams(vmem_limit_bytes=12 * 1024 * 1024),
         cost_estimate=pl.CostEstimate(
             flops=0, bytes_accessed=count * 32 * rows * width, transcendentals=0
         ),
@@ -438,7 +438,7 @@
         out_specs=[ANYWHERE] * 2,
         out_shape=[shape] * 2,
         scratch_shapes=[pltpu.VMEM((2, width, width), bf16), pltpu.SemaphoreType.DMA((2,))],
-        compiler_params=pltpu.CompilerParams(vmem_limit_bytes=32 * 1024 * 1024),
+        compiler_params=pltpu.CompilerParams(vmem_limit_bytes=24 * 1024 * 1024),
         cost_estimate=pl.CostEstimate(
             flops=2 * len(pairs) * rows * width * width,
             bytes_accessed=2 * len(pairs) * width * (width + 2 * rows),
@@ -495,8 +495,8 @@
     return (result, (stats, normed, active, slope), more)
 
 
-FORWARD_MB = 36
-BACKWARD_MB = 40
+FORWARD_MB = 32
+BACKWARD_MB = 38
 
 
 def ffn_backward_here(
@@ -712,7 +712,7 @@
         in_specs=[IN_SMEM] + [part] * 4 + [here] * 3,
         out_specs=[here] * 4,
         out_shape=[shape] * 3 + [jax.ShapeDtypeStruct(master.shape, bf16)],
-        compiler_params=pltpu.CompilerParams(vmem_limit_bytes=32 * 1024 * 1024),
+        compiler_params=pltpu.CompilerParams(vmem_limit_bytes=16 * 1024 * 1024),
         cost_estimate=pl.CostEstimate(
             flops=20 * slots * full * width,
             bytes_accessed=30 * slots * full * width,
@@ -819,7 +819,7 @@
             bytes_accessed=2 * rows * width * (len(operands) + out_count),
             transcendentals=rows * rows * width // HEAD_DIM,
         ),
-        compiler_params=pltpu.CompilerParams(vmem_limit_bytes=32 * 1024 * 1024),
+        compiler_params=pltpu.CompilerParams(vmem_limit_bytes=24 * 1024 * 1024),
     )(valid, *operands)
 
 
@@ -1026,12 +1026,10 @@
     grad_normal = dot_rows(incoming, p_output) * conv_slope
     own_sums = jnp.stack([jnp.sum(grad_normal, axis=0), jnp.sum(grad_normal * center, axis=0)])
     sums = butterfly_sum(own_sums, "dp")
+    block_out = send_home(result)
     if local:
-        block_out = send_home(result)
         sums, block_out = lax.optimization_barrier((sums, block_out))
         block_out = finish_hops(*block_out)
-    else:
-        block_out = send_home(result)
     sum_plain, sum_center = sums
     bn_scale = bn_gain * inv_std
     grad_depth = bn_scale * grad_normal - frame_mask * bn_scale * (

time: 750 us -> 742 us (0.989)
  Pallas kernels: 171 us -> 161 us
    pallas_call x1, Pallas kernels: 18.1 us -> 6.76 us  [assemble(): pl.pallas_call(lambda *refs: assemble_kernel(first, *refs), in_specs=[IN_...]
    unnamed x203 -> x215, local copies, waits for them, and re-layouts: 17.1 us -> 22.8 us
where the time goes in v5:
time: 742 us; the launch traced here: 734 us
  waiting for transfers between devices  410 us (55%)
  Pallas kernels  161 us (22%)
  other arithmetic  52.1 us (7%)
  starting transfers between devices  48.5 us (7%)
  local copies, waits for them, and re-layouts  36 us (5%)
  matrix products  23.5 us (3%)
    ppermute x43, waiting for transfers between devices, swap(): return lax.ppermute(value, BOTH, [(i, i ^ BITS[name]) for i in range(size)])  348 us
    ppermute x15, waiting for transfers between devices, exchange(): return lax.ppermute(value, axis, [(i, i ^ mask) for i in range(size)])  61.7 us
    pallas_call x3, Pallas kernels, ffn_backward_here(): pl.pallas_call(lambda *refs, cores=cores: ffn_back_kernel(cores, bool(bas...  61.5 us
    ppermute x43, starting transfers between devices, swap(): return lax.ppermute(value, BOTH, [(i, i ^ BITS[name]) for i in range(size)])  38.7 us
    pallas_call x2, Pallas kernels, ffn_forward_here(): pl.pallas_call(lambda *refs: ffn_kernel(firsts, count, tail, len(tail_ins...  34.2 us
    unnamed x215, local copies, waits for them, and re-layouts  22.8 us
    pallas_call x1, Pallas kernels, reduce_tiles_here(): pl.pallas_call(lambda *refs: scatter_kernel(groups, *refs), in_specs=[IN_...  19 us
    pallas_call x2, Pallas kernels, head_call(): pl.pallas_call(kernel, grid=(width // HEAD_DIM // TOGETHER,), in_specs=[I...  16.3 us
  transfers between devices with their start and end apart: 58, of which 26 were waited for; matrix products, arithmetic and copies ran while one was open for 5% of the time, Pallas kernels for 11%

profile of v5, /device:TPU:0, one launch (start us, length us, event | category | flops | bytes accessed | tf_op | source)
XLA Modules:
  0.0 734.2 jit_solution(7620787695390912516)
XLA Ops:
  13.7 12.6 %collective-permute-done.3 = bf16[1,2,128,1024]{3,2,1,0:T(8,128)(2,1)S(1)} collective-permute-done((bf16[1,2,128,1024]{3,2,1,0:T(8,128)(2,1)S(1)}, bf16[1,2,128,1024]{3,2,1,0:T(8,128)(2,1)S(1)}, u32[]{:S(2)}, u32[]{:S(2)}) %collective-permute-start.3) | collective-permute-done | bytes 524320 | tf_op jit(solution)/shard_map/ppermute | solution.py:48
  26.3 10.5 %collective-permute-done.4 = bf16[1,2,128,1024]{3,2,1,0:T(8,128)(2,1)S(1)} collective-permute-done((bf16[1,2,128,1024]{3,2,1,0:T(8,128)(2,1)S(1)}, bf16[1,2,128,1024]{3,2,1,0:T(8,128)(2,1)S(1)}, u32[]{:S(2)}, u32[]{:S(2)}) %collective-permute-start.4) | collective-permute-done | bytes 524320 | tf_op jit(solution)/shard_map/ppermute | solution.py:48
  36.7 6.4 collective-permute-done
  54.4 15.0 %collective-permute-done.9 = f32[7,256]{1,0:T(8,128)S(1)} collective-permute-done((f32[7,256]{1,0:T(8,128)S(1)}, f32[7,256]{1,0:T(8,128)S(1)}, u32[]{:S(2)}, u32[]{:S(2)}) %collective-permute-start.9) | collective-permute-done | bytes 7200 | tf_op jit(solution)/shard_map/ppermute | solution.py:48
  81.6 38.0 %collective-permute-done.12 = bf16[4,128,1024]{2,1,0:T(8,128)(2,1)S(1)} collective-permute-done((bf16[4,128,1024]{2,1,0:T(8,128)(2,1)S(1)}, bf16[4,128,1024]{2,1,0:T(8,128)(2,1)S(1)}, u32[]{:S(2)}, u32[]{:S(2)}) %collective-permute-start.12) | collective-permute-done | bytes 1048608 | tf_op jit(solution)/shard_map/ppermute | solution.py:123
  126.0 10.3 %pad_maximum_fusion = bf16[48,128,1024]{2,1,0:T(8,128)(2,1)} fusion(bf16[16,128,1024]{2,1,0:T(8,128)(2,1)S(1)} %constant_dynamic-update-slice_fusion.21.refs_8_.refs_4_.refs_9_, bf16[8,128,1024]{2,1,0:T(8,128)(2,1)} %pad_maximum_fusion.2.refs_7_.refs_3_.refs_8_, bf16[8,128,1024]{2,1,0:T(8,128)(2,1)S(1)} %pad_maximum_fusion.1.refs_6_.refs_2_.refs_7_, ...), kind=kLoop, calls=%fused_computation.2 | loop fusion | flops 18874368 | bytes 25165824 | tf_op jit(solution)/shard_map/concatenate | solution.py:288
  139.8 89.6 %collective-permute-done.15.refs_9_.refs_5_.refs_10_ = bf16[16,128,1024]{2,1,0:T(8,128)(2,1)} collective-permute-done((bf16[16,128,1024]{2,1,0:T(8,128)(2,1)S(1)}, bf16[16,128,1024]{2,1,0:T(8,128)(2,1)}, u32[]{:S(2)}, u32[]{:S(2)}) %collective-permute-start.15) | collective-permute-done | bytes 4194336 | tf_op jit(solution)/shard_map/ppermute | solution.py:123
  241.5 4.4 collective-permute-done.21.refs_15_.refs_11_.refs_16_
  249.0 16.8 %shard_map.229 = (f32[512,1024]{1,0:T(8,128)S(1)}, bf16[512,4096]{1,0:T(8,128)(2,1)}, bf16[512,4096]{1,0:T(8,128)(2,1)}, bf16[512,1024]{1,0:T(8,128)(2,1)S(1)}, f32[512,256]{1,0:T(8,128)S(1)}) custom-call(s32[4,23]{1,0:T(4,128)S(1)} %pad_add_fusion.refs_0_, bf16[512,1024]{1,0:T(8,128)(2,1)S(1)} %add_convert_fusion.9.refs_1_.refs_4_, ...), custom_call_target="tpu_custom_call" | custom-call | flops 8589934592 | bytes 25165824 | tf_op jit(solution)/shard_map/pallas_call | solution.py:477
  266.8 6.8 shard_map.230
  282.1 5.7 shard_map.231.refs_3_
  310.4 4.3 collective-permute-done.26
  321.6 17.5 %shard_map.232 = (f32[512,1024]{1,0:T(8,128)}, bf16[512,4096]{1,0:T(8,128)(2,1)}, bf16[512,4096]{1,0:T(8,128)(2,1)}, bf16[512,1024]{1,0:T(8,128)(2,1)S(1)}, f32[...) custom-call(s32[4,23]{1,0:T(4,128)S(1)} %pad_add_fusion.refs_0_, ...), custom_call_target="tpu_custom_call" | custom-call | flops 8589934592 | bytes 25165824 | tf_op jit(solution)/shard_map/pallas_call | solution.py:477
  339.1 28.0 %shard_map.233 = (f32[512,1024]{1,0:T(8,128)S(1)}, bf16[2048,1024]{1,0:T(8,128)(2,1)}, bf16[2048,1024]{1,0:T(8,128)(2,1)}, bf16[2048,1024]{1,0:T(8,128)(2,1)}, bf16[2048,1024]{1,0:T(8,128)(2,1)}) custom-call(s32[4,23]{1,0:T(4,128)S(1)} %pad_add_fusion.refs_0_, bf16[512,1024]{1,0:T(8,128)(2,1)S(1)} %get-tuple-element.228.refs_1_, ...), custom_call_target="tpu_custom_call" | custom-call | flops 17179869184 | bytes 50331648 | tf_op jit(solution)/shard_map/pallas_call | solution.py:513
  406.3 10.6 %shard_map.234 = (bf16[512,1024]{1,0:T(8,128)(2,1)S(1)}, bf16[512,1024]{1,0:T(8,128)(2,1)S(1)}, bf16[512,1024]{1,0:T(8,128)(2,1)S(1)}) custom-call(s32[1]{0:T(128)} %bitcast.14.valid_ref, bf16[512,1024]{1,0:T(8,128)(2,1)S(1)} %copy-done.26, bf16[512,1024]{1,0:T(8,128)(2,1)S(1)} %copy-done.24, bf16[512,1024]{1,0:T(8,128)(2,1)S(1)} %copy-done.28, ...), custom_call_target="tpu_custom_call" | custom-call | flops 2684354560 | bytes 7340032 | tf_op jit(solution)/shard_map/pallas_call | solution.py:811
  420.3 11.1 %shard_map.235 = (bf16[7,512,1024]{2,1,0:T(8,128)(2,1)}, bf16[7,512,1024]{2,1,0:T(8,128)(2,1)S(1)}) custom-call(bf16[512,1024]{1,0:T(8,128)(2,1)S(1)} %get-tuple-element.241.refs_0_, bf16[512,1024]{1,0:T(8,128)(2,1)S(1)} %get-tuple-element.242.refs_1_, bf16[512,1024]{1,0:T(8,128)(2,1)S(1)} %get-tuple-element.243.refs_2_, bf16[512,1024]{1,0:T(8,128)(2,1)S(1)} %copy-done.22, ...), custom_call_target="tpu_custom_call" | custom-call | flops 7516192768 | bytes 29360128 | tf_op jit(solution)/shard_map/pallas_call | solution.py:435
  435.4 16.7 %shard_map.236 = (f32[512,1024]{1,0:T(8,128)S(1)}, bf16[2048,1024]{1,0:T(8,128)(2,1)}, bf16[2048,1024]{1,0:T(8,128)(2,1)}) custom-call(s32[4,23]{1,0:T(4,128)S(1)} %pad_add_fusion.refs_0_, bf16[512,1024]{1,0:T(8,128)(2,1)S(1)} %multiply_convert_fusion.refs_1_, bf16[512,4096]{1,0:T(8,128)(2,1)} %get-tuple-element.247.refs_2_, ...), custom_call_target="tpu_custom_call" | custom-call | flops 8589934592 | bytes 25165824 | tf_op jit(solution)/shard_map/pallas_call | solution.py:513
  452.8 16.9 %shard_map.237 = (f32[512,1024]{1,0:T(8,128)S(1)}, bf16[2048,1024]{1,0:T(8,128)(2,1)}, bf16[2048,1024]{1,0:T(8,128)(2,1)}) custom-call(s32[4,23]{1,0:T(4,128)S(1)} %pad_add_fusion.refs_0_, bf16[512,1024]{1,0:T(8,128)(2,1)S(1)} %multiply_convert_fusion.refs_1_, bf16[512,4096]{1,0:T(8,128)(2,1)} %get-tuple-element.247.refs_2_, ...), custom_call_target="tpu_custom_call" | custom-call | flops 8589934592 | bytes 25165824 | tf_op jit(solution)/shard_map/pallas_call | solution.py:513
  478.3 19.0 %shard_map.238 = (bf16[16,128,1024]{2,1,0:T(8,128)(2,1)S(1)}, bf16[8,128,1024]{2,1,0:T(8,128)(2,1)S(1)}, bf16[8,128,1024]{2,1,0:T(8,128)(2,1)S(1)}, bf16[16,128,...) custom-call(s32[4,23]{1,0:T(4,128)S(1)} %pad_add_fusion.refs_0_, ...), custom_call_target="tpu_custom_call" | custom-call | bytes 72351744 | tf_op jit(solution)/shard_map/pallas_call | solution.py:644
  500.9 92.2 %collective-permute-done.44 = f32[17,1024]{1,0:T(8,128)S(1)} collective-permute-done((f32[17,1024]{1,0:T(8,128)S(1)}, f32[17,1024]{1,0:T(8,128)S(1)}, u32[]{:S(2)}, u32[]{:S(2)}) %collective-permute-start.44) | collective-permute-done | bytes 69664 | tf_op jit(solution)/shard_map/ppermute | solution.py:123
  606.2 44.1 %collective-permute-done.49 = f32[17,1024]{1,0:T(8,128)S(1)} collective-permute-done((f32[17,1024]{1,0:T(8,128)S(1)}, f32[17,1024]{1,0:T(8,128)S(1)}, u32[]{:S(2)}, u32[]{:S(2)}) %collective-permute-start.49) | collective-permute-done | bytes 69664 | tf_op jit(solution)/shard_map/ppermute | solution.py:123
  659.8 21.3 %collective-permute-done.54 = f32[17,1024]{1,0:T(8,128)S(1)} collective-permute-done((f32[17,1024]{1,0:T(8,128)S(1)}, f32[17,1024]{1,0:T(8,128)S(1)}, u32[]{:S(2)}, u32[]{:S(2)}) %collective-permute-start.54) | collective-permute-done | bytes 69664 | tf_op jit(solution)/shard_map/ppermute | solution.py:123
  691.9 34.5 %collective-permute-done.57 = f32[17,1024]{1,0:T(8,128)S(1)} collective-permute-done((f32[17,1024]{1,0:T(8,128)S(1)}, f32[17,1024]{1,0:T(8,128)S(1)}, u32[]{:S(2)}, u32[]{:S(2)}) %collective-permute-start.57) | collective-permute-done | bytes 69664 | tf_op jit(solution)/shard_map/ppermute | solution.py:123
  727.9 6.1 shard_map.241
  (467 shorter events, 192.5 us)
Async XLA Ops:
  5.9 37.2 %collective-permute-start = (bf16[3,128,1024]{2,1,0:T(8,128)(2,1)S(1)}, bf16[3,128,1024]{2,1,0:T(8,128)(2,1)S(1)}, u32[]{:S(2)}, u32[]{:S(2)}) collective-permute-start(bf16[3,128,1024]{2,1,0:T(8,128)(2,1)S(1)} %get-tuple-element.175), channel_id=1, source_target_pairs={{0,8},{1,9},{2,10},{3,11},{4,12},{5,13},{6,14},{7,15},{8,0},{9,1},... | collective-permute-start | bytes 2359304 | tf_op jit(solution)/shard_map/ppermute | solution.py:123
  76.4 46.8 %collective-permute-start.10 = (bf16[8,128,1024]{2,1,0:T(8,128)(2,1)S(1)}, bf16[8,128,1024]{2,1,0:T(8,128)(2,1)S(1)}, u32[]{:S(2)}, u32[]{:S(2)}) collective-permute-start(bf16[8,128,1024]{2,1,0:T(8,128)(2,1)S(1)} %get-tuple-element.196), channel_id=1, source_target_pairs={{0,4},{1,5},{2,6},{3,7},{4,0},{5,1},{6,2},{7,3},{8,12},{9,13},{10,... | collective-permute-start | bytes 6291464 | tf_op jit(solution)/shard_map/ppermute | solution.py:123
  77.0 46.2 %collective-permute-start.11 = (bf16[8,128,1024]{2,1,0:T(8,128)(2,1)S(1)}, bf16[8,128,1024]{2,1,0:T(8,128)(2,1)S(1)}, u32[]{:S(2)}, u32[]{:S(2)}) collective-permute-start(bf16[8,128,1024]{2,1,0:T(8,128)(2,1)S(1)} %get-tuple-element.197), channel_id=1, source_target_pairs={{0,2},{1,3},{2,0},{3,1},{4,6},{5,7},{6,4},{7,5},{8,10},{9,11},{10,... | collective-permute-start | bytes 6291464 | tf_op jit(solution)/shard_map/ppermute | solution.py:123
  77.5 42.1 %collective-permute-start.12 = (bf16[4,128,1024]{2,1,0:T(8,128)(2,1)S(1)}, bf16[4,128,1024]{2,1,0:T(8,128)(2,1)S(1)}, u32[]{:S(2)}, u32[]{:S(2)}) collective-permute-start(bf16[4,128,1024]{2,1,0:T(8,128)(2,1)S(1)} %pad_maximum_fusion.10), channel_id=1, source_target_pairs={{0,8},{1,9},{2,10},{3,11},{4,12},{5,13},{6,14},{7,15},{8,0},{9,1},... | collective-permute-start | bytes 3145736 | tf_op jit(solution)/shard_map/ppermute | solution.py:123
  77.8 45.4 %collective-permute-start.13 = (bf16[4,128,1024]{2,1,0:T(8,128)(2,1)S(1)}, bf16[4,128,1024]{2,1,0:T(8,128)(2,1)S(1)}, u32[]{:S(2)}, u32[]{:S(2)}) collective-permute-start(bf16[4,128,1024]{2,1,0:T(8,128)(2,1)S(1)} %pad_maximum_fusion.11), channel_id=1, source_target_pairs={{0,16},{1,17},{2,18},{3,19},{4,20},{5,21},{6,22},{7,23},{8,24},{9,... | collective-permute-start | bytes 3145736 | tf_op jit(solution)/shard_map/ppermute | solution.py:123
  136.3 112.6 %collective-permute-start.19 = (bf16[48,128,1024]{2,1,0:T(8,128)(2,1)}, bf16[48,128,1024]{2,1,0:T(8,128)(2,1)}, u32[]{:S(2)}, u32[]{:S(2)}) collective-permute-start(bf16[48,128,1024]{2,1,0:T(8,128)(2,1)} %pad_maximum_fusion), channel_id=1, source_target_pairs={{0,1},{1,0},{2,3},{3,2},{4,5},{5,4},{6,7},{7,6},{8,9},{9,8},{10,11... | collective-permute-start | bytes 37748744 | tf_op jit(solution)/shard_map/ppermute | solution.py:123
  136.3 93.1 %collective-permute-start.15 = (bf16[16,128,1024]{2,1,0:T(8,128)(2,1)S(1)}, bf16[16,128,1024]{2,1,0:T(8,128)(2,1)}, u32[]{:S(2)}, u32[]{:S(2)}) collective-permute-start(bf16[16,128,1024]{2,1,0:T(8,128)(2,1)S(1)} %get-tuple-element.211.refs_5_.refs_1_.refs_6_), channel_id=1, source_target_pairs={{0,4},{1,5},{2,6},{3,7},{4,0},{5,1},{6,2},{7,3},{8,12},{9,13},{10,... | collective-permute-start | bytes 12582920 | tf_op jit(solution)/shard_map/ppermute | solution.py:123
  137.8 92.8 %collective-permute-start.18 = (bf16[16,128,1024]{2,1,0:T(8,128)(2,1)S(1)}, bf16[16,128,1024]{2,1,0:T(8,128)(2,1)}, u32[]{:S(2)}, u32[]{:S(2)}) collective-permute-start(bf16[16,128,1024]{2,1,0:T(8,128)(2,1)S(1)} %constant_dynamic-update-slice_fusion.21.refs_8_.refs_4_.refs_9_), channel_id=1, source_target_pairs={{0,2},{1,3},{2,0},{3,1},{4,6},{5,7},{6,4},{7,5},{8,10},{9,11},{10,... | collective-permute-start | bytes 12582920 | tf_op jit(solution)/shard_map/ppermute | solution.py:123
  139.4 93.3 %collective-permute-start.16 = (bf16[8,128,1024]{2,1,0:T(8,128)(2,1)S(1)}, bf16[8,128,1024]{2,1,0:T(8,128)(2,1)}, u32[]{:S(2)}, u32[]{:S(2)}) collective-permute-start(bf16[8,128,1024]{2,1,0:T(8,128)(2,1)S(1)} %pad_maximum_fusion.1.refs_6_.refs_2_.refs_7_), channel_id=1, source_target_pairs={{0,8},{1,9},{2,10},{3,11},{4,12},{5,13},{6,14},{7,15},{8,0},{9,1},... | collective-permute-start | bytes 6291464 | tf_op jit(solution)/shard_map/ppermute | solution.py:123
  139.4 93.9 %collective-permute-start.17 = (bf16[8,128,1024]{2,1,0:T(8,128)(2,1)}, bf16[8,128,1024]{2,1,0:T(8,128)(2,1)}, u32[]{:S(2)}, u32[]{:S(2)}) collective-permute-start(bf16[8,128,1024]{2,1,0:T(8,128)(2,1)} %pad_maximum_fusion.2.refs_7_.refs_3_.refs_8_), channel_id=1, source_target_pairs={{0,16},{1,17},{2,18},{3,19},{4,20},{5,21},{6,22},{7,23},{8,24},{9,... | collective-permute-start | bytes 6291464 | tf_op jit(solution)/shard_map/ppermute | solution.py:123
  435.1 43.2 %collective-permute-start.36 = (bf16[7,512,1024]{2,1,0:T(8,128)(2,1)}, bf16[7,512,1024]{2,1,0:T(8,128)(2,1)}, u32[]{:S(2)}, u32[]{:S(2)}) collective-permute-start(bf16[7,512,1024]{2,1,0:T(8,128)(2,1)} %get-tuple-element.259), channel_id=1, source_target_pairs={{0,1},{1,0},{2,3},{3,2},{4,5},{5,4},{6,7},{7,6},{8,9},{9,8},{10,11... | collective-permute-start | bytes 22020104 | tf_op jit(solution)/shard_map/ppermute | solution.py:123
  497.4 95.8 %collective-permute-start.40 = (bf16[16,128,1024]{2,1,0:T(8,128)(2,1)S(1)}, bf16[16,128,1024]{2,1,0:T(8,128)(2,1)S(1)}, u32[]{:S(2)}, u32[]{:S(2)}) collective-permute-start(bf16[16,128,1024]{2,1,0:T(8,128)(2,1)S(1)} %get-tuple-element.277), channel_id=1, source_target_pairs={{0,4},{1,5},{2,6},{3,7},{4,0},{5,1},{6,2},{7,3},{8,12},{9,13},{10,... | collective-permute-start | bytes 12582920 | tf_op jit(solution)/shard_map/ppermute | solution.py:123
  498.1 95.0 %collective-permute-start.41 = (bf16[16,128,1024]{2,1,0:T(8,128)(2,1)}, bf16[16,128,1024]{2,1,0:T(8,128)(2,1)S(1)}, u32[]{:S(2)}, u32[]{:S(2)}) collective-permute-start(bf16[16,128,1024]{2,1,0:T(8,128)(2,1)} %get-tuple-element.278), channel_id=1, source_target_pairs={{0,2},{1,3},{2,0},{3,1},{4,6},{5,7},{6,4},{7,5},{8,10},{9,11},{10,... | collective-permute-start | bytes 12582920 | tf_op jit(solution)/shard_map/ppermute | solution.py:123
  498.6 94.5 %collective-permute-start.42 = (bf16[8,128,1024]{2,1,0:T(8,128)(2,1)S(1)}, bf16[8,128,1024]{2,1,0:T(8,128)(2,1)S(1)}, u32[]{:S(2)}, u32[]{:S(2)}) collective-permute-start(bf16[8,128,1024]{2,1,0:T(8,128)(2,1)S(1)} %get-tuple-element.279), channel_id=1, source_target_pairs={{0,8},{1,9},{2,10},{3,11},{4,12},{5,13},{6,14},{7,15},{8,0},{9,1},... | collective-permute-start | bytes 6291464 | tf_op jit(solution)/shard_map/ppermute | solution.py:123
  498.7 94.5 %collective-permute-start.43 = (bf16[8,128,1024]{2,1,0:T(8,128)(2,1)S(1)}, bf16[8,128,1024]{2,1,0:T(8,128)(2,1)S(1)}, u32[]{:S(2)}, u32[]{:S(2)}) collective-permute-start(bf16[8,128,1024]{2,1,0:T(8,128)(2,1)S(1)} %get-tuple-element.280), channel_id=1, source_target_pairs={{0,16},{1,17},{2,18},{3,19},{4,20},{5,21},{6,22},{7,23},{8,24},{9,... | collective-permute-start | bytes 6291464 | tf_op jit(solution)/shard_map/ppermute | solution.py:123
  500.6 92.5 %collective-permute-start.44 = (f32[17,1024]{1,0:T(8,128)S(1)}, f32[17,1024]{1,0:T(8,128)S(1)}, u32[]{:S(2)}, u32[]{:S(2)}) collective-permute-start(f32[17,1024]{1,0:T(8,128)S(1)} %add.601), channel_id=1, source_target_pairs={{0,2},{1,3},{2,0},{3,1},{4,6},{5,7},{6,4},{7,5},{8,10},{9,11},{10,... | collective-permute-start | bytes 208904 | tf_op jit(solution)/shard_map/ppermute | solution.py:123
  601.2 49.1 %collective-permute-start.45 = (bf16[8,128,1024]{2,1,0:T(8,128)(2,1)S(1)}, bf16[8,128,1024]{2,1,0:T(8,128)(2,1)S(1)}, u32[]{:S(2)}, u32[]{:S(2)}) collective-permute-start(bf16[8,128,1024]{2,1,0:T(8,128)(2,1)S(1)} %pad_maximum_fusion.5), channel_id=1, source_target_pairs={{0,4},{1,5},{2,6},{3,7},{4,0},{5,1},{6,2},{7,3},{8,12},{9,13},{10,... | collective-permute-start | bytes 6291464 | tf_op jit(solution)/shard_map/ppermute | solution.py:123
  602.3 48.0 %collective-permute-start.46 = (bf16[8,128,1024]{2,1,0:T(8,128)(2,1)S(1)}, bf16[8,128,1024]{2,1,0:T(8,128)(2,1)S(1)}, u32[]{:S(2)}, u32[]{:S(2)}) collective-permute-start(bf16[8,128,1024]{2,1,0:T(8,128)(2,1)S(1)} %pad_maximum_fusion.6), channel_id=1, source_target_pairs={{0,2},{1,3},{2,0},{3,1},{4,6},{5,7},{6,4},{7,5},{8,10},{9,11},{10,... | collective-permute-start | bytes 6291464 | tf_op jit(solution)/shard_map/ppermute | solution.py:123
  602.8 47.4 %collective-permute-start.47 = (bf16[4,128,1024]{2,1,0:T(8,128)(2,1)S(1)}, bf16[4,128,1024]{2,1,0:T(8,128)(2,1)S(1)}, u32[]{:S(2)}, u32[]{:S(2)}) collective-permute-start(bf16[4,128,1024]{2,1,0:T(8,128)(2,1)S(1)} %get-tuple-element.292), channel_id=1, source_target_pairs={{0,8},{1,9},{2,10},{3,11},{4,12},{5,13},{6,14},{7,15},{8,0},{9,1},... | collective-permute-start | bytes 3145736 | tf_op jit(solution)/shard_map/ppermute | solution.py:123
  602.8 47.5 %collective-permute-start.48 = (bf16[4,128,1024]{2,1,0:T(8,128)(2,1)S(1)}, bf16[4,128,1024]{2,1,0:T(8,128)(2,1)S(1)}, u32[]{:S(2)}, u32[]{:S(2)}) collective-permute-start(bf16[4,128,1024]{2,1,0:T(8,128)(2,1)S(1)} %get-tuple-element.293), channel_id=1, source_target_pairs={{0,16},{1,17},{2,18},{3,19},{4,20},{5,21},{6,22},{7,23},{8,24},{9,... | collective-permute-start | bytes 3145736 | tf_op jit(solution)/shard_map/ppermute | solution.py:123
  604.8 45.5 %collective-permute-start.49 = (f32[17,1024]{1,0:T(8,128)S(1)}, f32[17,1024]{1,0:T(8,128)S(1)}, u32[]{:S(2)}, u32[]{:S(2)}) collective-permute-start(f32[17,1024]{1,0:T(8,128)S(1)} %add.602), channel_id=1, source_target_pairs={{0,4},{1,5},{2,6},{3,7},{4,0},{5,1},{6,2},{7,3},{8,12},{9,13},{10,... | collective-permute-start | bytes 208904 | tf_op jit(solution)/shard_map/ppermute | solution.py:123
  685.7 40.8 %collective-permute-start.55 = (bf16[3,128,1024]{2,1,0:T(8,128)(2,1)S(1)}, bf16[3,128,1024]{2,1,0:T(8,128)(2,1)S(1)}, u32[]{:S(2)}, u32[]{:S(2)}) collective-permute-start(bf16[3,128,1024]{2,1,0:T(8,128)(2,1)S(1)} %get-tuple-element.321), channel_id=1, source_target_pairs={{0,8},{1,9},{2,10},{3,11},{4,12},{5,13},{6,14},{7,15},{8,0},{9,1},... | collective-permute-start | bytes 2359304 | tf_op jit(solution)/shard_map/ppermute | solution.py:123
  686.2 40.3 %collective-permute-start.56 = (bf16[3,128,1024]{2,1,0:T(8,128)(2,1)S(1)}, bf16[3,128,1024]{2,1,0:T(8,128)(2,1)S(1)}, u32[]{:S(2)}, u32[]{:S(2)}) collective-permute-start(bf16[3,128,1024]{2,1,0:T(8,128)(2,1)S(1)} %get-tuple-element.322), channel_id=1, source_target_pairs={{0,16},{1,17},{2,18},{3,19},{4,20},{5,21},{6,22},{7,23},{8,24},{9,... | collective-permute-start | bytes 2359304 | tf_op jit(solution)/shard_map/ppermute | solution.py:123
  689.1 37.3 %collective-permute-start.57 = (f32[17,1024]{1,0:T(8,128)S(1)}, f32[17,1024]{1,0:T(8,128)S(1)}, u32[]{:S(2)}, u32[]{:S(2)}) collective-permute-start(f32[17,1024]{1,0:T(8,128)S(1)} %add.610), channel_id=1, source_target_pairs={{0,16},{1,17},{2,18},{3,19},{4,20},{5,21},{6,22},{7,23},{8,24},{9,... | collective-permute-start | bytes 208904 | tf_op jit(solution)/shard_map/ppermute | solution.py:123
  (134 other events, 2159.0 us)

commit v6 on v5

--- a/solution.py
+++ b/solution.py
@@ -495,8 +495,8 @@
     return (result, (stats, normed, active, slope), more)
 
 
-FORWARD_MB = 32
-BACKWARD_MB = 38
+FORWARD_MB = 28
+BACKWARD_MB = 36
 
 
 def ffn_backward_here(

time: 742 us -> 750 us (1.011)
  matrix products: 23.5 us -> 31 us
    dot_general x7, matrix products: 11.9 us -> 19.4 us  [dot_plain(): return jnp.dot(left, right, preferred_element_type=f32)]
    unnamed x215 -> x217, local copies, waits for them, and re-layouts: 22.8 us -> 23 us
where the time goes in v6:
time: 750 us; the launch traced here: 742 us
  waiting for transfers between devices  410 us (55%)
  Pallas kernels  159 us (21%)
  other arithmetic  53.2 us (7%)
  starting transfers between devices  48.7 us (6%)
  local copies, waits for them, and re-layouts  36.2 us (5%)
  matrix products  31 us (4%)
    ppermute x43, waiting for transfers between devices, swap(): return lax.ppermute(value, BOTH, [(i, i ^ BITS[name]) for i in range(size)])  348 us
    ppermute x15, waiting for transfers between devices, exchange(): return lax.ppermute(value, axis, [(i, i ^ mask) for i in range(size)])  61.7 us
    pallas_call x3, Pallas kernels, ffn_backward_here(): pl.pallas_call(lambda *refs, cores=cores: ffn_back_kernel(cores, bool(bas...  61.5 us
    ppermute x43, starting transfers between devices, swap(): return lax.ppermute(value, BOTH, [(i, i ^ BITS[name]) for i in range(size)])  38.7 us
    pallas_call x2, Pallas kernels, ffn_forward_here(): pl.pallas_call(lambda *refs: ffn_kernel(firsts, count, tail, len(tail_ins...  33 us
    unnamed x217, local copies, waits for them, and re-layouts  23 us
    dot_general x7, matrix products, dot_plain(): return jnp.dot(left, right, preferred_element_type=f32)  19.4 us
    pallas_call x1, Pallas kernels, reduce_tiles_here(): pl.pallas_call(lambda *refs: scatter_kernel(groups, *refs), in_specs=[IN_...  19.4 us
  transfers between devices with their start and end apart: 58, of which 26 were waited for; matrix products, arithmetic and copies ran while one was open for 5% of the time, Pallas kernels for 11%

profile of v6, /device:TPU:0, one launch (start us, length us, event | category | flops | bytes accessed | tf_op | source)
XLA Modules:
  0.0 742.0 jit_solution(3848085544634785879)
XLA Ops:
  13.7 12.6 %collective-permute-done.3 = bf16[1,2,128,1024]{3,2,1,0:T(8,128)(2,1)S(1)} collective-permute-done((bf16[1,2,128,1024]{3,2,1,0:T(8,128)(2,1)S(1)}, bf16[1,2,128,1024]{3,2,1,0:T(8,128)(2,1)S(1)}, u32[]{:S(2)}, u32[]{:S(2)}) %collective-permute-start.3) | collective-permute-done | bytes 524320 | tf_op jit(solution)/shard_map/ppermute | solution.py:48
  26.3 10.5 %collective-permute-done.4 = bf16[1,2,128,1024]{3,2,1,0:T(8,128)(2,1)S(1)} collective-permute-done((bf16[1,2,128,1024]{3,2,1,0:T(8,128)(2,1)S(1)}, bf16[1,2,128,1024]{3,2,1,0:T(8,128)(2,1)S(1)}, u32[]{:S(2)}, u32[]{:S(2)}) %collective-permute-start.4) | collective-permute-done | bytes 524320 | tf_op jit(solution)/shard_map/ppermute | solution.py:48
  36.7 6.4 collective-permute-done
  54.4 15.0 %collective-permute-done.9 = f32[7,256]{1,0:T(8,128)S(1)} collective-permute-done((f32[7,256]{1,0:T(8,128)S(1)}, f32[7,256]{1,0:T(8,128)S(1)}, u32[]{:S(2)}, u32[]{:S(2)}) %collective-permute-start.9) | collective-permute-done | bytes 7200 | tf_op jit(solution)/shard_map/ppermute | solution.py:48
  81.6 38.0 %collective-permute-done.12 = bf16[4,128,1024]{2,1,0:T(8,128)(2,1)S(1)} collective-permute-done((bf16[4,128,1024]{2,1,0:T(8,128)(2,1)S(1)}, bf16[4,128,1024]{2,1,0:T(8,128)(2,1)S(1)}, u32[]{:S(2)}, u32[]{:S(2)}) %collective-permute-start.12) | collective-permute-done | bytes 1048608 | tf_op jit(solution)/shard_map/ppermute | solution.py:123
  126.1 10.3 %pad_maximum_fusion = bf16[48,128,1024]{2,1,0:T(8,128)(2,1)} fusion(bf16[16,128,1024]{2,1,0:T(8,128)(2,1)S(1)} %constant_dynamic-update-slice_fusion.21.refs_8_.refs_4_.refs_9_, bf16[8,128,1024]{2,1,0:T(8,128)(2,1)} %pad_maximum_fusion.2.refs_7_.refs_3_.refs_8_, bf16[8,128,1024]{2,1,0:T(8,128)(2,1)S(1)} %pad_maximum_fusion.1.refs_6_.refs_2_.refs_7_, ...), kind=kLoop, calls=%fused_computation.2 | loop fusion | flops 18874368 | bytes 25165824 | tf_op jit(solution)/shard_map/concatenate | solution.py:288
  139.8 89.6 %collective-permute-done.15.refs_9_.refs_5_.refs_10_ = bf16[16,128,1024]{2,1,0:T(8,128)(2,1)} collective-permute-done((bf16[16,128,1024]{2,1,0:T(8,128)(2,1)S(1)}, bf16[16,128,1024]{2,1,0:T(8,128)(2,1)}, u32[]{:S(2)}, u32[]{:S(2)}) %collective-permute-start.15) | collective-permute-done | bytes 4194336 | tf_op jit(solution)/shard_map/ppermute | solution.py:123
  241.5 4.4 collective-permute-done.21.refs_15_.refs_11_.refs_16_
  249.0 15.5 %shard_map.229 = (f32[512,1024]{1,0:T(8,128)S(1)}, bf16[512,4096]{1,0:T(8,128)(2,1)S(1)}, bf16[512,4096]{1,0:T(8,128)(2,1)}, bf16[512,1024]{1,0:T(8,128)(2,1)S(1)}, f32[512,256]{1,0:T(8,128)S(1)}) custom-call(s32[4,23]{1,0:T(4,128)S(1)} %pad_add_fusion.refs_0_, bf16[512,1024]{1,0:T(8,128)(2,1)S(1)} %add_convert_fusion.9.refs_1_.refs_4_, ...), custom_call_target="tpu_custom_call" | custom-call | flops 8589934592 | bytes 25165824 | tf_op jit(solution)/shard_map/pallas_call | solution.py:477
  267.5 6.5 shard_map.230
  282.6 5.7 shard_map.231.refs_3_
  322.1 17.5 %shard_map.232 = (f32[512,1024]{1,0:T(8,128)}, bf16[512,4096]{1,0:T(8,128)(2,1)}, bf16[512,4096]{1,0:T(8,128)(2,1)}, bf16[512,1024]{1,0:T(8,128)(2,1)S(1)}, f32[...) custom-call(s32[4,23]{1,0:T(4,128)S(1)} %pad_add_fusion.refs_0_, ...), custom_call_target="tpu_custom_call" | custom-call | flops 8589934592 | bytes 25165824 | tf_op jit(solution)/shard_map/pallas_call | solution.py:477
  339.7 27.9 %shard_map.233 = (f32[512,1024]{1,0:T(8,128)S(1)}, bf16[2048,1024]{1,0:T(8,128)(2,1)}, bf16[2048,1024]{1,0:T(8,128)(2,1)}, bf16[2048,1024]{1,0:T(8,128)(2,1)}, bf16[2048,1024]{1,0:T(8,128)(2,1)}) custom-call(s32[4,23]{1,0:T(4,128)S(1)} %pad_add_fusion.refs_0_, bf16[512,1024]{1,0:T(8,128)(2,1)S(1)} %get-tuple-element.228.refs_1_, ...), custom_call_target="tpu_custom_call" | custom-call | flops 17179869184 | bytes 50331648 | tf_op jit(solution)/shard_map/pallas_call | solution.py:513
  408.0 10.6 %shard_map.234 = (bf16[512,1024]{1,0:T(8,128)(2,1)S(1)}, bf16[512,1024]{1,0:T(8,128)(2,1)S(1)}, bf16[512,1024]{1,0:T(8,128)(2,1)S(1)}) custom-call(s32[1]{0:T(128)} %bitcast.14.valid_ref, bf16[512,1024]{1,0:T(8,128)(2,1)S(1)} %copy-done.27, bf16[512,1024]{1,0:T(8,128)(2,1)S(1)} %copy-done.25, bf16[512,1024]{1,0:T(8,128)(2,1)S(1)} %copy-done.29, ...), custom_call_target="tpu_custom_call" | custom-call | flops 2684354560 | bytes 7340032 | tf_op jit(solution)/shard_map/pallas_call | solution.py:811
  423.9 11.1 %shard_map.235 = (bf16[7,512,1024]{2,1,0:T(8,128)(2,1)}, bf16[7,512,1024]{2,1,0:T(8,128)(2,1)S(1)}) custom-call(bf16[512,1024]{1,0:T(8,128)(2,1)S(1)} %get-tuple-element.241.refs_0_, bf16[512,1024]{1,0:T(8,128)(2,1)S(1)} %get-tuple-element.242.refs_1_, bf16[512,1024]{1,0:T(8,128)(2,1)S(1)} %get-tuple-element.243.refs_2_, bf16[512,1024]{1,0:T(8,128)(2,1)S(1)} %copy-done.23, ...), custom_call_target="tpu_custom_call" | custom-call | flops 7516192768 | bytes 29360128 | tf_op jit(solution)/shard_map/pallas_call | solution.py:435
  435.0 6.8 multiply_reduce_fusion.7
  442.9 16.7 %shard_map.236 = (f32[512,1024]{1,0:T(8,128)S(1)}, bf16[2048,1024]{1,0:T(8,128)(2,1)}, bf16[2048,1024]{1,0:T(8,128)(2,1)}) custom-call(s32[4,23]{1,0:T(4,128)S(1)} %pad_add_fusion.refs_0_, bf16[512,1024]{1,0:T(8,128)(2,1)S(1)} %multiply_convert_fusion.refs_1_, bf16[512,4096]{1,0:T(8,128)(2,1)} %copy-done.8, bf16[512,4096]{1,0:T(8,128)(2,1)} %get-tuple-element.248.refs_3_, ...), custom_call_target="tpu_custom_call" | custom-call | flops 8589934592 | bytes 25165824 | tf_op jit(solution)/shard_map/pallas_call | solution.py:513
  460.3 16.8 %shard_map.237 = (f32[512,1024]{1,0:T(8,128)S(1)}, bf16[2048,1024]{1,0:T(8,128)(2,1)}, bf16[2048,1024]{1,0:T(8,128)(2,1)}) custom-call(s32[4,23]{1,0:T(4,128)S(1)} %pad_add_fusion.refs_0_, bf16[512,1024]{1,0:T(8,128)(2,1)S(1)} %multiply_convert_fusion.refs_1_, bf16[512,4096]{1,0:T(8,128)(2,1)} %copy-done.8, bf16[512,4096]{1,0:T(8,128)(2,1)} %get-tuple-element.248.refs_3_, ...), custom_call_target="tpu_custom_call" | custom-call | flops 8589934592 | bytes 25165824 | tf_op jit(solution)/shard_map/pallas_call | solution.py:513
  485.7 19.4 %shard_map.238 = (bf16[16,128,1024]{2,1,0:T(8,128)(2,1)S(1)}, bf16[8,128,1024]{2,1,0:T(8,128)(2,1)S(1)}, bf16[8,128,1024]{2,1,0:T(8,128)(2,1)S(1)}, bf16[16,128,...) custom-call(s32[4,23]{1,0:T(4,128)S(1)} %pad_add_fusion.refs_0_, ...), custom_call_target="tpu_custom_call" | custom-call | bytes 72351744 | tf_op jit(solution)/shard_map/pallas_call | solution.py:644
  508.7 92.2 %collective-permute-done.44 = f32[17,1024]{1,0:T(8,128)S(1)} collective-permute-done((f32[17,1024]{1,0:T(8,128)S(1)}, f32[17,1024]{1,0:T(8,128)S(1)}, u32[]{:S(2)}, u32[]{:S(2)}) %collective-permute-start.44) | collective-permute-done | bytes 69664 | tf_op jit(solution)/shard_map/ppermute | solution.py:123
  613.9 44.1 %collective-permute-done.49 = f32[17,1024]{1,0:T(8,128)S(1)} collective-permute-done((f32[17,1024]{1,0:T(8,128)S(1)}, f32[17,1024]{1,0:T(8,128)S(1)}, u32[]{:S(2)}, u32[]{:S(2)}) %collective-permute-start.49) | collective-permute-done | bytes 69664 | tf_op jit(solution)/shard_map/ppermute | solution.py:123
  667.6 21.3 %collective-permute-done.54 = f32[17,1024]{1,0:T(8,128)S(1)} collective-permute-done((f32[17,1024]{1,0:T(8,128)S(1)}, f32[17,1024]{1,0:T(8,128)S(1)}, u32[]{:S(2)}, u32[]{:S(2)}) %collective-permute-start.54) | collective-permute-done | bytes 69664 | tf_op jit(solution)/shard_map/ppermute | solution.py:123
  699.7 34.5 %collective-permute-done.57 = f32[17,1024]{1,0:T(8,128)S(1)} collective-permute-done((f32[17,1024]{1,0:T(8,128)S(1)}, f32[17,1024]{1,0:T(8,128)S(1)}, u32[]{:S(2)}, u32[]{:S(2)}) %collective-permute-start.57) | collective-permute-done | bytes 69664 | tf_op jit(solution)/shard_map/ppermute | solution.py:123
  735.7 6.1 shard_map.241
  (469 shorter events, 199.1 us)
Async XLA Ops:
  5.9 37.2 %collective-permute-start = (bf16[3,128,1024]{2,1,0:T(8,128)(2,1)S(1)}, bf16[3,128,1024]{2,1,0:T(8,128)(2,1)S(1)}, u32[]{:S(2)}, u32[]{:S(2)}) collective-permute-start(bf16[3,128,1024]{2,1,0:T(8,128)(2,1)S(1)} %get-tuple-element.175), channel_id=1, source_target_pairs={{0,8},{1,9},{2,10},{3,11},{4,12},{5,13},{6,14},{7,15},{8,0},{9,1},... | collective-permute-start | bytes 2359304 | tf_op jit(solution)/shard_map/ppermute | solution.py:123
  76.4 46.8 %collective-permute-start.10 = (bf16[8,128,1024]{2,1,0:T(8,128)(2,1)S(1)}, bf16[8,128,1024]{2,1,0:T(8,128)(2,1)S(1)}, u32[]{:S(2)}, u32[]{:S(2)}) collective-permute-start(bf16[8,128,1024]{2,1,0:T(8,128)(2,1)S(1)} %get-tuple-element.196), channel_id=1, source_target_pairs={{0,4},{1,5},{2,6},{3,7},{4,0},{5,1},{6,2},{7,3},{8,12},{9,13},{10,... | collective-permute-start | bytes 6291464 | tf_op jit(solution)/shard_map/ppermute | solution.py:123
  77.0 46.2 %collective-permute-start.11 = (bf16[8,128,1024]{2,1,0:T(8,128)(2,1)S(1)}, bf16[8,128,1024]{2,1,0:T(8,128)(2,1)S(1)}, u32[]{:S(2)}, u32[]{:S(2)}) collective-permute-start(bf16[8,128,1024]{2,1,0:T(8,128)(2,1)S(1)} %get-tuple-element.197), channel_id=1, source_target_pairs={{0,2},{1,3},{2,0},{3,1},{4,6},{5,7},{6,4},{7,5},{8,10},{9,11},{10,... | collective-permute-start | bytes 6291464 | tf_op jit(solution)/shard_map/ppermute | solution.py:123
  77.5 42.1 %collective-permute-start.12 = (bf16[4,128,1024]{2,1,0:T(8,128)(2,1)S(1)}, bf16[4,128,1024]{2,1,0:T(8,128)(2,1)S(1)}, u32[]{:S(2)}, u32[]{:S(2)}) collective-permute-start(bf16[4,128,1024]{2,1,0:T(8,128)(2,1)S(1)} %pad_maximum_fusion.10), channel_id=1, source_target_pairs={{0,8},{1,9},{2,10},{3,11},{4,12},{5,13},{6,14},{7,15},{8,0},{9,1},... | collective-permute-start | bytes 3145736 | tf_op jit(solution)/shard_map/ppermute | solution.py:123
  77.8 45.4 %collective-permute-start.13 = (bf16[4,128,1024]{2,1,0:T(8,128)(2,1)S(1)}, bf16[4,128,1024]{2,1,0:T(8,128)(2,1)S(1)}, u32[]{:S(2)}, u32[]{:S(2)}) collective-permute-start(bf16[4,128,1024]{2,1,0:T(8,128)(2,1)S(1)} %pad_maximum_fusion.11), channel_id=1, source_target_pairs={{0,16},{1,17},{2,18},{3,19},{4,20},{5,21},{6,22},{7,23},{8,24},{9,... | collective-permute-start | bytes 3145736 | tf_op jit(solution)/shard_map/ppermute | solution.py:123
  136.4 112.6 %collective-permute-start.19 = (bf16[48,128,1024]{2,1,0:T(8,128)(2,1)}, bf16[48,128,1024]{2,1,0:T(8,128)(2,1)}, u32[]{:S(2)}, u32[]{:S(2)}) collective-permute-start(bf16[48,128,1024]{2,1,0:T(8,128)(2,1)} %pad_maximum_fusion), channel_id=1, source_target_pairs={{0,1},{1,0},{2,3},{3,2},{4,5},{5,4},{6,7},{7,6},{8,9},{9,8},{10,11... | collective-permute-start | bytes 37748744 | tf_op jit(solution)/shard_map/ppermute | solution.py:123
  136.4 93.1 %collective-permute-start.15 = (bf16[16,128,1024]{2,1,0:T(8,128)(2,1)S(1)}, bf16[16,128,1024]{2,1,0:T(8,128)(2,1)}, u32[]{:S(2)}, u32[]{:S(2)}) collective-permute-start(bf16[16,128,1024]{2,1,0:T(8,128)(2,1)S(1)} %get-tuple-element.211.refs_5_.refs_1_.refs_6_), channel_id=1, source_target_pairs={{0,4},{1,5},{2,6},{3,7},{4,0},{5,1},{6,2},{7,3},{8,12},{9,13},{10,... | collective-permute-start | bytes 12582920 | tf_op jit(solution)/shard_map/ppermute | solution.py:123
  137.9 92.8 %collective-permute-start.18 = (bf16[16,128,1024]{2,1,0:T(8,128)(2,1)S(1)}, bf16[16,128,1024]{2,1,0:T(8,128)(2,1)}, u32[]{:S(2)}, u32[]{:S(2)}) collective-permute-start(bf16[16,128,1024]{2,1,0:T(8,128)(2,1)S(1)} %constant_dynamic-update-slice_fusion.21.refs_8_.refs_4_.refs_9_), channel_id=1, source_target_pairs={{0,2},{1,3},{2,0},{3,1},{4,6},{5,7},{6,4},{7,5},{8,10},{9,11},{10,... | collective-permute-start | bytes 12582920 | tf_op jit(solution)/shard_map/ppermute | solution.py:123
  139.4 93.3 %collective-permute-start.16 = (bf16[8,128,1024]{2,1,0:T(8,128)(2,1)S(1)}, bf16[8,128,1024]{2,1,0:T(8,128)(2,1)}, u32[]{:S(2)}, u32[]{:S(2)}) collective-permute-start(bf16[8,128,1024]{2,1,0:T(8,128)(2,1)S(1)} %pad_maximum_fusion.1.refs_6_.refs_2_.refs_7_), channel_id=1, source_target_pairs={{0,8},{1,9},{2,10},{3,11},{4,12},{5,13},{6,14},{7,15},{8,0},{9,1},... | collective-permute-start | bytes 6291464 | tf_op jit(solution)/shard_map/ppermute | solution.py:123
  139.4 93.9 %collective-permute-start.17 = (bf16[8,128,1024]{2,1,0:T(8,128)(2,1)}, bf16[8,128,1024]{2,1,0:T(8,128)(2,1)}, u32[]{:S(2)}, u32[]{:S(2)}) collective-permute-start(bf16[8,128,1024]{2,1,0:T(8,128)(2,1)} %pad_maximum_fusion.2.refs_7_.refs_3_.refs_8_), channel_id=1, source_target_pairs={{0,16},{1,17},{2,18},{3,19},{4,20},{5,21},{6,22},{7,23},{8,24},{9,... | collective-permute-start | bytes 6291464 | tf_op jit(solution)/shard_map/ppermute | solution.py:123
  442.6 43.1 %collective-permute-start.36 = (bf16[7,512,1024]{2,1,0:T(8,128)(2,1)}, bf16[7,512,1024]{2,1,0:T(8,128)(2,1)}, u32[]{:S(2)}, u32[]{:S(2)}) collective-permute-start(bf16[7,512,1024]{2,1,0:T(8,128)(2,1)} %get-tuple-element.259), channel_id=1, source_target_pairs={{0,1},{1,0},{2,3},{3,2},{4,5},{5,4},{6,7},{7,6},{8,9},{9,8},{10,11... | collective-permute-start | bytes 22020104 | tf_op jit(solution)/shard_map/ppermute | solution.py:123
  505.1 95.8 %collective-permute-start.40 = (bf16[16,128,1024]{2,1,0:T(8,128)(2,1)S(1)}, bf16[16,128,1024]{2,1,0:T(8,128)(2,1)S(1)}, u32[]{:S(2)}, u32[]{:S(2)}) collective-permute-start(bf16[16,128,1024]{2,1,0:T(8,128)(2,1)S(1)} %get-tuple-element.277), channel_id=1, source_target_pairs={{0,4},{1,5},{2,6},{3,7},{4,0},{5,1},{6,2},{7,3},{8,12},{9,13},{10,... | collective-permute-start | bytes 12582920 | tf_op jit(solution)/shard_map/ppermute | solution.py:123
  505.9 95.0 %collective-permute-start.41 = (bf16[16,128,1024]{2,1,0:T(8,128)(2,1)}, bf16[16,128,1024]{2,1,0:T(8,128)(2,1)S(1)}, u32[]{:S(2)}, u32[]{:S(2)}) collective-permute-start(bf16[16,128,1024]{2,1,0:T(8,128)(2,1)} %get-tuple-element.278), channel_id=1, source_target_pairs={{0,2},{1,3},{2,0},{3,1},{4,6},{5,7},{6,4},{7,5},{8,10},{9,11},{10,... | collective-permute-start | bytes 12582920 | tf_op jit(solution)/shard_map/ppermute | solution.py:123
  506.4 94.4 %collective-permute-start.42 = (bf16[8,128,1024]{2,1,0:T(8,128)(2,1)S(1)}, bf16[8,128,1024]{2,1,0:T(8,128)(2,1)S(1)}, u32[]{:S(2)}, u32[]{:S(2)}) collective-permute-start(bf16[8,128,1024]{2,1,0:T(8,128)(2,1)S(1)} %get-tuple-element.279), channel_id=1, source_target_pairs={{0,8},{1,9},{2,10},{3,11},{4,12},{5,13},{6,14},{7,15},{8,0},{9,1},... | collective-permute-start | bytes 6291464 | tf_op jit(solution)/shard_map/ppermute | solution.py:123
  506.4 94.5 %collective-permute-start.43 = (bf16[8,128,1024]{2,1,0:T(8,128)(2,1)S(1)}, bf16[8,128,1024]{2,1,0:T(8,128)(2,1)S(1)}, u32[]{:S(2)}, u32[]{:S(2)}) collective-permute-start(bf16[8,128,1024]{2,1,0:T(8,128)(2,1)S(1)} %get-tuple-element.280), channel_id=1, source_target_pairs={{0,16},{1,17},{2,18},{3,19},{4,20},{5,21},{6,22},{7,23},{8,24},{9,... | collective-permute-start | bytes 6291464 | tf_op jit(solution)/shard_map/ppermute | solution.py:123
  508.4 92.5 %collective-permute-start.44 = (f32[17,1024]{1,0:T(8,128)S(1)}, f32[17,1024]{1,0:T(8,128)S(1)}, u32[]{:S(2)}, u32[]{:S(2)}) collective-permute-start(f32[17,1024]{1,0:T(8,128)S(1)} %add.601), channel_id=1, source_target_pairs={{0,2},{1,3},{2,0},{3,1},{4,6},{5,7},{6,4},{7,5},{8,10},{9,11},{10,... | collective-permute-start | bytes 208904 | tf_op jit(solution)/shard_map/ppermute | solution.py:123
  609.0 49.1 %collective-permute-start.45 = (bf16[8,128,1024]{2,1,0:T(8,128)(2,1)S(1)}, bf16[8,128,1024]{2,1,0:T(8,128)(2,1)S(1)}, u32[]{:S(2)}, u32[]{:S(2)}) collective-permute-start(bf16[8,128,1024]{2,1,0:T(8,128)(2,1)S(1)} %pad_maximum_fusion.5), channel_id=1, source_target_pairs={{0,4},{1,5},{2,6},{3,7},{4,0},{5,1},{6,2},{7,3},{8,12},{9,13},{10,... | collective-permute-start | bytes 6291464 | tf_op jit(solution)/shard_map/ppermute | solution.py:123
  610.1 48.0 %collective-permute-start.46 = (bf16[8,128,1024]{2,1,0:T(8,128)(2,1)S(1)}, bf16[8,128,1024]{2,1,0:T(8,128)(2,1)S(1)}, u32[]{:S(2)}, u32[]{:S(2)}) collective-permute-start(bf16[8,128,1024]{2,1,0:T(8,128)(2,1)S(1)} %pad_maximum_fusion.6), channel_id=1, source_target_pairs={{0,2},{1,3},{2,0},{3,1},{4,6},{5,7},{6,4},{7,5},{8,10},{9,11},{10,... | collective-permute-start | bytes 6291464 | tf_op jit(solution)/shard_map/ppermute | solution.py:123
  610.6 47.4 %collective-permute-start.47 = (bf16[4,128,1024]{2,1,0:T(8,128)(2,1)S(1)}, bf16[4,128,1024]{2,1,0:T(8,128)(2,1)S(1)}, u32[]{:S(2)}, u32[]{:S(2)}) collective-permute-start(bf16[4,128,1024]{2,1,0:T(8,128)(2,1)S(1)} %get-tuple-element.292), channel_id=1, source_target_pairs={{0,8},{1,9},{2,10},{3,11},{4,12},{5,13},{6,14},{7,15},{8,0},{9,1},... | collective-permute-start | bytes 3145736 | tf_op jit(solution)/shard_map/ppermute | solution.py:123
  610.6 47.4 %collective-permute-start.48 = (bf16[4,128,1024]{2,1,0:T(8,128)(2,1)S(1)}, bf16[4,128,1024]{2,1,0:T(8,128)(2,1)S(1)}, u32[]{:S(2)}, u32[]{:S(2)}) collective-permute-start(bf16[4,128,1024]{2,1,0:T(8,128)(2,1)S(1)} %get-tuple-element.293), channel_id=1, source_target_pairs={{0,16},{1,17},{2,18},{3,19},{4,20},{5,21},{6,22},{7,23},{8,24},{9,... | collective-permute-start | bytes 3145736 | tf_op jit(solution)/shard_map/ppermute | solution.py:123
  612.5 45.5 %collective-permute-start.49 = (f32[17,1024]{1,0:T(8,128)S(1)}, f32[17,1024]{1,0:T(8,128)S(1)}, u32[]{:S(2)}, u32[]{:S(2)}) collective-permute-start(f32[17,1024]{1,0:T(8,128)S(1)} %add.602), channel_id=1, source_target_pairs={{0,4},{1,5},{2,6},{3,7},{4,0},{5,1},{6,2},{7,3},{8,12},{9,13},{10,... | collective-permute-start | bytes 208904 | tf_op jit(solution)/shard_map/ppermute | solution.py:123
  693.5 40.8 %collective-permute-start.55 = (bf16[3,128,1024]{2,1,0:T(8,128)(2,1)S(1)}, bf16[3,128,1024]{2,1,0:T(8,128)(2,1)S(1)}, u32[]{:S(2)}, u32[]{:S(2)}) collective-permute-start(bf16[3,128,1024]{2,1,0:T(8,128)(2,1)S(1)} %get-tuple-element.321), channel_id=1, source_target_pairs={{0,8},{1,9},{2,10},{3,11},{4,12},{5,13},{6,14},{7,15},{8,0},{9,1},... | collective-permute-start | bytes 2359304 | tf_op jit(solution)/shard_map/ppermute | solution.py:123
  693.9 40.3 %collective-permute-start.56 = (bf16[3,128,1024]{2,1,0:T(8,128)(2,1)S(1)}, bf16[3,128,1024]{2,1,0:T(8,128)(2,1)S(1)}, u32[]{:S(2)}, u32[]{:S(2)}) collective-permute-start(bf16[3,128,1024]{2,1,0:T(8,128)(2,1)S(1)} %get-tuple-element.322), channel_id=1, source_target_pairs={{0,16},{1,17},{2,18},{3,19},{4,20},{5,21},{6,22},{7,23},{8,24},{9,... | collective-permute-start | bytes 2359304 | tf_op jit(solution)/shard_map/ppermute | solution.py:123
  696.9 37.4 %collective-permute-start.57 = (f32[17,1024]{1,0:T(8,128)S(1)}, f32[17,1024]{1,0:T(8,128)S(1)}, u32[]{:S(2)}, u32[]{:S(2)}) collective-permute-start(f32[17,1024]{1,0:T(8,128)S(1)} %add.610), channel_id=1, source_target_pairs={{0,16},{1,17},{2,18},{3,19},{4,20},{5,21},{6,22},{7,23},{8,24},{9,... | collective-permute-start | bytes 208904 | tf_op jit(solution)/shard_map/ppermute | solution.py:123
  (135 other events, 2177.5 us)
